TPU v7x, 128 devices: a whole 4x4x4 slice. The times are simulated.
128 devices in a mesh: seq: 16 (over z, x), tp: 4 (over y), grp: 2 (over core).
Axes of the slice: x: 4, y: 4, z: 4, core: 2. Of those that a mesh axis runs over, the one named last changes fastest.
Arguments:
- group_hidden: bfloat16 [4, 512, 7168], P(None, 'seq', ('tp', 'grp')), may hold values from -6 to 6
- group_query: bfloat16 [4, 512, 128, 576], P(None, 'seq', ('tp', 'grp')), may hold values from -36 to 36
- past_cache: bfloat16 [4, 3072, 576], P(None, 'seq'), may hold values from -6 to 6
- past_len: int32 [4], replicated, may hold values from 1536 to 3072, as said below
- decode_hidden: bfloat16 [256, 2, 7168], P('seq', None, ('tp', 'grp')), may hold values from -6 to 6
- decode_query: bfloat16 [256, 2, 128, 576], P('seq', None, ('tp', 'grp')), may hold values from -36 to 36
- decode_pool: bfloat16 [512, 384, 576], P('seq'), may hold values from -6 to 6
- owner: int32 [256, 1], P('seq'), may hold values from 0 to 15; in each aligned block of 16 rows (0 to 15, 16 to 31, ...) at most 2 rows name the same one
- dec_len: int32 [256], P('seq'), may hold values from 1 to 382, as said below
- w_latent: bfloat16 [7168, 576], P(('tp', 'grp')), may hold values from -0.0625 to 0.0625
- kv_gain: float32 [512], replicated, may hold values from 0.5 to 1.5
- w_value: bfloat16 [128, 512, 128], P(('tp', 'grp')), may hold values from -0.25 to 0.25
Outputs:
- prefill_out: bfloat16 [4, 512, 128, 128], P(None, 'seq', ('tp', 'grp'))
- decode_out: bfloat16 [256, 2, 128, 128], P('seq', None, ('tp', 'grp'))
Inputs may be any that keep to these rules, and one draw needn't show every extreme that they name: `past_len`: at least half of the earlier positions are cached; some prompt has all 3072. `dec_len`: leaves room for the two new rows; some request has 382. Among the 16 requests that arrive at one index of seq, at most 2 name the same owner.
All inputs are finite; a program needn't handle non-finite values.
Results may differ from a plain program's by a relative error of at most 0.02.
Values may be sent and summed in bfloat16 or wider, within the bound.
No kernel may reach another device: no remote copies, remote signals or barrier semaphores. Data moves between devices by JAX's collectives and lax.ppermute only.
A program may use at most 192 MiB of HBM per device.

v0:
```python
import functools

import jax
import jax.numpy as jnp
from jax import lax
from jax.experimental import pallas as pl
from jax.experimental.pallas import tpu as pltpu
from jax.sharding import PartitionSpec as P

epsilon = 1e-06
negative = -1e30
log2_e = 1.4426950408889634
NT = (((1,), (1,)), ((), ()))
NN = (((1,), (0,)), ((), ()))
VMEM_BYTES = 56 * 2**20


def rotate(rope_part, positions):
    half_width = rope_part.shape[-1] // 2
    frequency = jnp.exp(-jnp.log(10000.0) * jnp.arange(half_width).astype(jnp.float32) / half_width)
    angles = positions.astype(jnp.float32)[..., None] * frequency
    cosine = jnp.cos(angles)
    sine_part = jnp.sin(angles)
    former = rope_part[..., :half_width]
    latter = rope_part[..., half_width:]
    return jnp.concatenate(
        [former * cosine - latter * sine_part, latter * cosine + former * sine_part], axis=-1
    )


def make_rows(latent, kv_gain, positions):
    lat_width = kv_gain.shape[0]
    latent_part = latent[..., :lat_width]
    spread = jnp.mean(latent_part * latent_part, axis=-1, keepdims=True)
    normed = latent_part * lax.rsqrt(spread + epsilon) * kv_gain
    return jnp.concatenate([normed, rotate(latent[..., lat_width:], positions)], axis=-1).astype(
        jnp.bfloat16
    )


def dot(left, right, dims):
    return lax.dot_general(left, right, dims, preferred_element_type=jnp.float32)


def key_scores(queries, keys, lat, dims):
    if dims is NT:
        return dot(queries[:, :lat], keys[:, :lat], NT) + dot(queries[:, lat:], keys[:, lat:], NT)
    return dot(queries[:, :lat], keys[:lat], NN) + dot(queries[:, lat:], keys[lat:], NN)


def lane_fold(op, total, block):
    for start in range(0, block.shape[1], 128):
        part = block[:, start : start + 128]
        total = part if total is None else op(total, part)
    return total


def attend_tiles(config, count, load, store, hold, keys, masks):
    lat, factor = config
    for i in range(count):
        queries = load(i)
        row = lax.broadcasted_iota(jnp.int32, (queries.shape[0], 1), 0) + i * queries.shape[0]
        highest = None
        end = 0
        for block, mask in zip(keys, masks):
            values = block()
            scores = key_scores(queries, values, lat, NT)
            allowed = mask(row)
            if allowed is not None:
                scores = jnp.where(allowed, scores, negative)
            hold[i % 2, :, end : end + values.shape[0]] = scores
            end += values.shape[0]
            highest = lane_fold(jnp.maximum, highest, scores)
        peak = jnp.max(highest, axis=1, keepdims=True)
        total = None
        summed = None
        end = 0
        for block in keys:
            values = block()
            weights = jnp.exp2((hold[i % 2, :, end : end + values.shape[0]] - peak) * factor)
            end += values.shape[0]
            total = lane_fold(jnp.add, total, weights)
            part = dot(weights.astype(jnp.bfloat16), values[:, :lat], NN)
            summed = part if summed is None else summed + part
        total = jnp.sum(total, axis=1, keepdims=True)
        store(i, summed / total, peak * factor + jnp.log2(total))


def attend_body(config, chunk, head_local, info, q_ref, dq_ref, past_ref, near_ref, far_ref, *rest):
    fresh_ref, out_ref, decode_ref, lse_ref, hold = rest
    step = pl.program_id(0)
    tile = hold.shape[1]
    seq_count, _, piece_rows, width = past_ref.shape
    lines, half_tokens, _ = near_ref.shape
    held = chunk // (2 * piece_rows)
    past_count = seq_count // held
    past_len = info[jnp.maximum(step - 1, 0)]
    z_place, x_place, core = info[5], info[6], info[7]

    def past_keys(j):
        return lambda: past_ref[j * held : (j + 1) * held].reshape(chunk, width)

    def past_mask(j):
        def allowed(row):
            if 2 * (j + 1) <= past_count:
                return None
            return lax.broadcasted_iota(jnp.int32, (1, chunk), 1) + j * chunk < past_len

        return allowed

    def group_mask(side):
        def allowed(row):
            place = lax.broadcasted_iota(jnp.int32, (1, lines * half_tokens), 1)
            outer = place // (4 * half_tokens)
            inner = (place // half_tokens) & 3
            z_from = (z_place + outer + (inner - outer) * side) & 3
            x_from = (x_place + inner + (outer - inner) * side) & 3
            key_token = (z_from * 4 + x_from) * (2 * half_tokens) + side * half_tokens
            key_token = key_token + (place & (half_tokens - 1))
            return key_token <= info[4] + row // head_local

        return allowed

    def fresh_mask(row):
        place = lax.broadcasted_iota(jnp.int32, (1, fresh_ref.shape[0]), 1)
        return (place >= row // (2 * head_local) * 2) & (place <= row // head_local)

    keys = [past_keys(j) for j in range(past_count)]
    keys += [
        lambda: near_ref[...].reshape(lines * half_tokens, width),
        lambda: far_ref[...].reshape(lines * half_tokens, width),
    ]
    masks = [past_mask(j) for j in range(past_count)]

    @pl.when(step == 0)
    def _():
        def store(i, value, lse):
            decode_ref[i * tile : (i + 1) * tile, :] = value.astype(jnp.bfloat16)
            lse_ref[i * tile : (i + 1) * tile, :] = jnp.broadcast_to(lse, (tile, lse_ref.shape[1]))

        attend_tiles(
            config,
            dq_ref.shape[0] // tile,
            lambda i: dq_ref[i * tile : (i + 1) * tile, :],
            store,
            hold,
            keys + [lambda: fresh_ref[...]],
            masks + [lambda row: None, lambda row: None, fresh_mask],
        )

    @pl.when(step > 0)
    def _():
        def store(i, value, lse):
            out_ref[i * tile : (i + 1) * tile, :] = value.astype(jnp.bfloat16)

        attend_tiles(
            config,
            q_ref.shape[0] // tile,
            lambda i: q_ref[i * tile : (i + 1) * tile, :],
            store,
            hold,
            keys,
            masks + [group_mask(core), group_mask(1 - core)],
        )


def attend_all(info, query, decode_query, past, near, far, fresh, lat, factor, head_local):
    prompts, rows, width = query.shape
    decode_rows = decode_query.shape[0]
    seq_count, _, halves, piece_rows, _ = past.shape
    lines, _, half_tokens, _ = near.shape
    keys = seq_count * halves * piece_rows + 2 * lines * half_tokens + fresh.shape[0]
    tile = 256
    chunk = 768

    def prompt(i):
        return jnp.maximum(i - 1, 0)

    group_spec = pl.BlockSpec(
        (lines, None, half_tokens, width), lambda i, _: (0, prompt(i), 0, 0)
    )
    return pl.pallas_call(
        functools.partial(attend_body, (lat, factor), chunk, head_local),
        grid_spec=pltpu.PrefetchScalarGridSpec(
            num_scalar_prefetch=1,
            grid=(prompts + 1,),
            in_specs=[
                pl.BlockSpec((None, rows, width), lambda i, _: (prompt(i), 0, 0)),
                pl.BlockSpec((decode_rows, width), lambda i, _: (0, 0)),
                pl.BlockSpec(
                    (seq_count, None, halves, piece_rows, width),
                    lambda i, _: (0, prompt(i), 0, 0, 0),
                ),
                group_spec,
                group_spec,
                pl.BlockSpec(fresh.shape, lambda i, _: (0, 0)),
            ],
            out_specs=[
                pl.BlockSpec((None, rows, lat), lambda i, _: (prompt(i), 0, 0)),
                pl.BlockSpec((decode_rows, lat), lambda i, _: (0, 0)),
                pl.BlockSpec((decode_rows, 128), lambda i, _: (0, 0)),
            ],
            scratch_shapes=[pltpu.VMEM((2, tile, keys), jnp.float32)],
        ),
        out_shape=[
            jax.ShapeDtypeStruct((prompts, rows, lat), jnp.bfloat16),
            jax.ShapeDtypeStruct((decode_rows, lat), jnp.bfloat16),
            jax.ShapeDtypeStruct((decode_rows, 128), jnp.float32),
        ],
        compiler_params=pltpu.CompilerParams(vmem_limit_bytes=VMEM_BYTES),
        cost_estimate=pl.CostEstimate(
            flops=2 * (prompts * rows + decode_rows) * keys * (768 + lat),
            bytes_accessed=2 * prompts * (keys + 2 * rows) * width,
            transcendentals=(prompts * rows + decode_rows) * keys,
        ),
        name="attend_all",
    )(info, query, decode_query, past, near, far, fresh)


def dispatch_body(source, length, q_ref, out_ref):
    slots, rows, width = out_ref.shape
    lat_rope = q_ref.shape[2]
    lane = lax.broadcasted_iota(jnp.int32, (rows, width - lat_rope), 1)
    for slot in range(slots):
        out_ref[slot, :, :lat_rope] = q_ref[source[slot]]
        size = length[slot]
        tail = jnp.where(lane < 32, size >> 4, size & 15)
        out_ref[slot, :, lat_rope:] = tail.astype(jnp.float32).astype(jnp.bfloat16)


def dispatch_queries(source, length, query, width):
    slots = source.shape[0]
    _, rows, _ = query.shape
    smem = pl.BlockSpec(memory_space=pltpu.SMEM)
    vmem = pl.BlockSpec(memory_space=pltpu.VMEM)
    return pl.pallas_call(
        dispatch_body,
        in_specs=[smem, smem, vmem],
        out_specs=vmem,
        out_shape=jax.ShapeDtypeStruct((slots, rows, width), jnp.bfloat16),
        compiler_params=pltpu.CompilerParams(vmem_limit_bytes=VMEM_BYTES),
        name="dispatch_queries",
    )(source, length, query)


def cache_body(lat, factor, batch, order, length, used, q_ref, *rest):
    pool_refs = rest[:batch]
    out_ref, lse_ref = rest[batch:]
    step = pl.program_id(0)
    rows = q_ref.shape[1]
    width, cache_rows = pool_refs[0].shape

    @pl.when(step * batch < used[0])
    def _():
        place = lax.broadcasted_iota(jnp.int32, (1, cache_rows), 1)
        lane = lax.broadcasted_iota(jnp.int32, (rows, lse_ref.shape[2]), 1)
        slots = [order[step * batch + b] for b in range(batch)]
        scores = [
            key_scores(q_ref[slots[b], :, :width], pool_refs[b][...], lat, NN)
            for b in range(batch)
        ]
        for b in range(batch):
            masked = jnp.where(place < length[slots[b]], scores[b], negative)
            peak = jnp.max(masked, axis=1, keepdims=True)
            weights = jnp.exp2((masked - peak) * factor)
            total = jnp.sum(weights, axis=1, keepdims=True)
            summed = dot(weights.astype(jnp.bfloat16), pool_refs[b][:lat], NT)
            out_ref[slots[b]] = (summed / total).astype(jnp.bfloat16)
            lse = peak * factor + jnp.log2(total)
            high = lse.astype(jnp.bfloat16).astype(jnp.float32)
            middle = (lse - high).astype(jnp.bfloat16).astype(jnp.float32)
            low = lse - high - middle
            lse_ref[slots[b]] = jnp.where(
                lane == 0, high, jnp.where(lane == 1, middle, low)
            ).astype(jnp.bfloat16)


def attend_cache(order, length, used, query, pool, lat, factor):
    batch = 4
    slots, rows, padded = query.shape
    _, width, cache_rows = pool.shape
    whole = pl.BlockSpec((slots, rows, padded), lambda i, *_: (0, 0, 0))

    def pool_spec(b):
        return pl.BlockSpec(
            (None, width, cache_rows), lambda i, order, *_: (order[i * batch + b], 0, 0)
        )

    return pl.pallas_call(
        functools.partial(cache_body, lat, factor, batch),
        grid_spec=pltpu.PrefetchScalarGridSpec(
            num_scalar_prefetch=3,
            grid=(slots // batch,),
            in_specs=[whole] + [pool_spec(b) for b in range(batch)],
            out_specs=[
                pl.BlockSpec((slots, rows, lat), lambda i, *_: (0, 0, 0)),
                pl.BlockSpec((slots, rows, 128), lambda i, *_: (0, 0, 0)),
            ],
        ),
        out_shape=[
            jax.ShapeDtypeStruct((slots, rows, lat), jnp.bfloat16),
            jax.ShapeDtypeStruct((slots, rows, 128), jnp.bfloat16),
        ],
        compiler_params=pltpu.CompilerParams(vmem_limit_bytes=VMEM_BYTES),
        cost_estimate=pl.CostEstimate(
            flops=2 * slots * 128 * cache_rows * (width + lat),
            bytes_accessed=2 * slots * cache_rows * width,
            transcendentals=slots * rows * cache_rows,
        ),
        name="attend_cache",
    )(order, length, used, query, *([pool] * batch))


def merge_body(slot, back_ref, near_ref, near_lse_ref, out_ref):
    count = near_ref.shape[0]
    width = near_ref.shape[2]
    for r in range(count):
        back = back_ref[slot[r]].astype(jnp.float32)
        far = back[:, :width]
        far_lse = back[:, width : width + 1] + back[:, width + 1 : width + 2]
        far_lse = far_lse + back[:, width + 2 : width + 3]
        near_lse = near_lse_ref[r][:, :1]
        peak = jnp.maximum(far_lse, near_lse)
        far_part = jnp.exp2(far_lse - peak)
        near_part = jnp.exp2(near_lse - peak)
        mixed = far * far_part + near_ref[r] * near_part
        out_ref[r] = (mixed / (far_part + near_part)).astype(jnp.bfloat16)


def merge_decode(slot, back, near, near_lse):
    smem = pl.BlockSpec(memory_space=pltpu.SMEM)
    vmem = pl.BlockSpec(memory_space=pltpu.VMEM)
    return pl.pallas_call(
        merge_body,
        in_specs=[smem, vmem, vmem, vmem],
        out_specs=vmem,
        out_shape=jax.ShapeDtypeStruct(near.shape, jnp.bfloat16),
        compiler_params=pltpu.CompilerParams(vmem_limit_bytes=VMEM_BYTES),
        name="merge_decode",
    )(slot, back, near, near_lse)


def swap_core(value):
    return lax.ppermute(value, "grp", [(0, 1), (1, 0)])


def fetch_tp(value, shift):
    return lax.ppermute(value, "tp", [((i + shift) % 4, i) for i in range(4)])


def fetch_ring(value, shift, turn):
    moves = []
    for i in range(16):
        z, x = i // 4, i % 4
        for c in range(2):
            if (c + turn) % 2 == 0:
                origin = z * 4 + (x + shift) % 4
            else:
                origin = (z + shift) % 4 * 4 + x
            moves.append((origin * 2 + c, i * 2 + c))
    return lax.ppermute(value, ("seq", "grp"), moves)


def on_device(
    group_hidden,
    group_query,
    past_cache,
    past_len,
    decode_hidden,
    decode_query,
    decode_pool,
    owner,
    dec_len,
    w_latent,
    kv_gain,
    w_value,
):
    seq_count = lax.axis_size("seq")
    seq_place = lax.axis_index("seq")
    tp_place = lax.axis_index("tp")
    core = lax.axis_index("grp")
    z_place, x_place = seq_place >> 2, seq_place & 3
    prompt_count, group_local, head_local, row_width = group_query.shape
    past_local = past_cache.shape[1]
    request_local = decode_query.shape[0]
    lat = kv_gain.shape[0]
    value_width = w_value.shape[2]
    slot_count = decode_pool.shape[0]
    pair_limit = slot_count // seq_count
    query_pairs = 2 * head_local
    factor = (value_width + row_width - lat) ** (-0.5) * log2_e

    half = past_local // 2
    past_part = lax.dynamic_slice(past_cache, (tp_place, core * half, 0), (1, half, row_width))
    past_all = lax.all_gather(
        past_part.reshape(half, row_width), ("seq", "tp", "grp"), axis=0, tiled=False
    ).reshape(seq_count, prompt_count, 2, half, row_width)

    half_tokens = group_local // 2
    pairs = 2 * request_local
    partial_group = jnp.einsum(
        "ptd,dc->ptc", group_hidden, w_latent, preferred_element_type=jnp.float32
    ).astype(jnp.bfloat16)
    partial_group = partial_group.reshape(prompt_count, 2, half_tokens, row_width)
    partial_decode = jnp.einsum(
        "rd,dc->rc",
        decode_hidden.reshape(pairs, -1),
        w_latent,
        preferred_element_type=jnp.float32,
    ).astype(jnp.bfloat16)
    group_part = prompt_count * half_tokens

    def both(chosen):
        part = lax.dynamic_index_in_dim(partial_group, chosen, axis=1, keepdims=False)
        return jnp.concatenate([part.reshape(group_part, row_width), partial_decode])

    pair_sum = both(core).astype(jnp.float32) + swap_core(both(1 - core)).astype(jnp.float32)
    pair_sum = pair_sum.astype(jnp.bfloat16)

    latent = pair_sum.astype(jnp.float32)
    for shift in range(1, 4):
        latent = latent + fetch_tp(pair_sum, shift).astype(jnp.float32)
    half_order = jnp.arange(half_tokens, dtype=jnp.int32)
    group_positions = (
        past_len[:, None] + seq_place * group_local + core * half_tokens + half_order[None, :]
    )
    decode_positions = (
        past_len[0]
        + group_local * seq_count
        + (dec_len[:, None] + jnp.arange(2, dtype=jnp.int32)).reshape(-1)
    )
    positions = jnp.concatenate([group_positions.reshape(-1), decode_positions])
    rows_own = make_rows(latent, kv_gain, positions)
    fresh = jnp.pad(rows_own[group_part:], ((0, 128 - pairs), (0, 0)))

    group_own = rows_own[:group_part].reshape(prompt_count, half_tokens, row_width)
    group_line = [group_own] + [fetch_ring(group_own, shift, 0) for shift in range(1, 4)]
    group_line = jnp.stack(group_line)
    group_lines = [group_line] + [fetch_ring(group_line, shift, 1) for shift in range(1, 4)]
    group_near = jnp.concatenate(group_lines)
    group_far = swap_core(group_near)

    targets = owner[:, 0]
    request_order = jnp.arange(request_local, dtype=jnp.int32)
    earlier = (targets[:, None] == targets[None, :]) & (
        request_order[None, :] < request_order[:, None]
    )
    slot_rank = jnp.sum(earlier.astype(jnp.int32), axis=1)
    destination = targets * pair_limit + slot_rank
    matches = jnp.arange(slot_count, dtype=jnp.int32)[:, None] == destination[None, :]
    source = jnp.sum(jnp.where(matches, request_order[None, :], 0), axis=1)
    send_length = jnp.sum(jnp.where(matches, dec_len[None, :], 0), axis=1)
    send_query = dispatch_queries(
        source,
        send_length,
        decode_query.reshape(request_local, query_pairs, row_width),
        row_width + 64,
    )
    arrived = lax.all_to_all(
        send_query.reshape(seq_count, pair_limit * query_pairs, row_width + 64),
        "seq",
        split_axis=0,
        concat_axis=0,
        tiled=True,
    ).reshape(slot_count, query_pairs, row_width + 64)
    marks = arrived[:, 0, row_width:].astype(jnp.float32)
    slot_length = (marks[:, 0] * 16 + marks[:, 32]).astype(jnp.int32)

    is_used = slot_length > 0
    used_rank = jnp.cumsum(is_used.astype(jnp.int32)) - 1
    used = jnp.sum(is_used.astype(jnp.int32))
    slots = jnp.arange(slot_count, dtype=jnp.int32)
    wanted = jnp.minimum(slots, jnp.maximum(used - 1, 0))
    order = jnp.sum(
        jnp.where(is_used[None, :] & (used_rank[None, :] == wanted[:, None]), slots[None, :], 0),
        axis=1,
    )
    cache_latent, cache_lse = attend_cache(
        order, slot_length, used.reshape(1), arrived, jnp.swapaxes(decode_pool, 1, 2), lat, factor
    )
    cache_value = jnp.einsum(
        "nshc,hcv->nshv",
        cache_latent.reshape(slot_count, 2, head_local, lat),
        w_value,
        preferred_element_type=jnp.float32,
    ).astype(jnp.bfloat16)
    back = jnp.concatenate(
        [cache_value.reshape(slot_count, query_pairs, value_width), cache_lse], axis=-1
    )
    back = lax.all_to_all(
        back.reshape(seq_count, pair_limit * query_pairs, 2 * value_width),
        "seq",
        split_axis=0,
        concat_axis=0,
        tiled=True,
    ).reshape(slot_count, query_pairs, 2 * value_width)

    info = jnp.stack(
        [past_len[p] for p in range(prompt_count)]
        + [seq_place * group_local, z_place, x_place, core]
    ).astype(jnp.int32)
    group_query, _ = lax.optimization_barrier((group_query, cache_value))
    prefill_latent, near_latent, near_lse = attend_all(
        info,
        group_query.reshape(prompt_count, group_local * head_local, row_width),
        decode_query.reshape(request_local * query_pairs, row_width),
        past_all,
        group_near,
        group_far,
        fresh,
        lat,
        factor,
        head_local,
    )
    near = jnp.einsum(
        "rshc,hcv->rshv",
        near_latent.reshape(request_local, 2, head_local, lat),
        w_value,
        preferred_element_type=jnp.float32,
    )
    decode_out = merge_decode(
        destination,
        back,
        near.reshape(request_local, query_pairs, value_width),
        near_lse.reshape(request_local, query_pairs, 128),
    ).reshape(request_local, 2, head_local, value_width)

    prefill_out = jnp.einsum(
        "pthc,hcv->pthv",
        prefill_latent.reshape(prompt_count, group_local, head_local, lat),
        w_value,
        preferred_element_type=jnp.float32,
    ).astype(jnp.bfloat16)
    return (prefill_out, decode_out)


def solution(mesh):
    in_specs = (
        P(None, "seq", ("tp", "grp")),
        P(None, "seq", ("tp", "grp"), None),
        P(None, "seq", None),
        P(),
        P("seq", None, ("tp", "grp")),
        P("seq", None, ("tp", "grp"), None),
        P("seq", None, None),
        P("seq", None),
        P("seq"),
        P(("tp", "grp"), None),
        P(),
        P(("tp", "grp"), None, None),
    )
    out_specs = (P(None, "seq", ("tp", "grp"), None), P("seq", None, ("tp", "grp"), None))
    return jax.shard_map(
        on_device, mesh=mesh, in_specs=in_specs, out_specs=out_specs, check_vma=False
    )
```

profile of v0, /device:TPU:1, one launch (start us, length us, event | category | flops | bytes accessed | tf_op | source)
XLA Modules:
  0.0 161.5 jit_solution(9793169657530815774)
XLA Ops:
  7.2 1.8 %constant_dynamic-slice_fusion.2 = bf16[1,96,576]{2,1,0:T(8,128)(2,1)} fusion(bf16[4,192,576]{2,1,0:T(8,128)(2,1)} %param.14, s32[]{:T(128)S(6)} %select_n.27, s32[]{:T(128)S(6)} %select_n.28), kind=kLoop, calls=%fused_computation.67 | loop fusion | bytes 221192 | tf_op jit(solution)/shard_map/dynamic_slice | solution.py:394
  9.0 0.8 reshape.182
  9.9 1.8 %convolution_convert_fusion = bf16[4,32,576]{2,1,0:T(8,128)(2,1)S(1)} fusion(bf16[4,32,896]{2,1,0:T(8,128)(2,1)} %param.12, bf16[896,576]{0,1:T(8,128)(2,1)} %param.21), kind=kOutput, calls=%fused_computation.12 | convolution fusion | flops 132194304 | bytes 1409024 | tf_op jit(solution)/shard_map/ptd,dc->ptc/dot_general | solution.py:401
  11.7 0.4 convolution_convert_fusion.1
  12.2 0.7 pad_maximum_fusion.2
  12.8 1.4 collective-permute-start
  14.3 0.2 convert_reduce_fusion
  14.5 0.7 select_reduce_fusion.1
  15.2 2.3 %dispatch_queries.1 = bf16[32,32,640]{2,1,0:T(8,128)(2,1)} custom-call(s32[32]{0:T(128)} %get-tuple-element.25.source, s32[32]{0:T(128)} %get-tuple-element.24.length, bf16[16,32,576]{2,1,0:T(8,128)(2,1)} %bitcast.88), custom_call_target="tpu_custom_call" | custom-call | tf_op jit(solution)/shard_map/dispatch_queries/pallas_call | solution.py:236
  17.5 7.8 %all-to-all-start = ((bf16[16,64,640]{2,1,0:T(8,128)(2,1)}), bf16[16,64,640]{2,1,0:T(8,128)(2,1)S(1)}, u32[]{:S(2)}, u32[]{:S(2)}) async-start(bf16[16,64,640]{2,1,0:T(8,128)(2,1)} %bitcast.78), calls=%async_computation | async-start | bytes 2621440 | tf_op jit(solution)/shard_map/all_to_all | solution.py:459
  25.3 0.1 iota_add_fusion
  25.4 0.1 add.147
  25.5 0.1 add_add_fusion
  25.6 0.1 add.155
  25.7 0.6 stack.31.info
  26.3 0.9 add_convert_fusion
  27.3 1.4 collective-permute-start.3
  28.6 2.6 %collective-permute-start.2 = (bf16[96,576]{1,0:T(8,128)(2,1)S(1)}, bf16[96,576]{1,0:T(8,128)(2,1)S(1)}, u32[]{:S(2)}, u32[]{:S(2)}) collective-permute-start(bf16[96,576]{1,0:T(8,128)(2,1)S(1)} %add_convert_fusion), channel_id=1, source_target_pairs={{4,0},{6,2},{0,4},{2,6},{5,1},{7,3},{1,5},{3,7},{12,8},{14,10},{8,... | collective-permute-start | bytes 331784 | tf_op jit(solution)/shard_map/ppermute | solution.py:348
  31.3 1.1 collective-permute-start.1
  32.3 0.1 add_convert_fusion.1
  32.4 1.0 collective-permute-done.3
  33.4 3.9 %collective-permute-done.2 = bf16[96,576]{1,0:T(8,128)(2,1)S(1)} collective-permute-done((bf16[96,576]{1,0:T(8,128)(2,1)S(1)}, bf16[96,576]{1,0:T(8,128)(2,1)S(1)}, u32[]{:S(2)}, u32[]{:S(2)}) %collective-permute-start.2) | collective-permute-done | bytes 110624 | tf_op jit(solution)/shard_map/ppermute | solution.py:348
  37.4 0.1 multiply_reduce_fusion
  37.5 0.3 fusion.39
  37.8 0.1 multiply_convert_fusion
  37.9 0.1 pad_maximum_fusion.4
  38.0 1.1 collective-permute-start.6
  39.1 2.3 %collective-permute-start.5 = (bf16[4,16,576]{2,1,0:T(8,128)(2,1)S(1)}, bf16[4,16,576]{2,1,0:T(8,128)(2,1)S(1)}, u32[]{:S(2)}, u32[]{:S(2)}) collective-permute-start(bf16[4,16,576]{2,1,0:T(8,128)(2,1)S(1)} %bitcast.84), channel_id=1, source_target_pairs={{16,0},{65,1},{24,8},{73,9},{0,16},{81,17},{8,24},{89,25},{48,32},... | collective-permute-start | bytes 221192 | tf_op jit(solution)/shard_map/ppermute | solution.py:361
  41.4 1.2 collective-permute-start.4
  42.6 0.7 fusion.33.rest_0_
  43.3 0.6 constant_dynamic-update-slice_fusion.6
  44.0 1.0 collective-permute-done.5
  45.0 0.8 collective-permute-done.4
  45.8 0.1 pad_maximum_fusion.1
  45.9 2.0 %collective-permute-start.9 = (bf16[4,4,16,576]{3,2,1,0:T(8,128)(2,1)S(1)}, bf16[4,4,16,576]{3,2,1,0:T(8,128)(2,1)S(1)}, u32[]{:S(2)}, u32[]{:S(2)}) collective-permute-start(bf16[4,4,16,576]{3,2,1,0:T(8,128)(2,1)S(1)} %pad_maximum_fusion.1), channel_id=1, source_target_pairs={{96,0},{25,1},{104,8},{1,9},{112,16},{9,17},{120,24},{17,25},{0,32... | collective-permute-start | bytes 884744 | tf_op jit(solution)/shard_map/ppermute | solution.py:361
  47.9 2.6 %collective-permute-start.8 = (bf16[4,4,16,576]{3,2,1,0:T(8,128)(2,1)S(1)}, bf16[4,4,16,576]{3,2,1,0:T(8,128)(2,1)S(1)}, u32[]{:S(2)}, u32[]{:S(2)}) collective-permute-start(bf16[4,4,16,576]{3,2,1,0:T(8,128)(2,1)S(1)} %pad_maximum_fusion.1), channel_id=1, source_target_pairs={{64,0},{17,1},{72,8},{25,9},{80,16},{1,17},{88,24},{9,25},{96,32},... | collective-permute-start | bytes 884744 | tf_op jit(solution)/shard_map/ppermute | solution.py:361
  50.4 0.8 collective-permute-start.7
  51.2 0.6 constant_dynamic-update-slice_fusion.5
  51.8 0.6 constant_dynamic-update-slice_fusion.4
  52.4 0.6 constant_dynamic-update-slice_fusion.3
  53.1 5.8 %collective-permute-done.7 = bf16[4,4,16,576]{3,2,1,0:T(8,128)(2,1)S(1)} collective-permute-done((bf16[4,4,16,576]{3,2,1,0:T(8,128)(2,1)S(1)}, bf16[4,4,16,576]{3,2,1,0:T(8,128)(2,1)S(1)}, u32[]{:S(2)}, u32[]{:S(2)}) %collective-permute-start.7) | collective-permute-done | bytes 294944 | tf_op jit(solution)/shard_map/ppermute | solution.py:361
  58.9 0.8 constant_dynamic-update-slice_fusion.2
  59.7 0.7 constant_dynamic-update-slice_fusion.1
  60.4 0.8 constant_dynamic-update-slice_fusion.near_ref
  61.2 7.7 %collective-permute-start.10 = (bf16[16,4,16,576]{3,2,1,0:T(8,128)(2,1)}, bf16[16,4,16,576]{3,2,1,0:T(8,128)(2,1)}, u32[]{:S(2)}, u32[]{:S(2)}) collective-permute-start(bf16[16,4,16,576]{3,2,1,0:T(8,128)(2,1)} %constant_dynamic-update-slice_fusion.near_ref), channel_id=1, source_target_pairs={{0,1},{1,0},{2,3},{3,2},{4,5},{5,4},{6,7},{7,6},{8,9},{9,8},{10,11... | collective-permute-start | bytes 3538952 | tf_op jit(solution)/shard_map/ppermute | solution.py:344
  68.9 0.1 slice_convert_fusion
  69.0 0.2 fusion.44.length
  69.2 0.8 convert_reduce_fusion.1
  70.6 0.1 compare_convert_fusion
  70.7 0.1 add_reduce_fusion
  70.8 0.8 select_reduce_fusion.order
  71.6 13.7 %attend_cache.1 = (bf16[32,32,512]{2,1,0:T(8,128)(2,1)}, bf16[32,32,128]{2,1,0:T(8,128)(2,1)}) custom-call(s32[32]{0:T(128)} %select_reduce_fusion.order, s32[32]{0:T(128)} %copy-done.6, s32[1]{0:T(128)} %bitcast.9.used, bf16[32,32,640]{2,1,0:T(8,128)(2,1)} %bitcast.77, bf16[32,576,384]{2,1,0:T(8,128)(2,1)} %bitcast.72, bf16[32,576,384]{2,1,0:T(8,128)(2,1)} %bitcast.73, ...), custom_call_target="tpu_custom_call" | custom-call | flops 3422552064 | bytes 14155776 | tf_op jit(solution)/shard_map/attend_cache/pallas_call | solution.py:289
  85.4 2.8 %fusion.23 = bf16[32,2,16,128]{3,0,1,2:T(8,128)(2,1)S(1)} fusion(bf16[16,512,128]{2,1,0:T(8,128)(2,1)S(1)} %copy-done, bf16[32,2,16,512]{3,2,1,0:T(8,128)(2,1)} %bitcast.80), kind=kOutput, calls=%fused_computation.11 | convolution fusion | flops 134348800 | bytes 3407872 | tf_op jit(solution)/shard_map/nshc,hcv->nshv/dot_general | solution.py:481
  88.2 0.2 copy.50
  88.4 0.9 pad_maximum_fusion
  89.2 3.8 %all-to-all-start.1 = ((bf16[16,64,256]{2,1,0:T(8,128)(2,1)}), bf16[16,64,256]{2,1,0:T(8,128)(2,1)S(1)}, u32[]{:S(2)}, u32[]{:S(2)}) async-start(bf16[16,64,256]{2,1,0:T(8,128)(2,1)} %pad_maximum_fusion), calls=%async_computation.1 | async-start | bytes 1048576 | tf_op jit(solution)/shard_map/all_to_all | solution.py:490
  93.0 17.0 %all-gather.2.cloned.1.call-done = bf16[128,96,576]{2,1,0:T(8,128)(2,1)} async-done(((bf16[1,96,576]{2,1,0:T(8,128)(2,1)}), bf16[128,96,576]{2,1,0:T(8,128)(2,1)}) %all-gather.2.cloned.1.call-update) | async-done | bytes 14155792 | tf_op jit(solution)/shard_map/all_gather | solution.py:395
  110.0 34.2 %attend_all.1 = (bf16[4,512,512]{2,1,0:T(8,128)(2,1)}, bf16[512,512]{1,0:T(8,128)(2,1)}, f32[512,128]{1,0:T(8,128)}) custom-call(s32[8]{0:T(128)} %stack.31.info, bf16[4,512,576]{2,1,0:T(8,128)(2,1)} %bitcast.104, bf16[512,576]{1,0:T(8,128)(2,1)} %bitcast.89, bf16[16,4,2,96,576]{4,3,2,1,0:T(8,128)(2,1)} %bitcast.103, ...), custom_call_target="tpu_custom_call" | custom-call | flops 24326963200 | bytes 21823488 | tf_op jit(solution)/shard_map/attend_all/pallas_call | solution.py:182
  144.2 4.1 %fusion.12 = bf16[4,32,16,128]{3,1,0,2:T(8,128)(2,1)S(1)} fusion(bf16[16,512,128]{2,1,0:T(8,128)(2,1)S(1)} %copy-done, bf16[4,32,16,512]{3,2,1,0:T(8,128)(2,1)} %bitcast.106), kind=kOutput, calls=%fused_computation.8 | convolution fusion | flops 268697600 | bytes 4718592 | tf_op jit(solution)/shard_map/pthc,hcv->pthv/dot_general | solution.py:528
  148.3 1.1 copy.53
  149.4 0.6 fusion.20
  150.0 0.9 copy.52
  150.9 0.8 copy-done.3
  151.7 3.0 %merge_decode.1 = bf16[16,32,128]{2,1,0:T(8,128)(2,1)} custom-call(s32[16]{0:T(128)} %copy-done.8, bf16[32,32,256]{2,1,0:T(8,128)(2,1)} %bitcast.79, f32[16,32,128]{2,1,0:T(8,128)} %bitcast.81, f32[16,32,128]{2,1,0:T(8,128)} %bitcast.99), custom_call_target="tpu_custom_call" | custom-call | tf_op jit(solution)/shard_map/merge_decode/pallas_call | solution.py:333
  (43 shorter events, 0.3 us)
Async XLA Ops:
  7.2 78.2 %copy-start = (bf16[16,512,128]{2,1,0:T(8,128)(2,1)S(1)}, bf16[16,512,128]{2,1,0:T(8,128)(2,1)}, u32[]{:S(2)}) copy-start(bf16[16,512,128]{2,1,0:T(8,128)(2,1)} %param.23) | copy-start | bytes 6291460
  7.2 4.6 %copy-start.2 = (bf16[896,576]{0,1:T(8,128)(2,1)S(1)}, bf16[896,576]{0,1:T(8,128)(2,1)}, u32[]{:S(2)}) copy-start(bf16[896,576]{0,1:T(8,128)(2,1)} %param.21) | copy-start | bytes 3096580
  7.2 102.8 %all-gather.2.cloned.1.call-start = ((), (), s32[]{:S(2)}) async-start(), calls=%async_computation.2 | async-start | bytes 15851520 | tf_op jit(solution)/shard_map/all_gather | solution.py:395
  9.9 4.4 %copy-start.11 = (s32[16,1]{0,1:T(1,128)S(1)}, s32[16,1]{0,1:T(1,128)}, u32[]{:S(2)}) copy-start(s32[16,1]{0,1:T(1,128)} %param.19) | copy-start | bytes 196
  9.9 4.6 %copy-start.9 = (s32[16]{0:T(128)S(1)}, s32[16]{0:T(128)}, u32[]{:S(2)}) copy-start(s32[16]{0:T(128)} %param.20) | copy-start | bytes 196
  12.8 13.5 %collective-permute-start = (bf16[96,576]{1,0:T(8,128)(2,1)}, bf16[96,576]{1,0:T(8,128)(2,1)}, u32[]{:S(2)}, u32[]{:S(2)}) collective-permute-start(bf16[96,576]{1,0:T(8,128)(2,1)} %pad_maximum_fusion.2), channel_id=1, source_target_pairs={{0,1},{1,0},{2,3},{3,2},{4,5},{5,4},{6,7},{7,6},{8,9},{9,8},{10,11... | collective-permute-start | bytes 331784 | tf_op jit(solution)/shard_map/ppermute | solution.py:344
  14.5 3.0 %copy-start.8 = (s32[16]{0:T(128)}, s32[16]{0:T(128)S(1)}, u32[]{:S(2)}) copy-start(s32[16]{0:T(128)S(1)} %multiply_add_fusion.slot) | copy-start | bytes 196
  17.5 7.9 %copy-start.10 = (s32[4]{0:T(128)S(1)}, s32[4]{0:T(128)}, u32[]{:S(2)}) copy-start(s32[4]{0:T(128)} %param.15) | copy-start | bytes 52
  17.5 51.4 %all-to-all-start = ((bf16[16,64,640]{2,1,0:T(8,128)(2,1)}), bf16[16,64,640]{2,1,0:T(8,128)(2,1)S(1)}, u32[]{:S(2)}, u32[]{:S(2)}) async-start(bf16[16,64,640]{2,1,0:T(8,128)(2,1)} %bitcast.78), calls=%async_computation | async-start | bytes 2621440 | tf_op jit(solution)/shard_map/all_to_all | solution.py:459
  25.3 12.5 %copy-start.7 = (f32[512]{0:T(512)S(1)}, f32[512]{0:T(512)}, u32[]{:S(2)}) copy-start(f32[512]{0:T(512)} %param.22) | copy-start | bytes 6148
  27.3 6.1 %collective-permute-start.3 = (bf16[96,576]{1,0:T(8,128)(2,1)S(1)}, bf16[96,576]{1,0:T(8,128)(2,1)S(1)}, u32[]{:S(2)}, u32[]{:S(2)}) collective-permute-start(bf16[96,576]{1,0:T(8,128)(2,1)S(1)} %add_convert_fusion), channel_id=1, source_target_pairs={{6,0},{0,2},{2,4},{4,6},{7,1},{1,3},{3,5},{5,7},{14,8},{8,10},{10,... | collective-permute-start | bytes 331784 | tf_op jit(solution)/shard_map/ppermute | solution.py:348
  28.6 8.7 %collective-permute-start.2 = (bf16[96,576]{1,0:T(8,128)(2,1)S(1)}, bf16[96,576]{1,0:T(8,128)(2,1)S(1)}, u32[]{:S(2)}, u32[]{:S(2)}) collective-permute-start(bf16[96,576]{1,0:T(8,128)(2,1)S(1)} %add_convert_fusion), channel_id=1, source_target_pairs={{4,0},{6,2},{0,4},{2,6},{5,1},{7,3},{1,5},{3,7},{12,8},{14,10},{8,... | collective-permute-start | bytes 331784 | tf_op jit(solution)/shard_map/ppermute | solution.py:348
  31.3 6.1 %collective-permute-start.1 = (bf16[96,576]{1,0:T(8,128)(2,1)S(1)}, bf16[96,576]{1,0:T(8,128)(2,1)S(1)}, u32[]{:S(2)}, u32[]{:S(2)}) collective-permute-start(bf16[96,576]{1,0:T(8,128)(2,1)S(1)} %add_convert_fusion), channel_id=1, source_target_pairs={{2,0},{4,2},{6,4},{0,6},{3,1},{5,3},{7,5},{1,7},{10,8},{12,10},{14... | collective-permute-start | bytes 331784 | tf_op jit(solution)/shard_map/ppermute | solution.py:348
  38.0 6.0 %collective-permute-start.6 = (bf16[4,16,576]{2,1,0:T(8,128)(2,1)S(1)}, bf16[4,16,576]{2,1,0:T(8,128)(2,1)S(1)}, u32[]{:S(2)}, u32[]{:S(2)}) collective-permute-start(bf16[4,16,576]{2,1,0:T(8,128)(2,1)S(1)} %bitcast.83), channel_id=1, source_target_pairs={{24,0},{97,1},{0,8},{105,9},{8,16},{113,17},{16,24},{121,25},{56,3... | collective-permute-start | bytes 221192 | tf_op jit(solution)/shard_map/ppermute | solution.py:361
  39.1 5.8 %collective-permute-start.5 = (bf16[4,16,576]{2,1,0:T(8,128)(2,1)S(1)}, bf16[4,16,576]{2,1,0:T(8,128)(2,1)S(1)}, u32[]{:S(2)}, u32[]{:S(2)}) collective-permute-start(bf16[4,16,576]{2,1,0:T(8,128)(2,1)S(1)} %bitcast.84), channel_id=1, source_target_pairs={{16,0},{65,1},{24,8},{73,9},{0,16},{81,17},{8,24},{89,25},{48,32},... | collective-permute-start | bytes 221192 | tf_op jit(solution)/shard_map/ppermute | solution.py:361
  41.4 4.4 %collective-permute-start.4 = (bf16[4,16,576]{2,1,0:T(8,128)(2,1)S(1)}, bf16[4,16,576]{2,1,0:T(8,128)(2,1)S(1)}, u32[]{:S(2)}, u32[]{:S(2)}) collective-permute-start(bf16[4,16,576]{2,1,0:T(8,128)(2,1)S(1)} %bitcast.85), channel_id=1, source_target_pairs={{8,0},{33,1},{16,8},{41,9},{24,16},{49,17},{0,24},{57,25},{40,32},... | collective-permute-start | bytes 221192 | tf_op jit(solution)/shard_map/ppermute | solution.py:361
  45.9 14.6 %collective-permute-start.9 = (bf16[4,4,16,576]{3,2,1,0:T(8,128)(2,1)S(1)}, bf16[4,4,16,576]{3,2,1,0:T(8,128)(2,1)S(1)}, u32[]{:S(2)}, u32[]{:S(2)}) collective-permute-start(bf16[4,4,16,576]{3,2,1,0:T(8,128)(2,1)S(1)} %pad_maximum_fusion.1), channel_id=1, source_target_pairs={{96,0},{25,1},{104,8},{1,9},{112,16},{9,17},{120,24},{17,25},{0,32... | collective-permute-start | bytes 884744 | tf_op jit(solution)/shard_map/ppermute | solution.py:361
  47.9 11.8 %collective-permute-start.8 = (bf16[4,4,16,576]{3,2,1,0:T(8,128)(2,1)S(1)}, bf16[4,4,16,576]{3,2,1,0:T(8,128)(2,1)S(1)}, u32[]{:S(2)}, u32[]{:S(2)}) collective-permute-start(bf16[4,4,16,576]{3,2,1,0:T(8,128)(2,1)S(1)} %pad_maximum_fusion.1), channel_id=1, source_target_pairs={{64,0},{17,1},{72,8},{25,9},{80,16},{1,17},{88,24},{9,25},{96,32},... | collective-permute-start | bytes 884744 | tf_op jit(solution)/shard_map/ppermute | solution.py:361
  50.4 8.5 %collective-permute-start.7 = (bf16[4,4,16,576]{3,2,1,0:T(8,128)(2,1)S(1)}, bf16[4,4,16,576]{3,2,1,0:T(8,128)(2,1)S(1)}, u32[]{:S(2)}, u32[]{:S(2)}) collective-permute-start(bf16[4,4,16,576]{3,2,1,0:T(8,128)(2,1)S(1)} %pad_maximum_fusion.1), channel_id=1, source_target_pairs={{32,0},{9,1},{40,8},{17,9},{48,16},{25,17},{56,24},{1,25},{64,32},... | collective-permute-start | bytes 884744 | tf_op jit(solution)/shard_map/ppermute | solution.py:361
  61.2 31.8 %collective-permute-start.10 = (bf16[16,4,16,576]{3,2,1,0:T(8,128)(2,1)}, bf16[16,4,16,576]{3,2,1,0:T(8,128)(2,1)}, u32[]{:S(2)}, u32[]{:S(2)}) collective-permute-start(bf16[16,4,16,576]{3,2,1,0:T(8,128)(2,1)} %constant_dynamic-update-slice_fusion.near_ref), channel_id=1, source_target_pairs={{0,1},{1,0},{2,3},{3,2},{4,5},{5,4},{6,7},{7,6},{8,9},{9,8},{10,11... | collective-permute-start | bytes 3538952 | tf_op jit(solution)/shard_map/ppermute | solution.py:344
  68.9 2.7 %copy-start.1 = (bf16[16,64,640]{2,1,0:T(8,128)(2,1)}, bf16[16,64,640]{2,1,0:T(8,128)(2,1)S(1)}, u32[]{:S(2)}) copy-start(bf16[16,64,640]{2,1,0:T(8,128)(2,1)S(1)} %all-to-all-done) | copy-start | bytes 3932164
  69.2 2.4 %copy-start.6 = (s32[32]{0:T(128)}, s32[32]{0:T(128)S(1)}, u32[]{:S(2)}) copy-start(s32[32]{0:T(128)S(1)} %fusion.44.length) | copy-start | bytes 388
  85.4 3.0 %copy-start.5 = (bf16[32,32,128]{2,1,0:T(8,128)(2,1)S(1)}, bf16[32,32,128]{2,1,0:T(8,128)(2,1)}, u32[]{:S(2)}) copy-start(bf16[32,32,128]{2,1,0:T(8,128)(2,1)} %get-tuple-element.11) | copy-start | bytes 786436
  89.2 61.6 %all-to-all-start.1 = ((bf16[16,64,256]{2,1,0:T(8,128)(2,1)}), bf16[16,64,256]{2,1,0:T(8,128)(2,1)S(1)}, u32[]{:S(2)}, u32[]{:S(2)}) async-start(bf16[16,64,256]{2,1,0:T(8,128)(2,1)} %pad_maximum_fusion), calls=%async_computation.1 | async-start | bytes 1048576 | tf_op jit(solution)/shard_map/all_to_all | solution.py:490
  148.3 1.1 copy-start.4
  150.9 0.8 copy-start.3
Sparse Core Ops, SparseCore 0:
  11.7 98.2 all-gather.1
where the time goes:
time: 163 us; the launch traced here: 162 us
  Pallas kernels  53.3 us (33%)
  starting transfers between devices  35.7 us (22%)
  waiting for transfers between devices  29.6 us (18%)
  between operations  15 us (9%)
  local copies, waits for them, and re-layouts  11.3 us (7%)
  matrix products  9.67 us (6%)
  other arithmetic  7.03 us (4%)
    pallas_call x1, Pallas kernels, attend_all(): pl.pallas_call(functools.partial(attend_body, (lat, factor), chunk, head_...  34.2 us
    all_gather x1, waiting for transfers between devices, on_device(): lax.all_gather(past_part.reshape(half, row_width), ('seq', 'tp', 'grp'),...  17 us
    pallas_call x1, Pallas kernels, attend_cache(): pl.pallas_call(functools.partial(cache_body, lat, factor, batch), grid_sp...  13.7 us
    ppermute x6, starting transfers between devices, fetch_ring(): return lax.ppermute(value, ('seq', 'grp'), moves)  9.9 us
    ppermute x2, starting transfers between devices, swap_core(): return lax.ppermute(value, 'grp', [(0, 1), (1, 0)])  9.08 us
    all_to_all x1, starting transfers between devices, on_device(): lax.all_to_all(send_query.reshape(seq_count, pair_limit * query_pairs, ro...  7.82 us
    ppermute x6, waiting for transfers between devices, fetch_ring(): return lax.ppermute(value, ('seq', 'grp'), moves)  7.66 us
    unnamed x31, local copies, waits for them, and re-layouts  6.06 us
  transfers between devices with their start and end apart: 14, of which 6 were waited for; matrix products, arithmetic and copies ran while one was open for 16% of the time, Pallas kernels for 31%

commit v1 on v0

--- a/solution.py
+++ b/solution.py
@@ -86,19 +86,56 @@
         store(i, summed / total, peak * factor + jnp.log2(total))
 
 
-def attend_body(config, chunk, head_local, info, q_ref, dq_ref, past_ref, near_ref, far_ref, *rest):
-    fresh_ref, out_ref, decode_ref, lse_ref, hold = rest
+def attend_body(config, chunk, head_local, info, q_ref, dq_ref, near_ref, far_ref, fresh_ref, *rest):
+    pieces = rest[:8]
+    out_ref, decode_ref, lse_ref, hold, past, arrive = rest[8:]
     step = pl.program_id(0)
+    prompts = pl.num_programs(0) - 1
     tile = hold.shape[1]
-    seq_count, _, piece_rows, width = past_ref.shape
+    _, holders, piece_rows, width = past.shape
     lines, half_tokens, _ = near_ref.shape
-    held = chunk // (2 * piece_rows)
-    past_count = seq_count // held
-    past_len = info[jnp.maximum(step - 1, 0)]
+    held = chunk // piece_rows
+    past_count = holders // held
+    prompt = jnp.maximum(step - 1, 0)
+    slot = prompt & 1
+    past_len = info[prompt]
     z_place, x_place, core = info[5], info[6], info[7]
 
+    def copies(p):
+        made = []
+        for c in range(2):
+            side = core if c == 0 else 1 - core
+            for s in range(4):
+                for j in range(4):
+                    dz = s + (j - s) * side
+                    dx = j + (s - j) * side
+                    holder = ((z_place + dz) & 3) * 4 + ((x_place + dx) & 3)
+                    made.append(
+                        pltpu.make_async_copy(
+                            pieces[c * 4 + s].at[j, p],
+                            past.at[p & 1, holder * 2 + side],
+                            arrive.at[p & 1, c * 16 + s * 4 + j],
+                        )
+                    )
+        return made
+
+    @pl.when(step == 0)
+    def _():
+        for copy in copies(0):
+            copy.start()
+
+    @pl.when((step > 0) & (step < prompts))
+    def _():
+        for copy in copies(step):
+            copy.start()
+
+    @pl.when(step != 1)
+    def _():
+        for copy in copies(prompt):
+            copy.wait()
+
     def past_keys(j):
-        return lambda: past_ref[j * held : (j + 1) * held].reshape(chunk, width)
+        return lambda: past[slot, j * held : (j + 1) * held].reshape(chunk, width)
 
     def past_mask(j):
         def allowed(row):
@@ -164,12 +201,13 @@
         )
 
 
-def attend_all(info, query, decode_query, past, near, far, fresh, lat, factor, head_local):
+def attend_all(info, query, decode_query, pieces, near, far, fresh, lat, factor, head_local):
     prompts, rows, width = query.shape
     decode_rows = decode_query.shape[0]
-    seq_count, _, halves, piece_rows, _ = past.shape
+    piece_rows = pieces[0].shape[2]
+    holders = 4 * len(pieces)
     lines, _, half_tokens, _ = near.shape
-    keys = seq_count * halves * piece_rows + 2 * lines * half_tokens + fresh.shape[0]
+    keys = holders * piece_rows + 2 * lines * half_tokens + fresh.shape[0]
     tile = 256
     chunk = 768
 
@@ -187,20 +225,21 @@
             in_specs=[
                 pl.BlockSpec((None, rows, width), lambda i, _: (prompt(i), 0, 0)),
                 pl.BlockSpec((decode_rows, width), lambda i, _: (0, 0)),
-                pl.BlockSpec(
-                    (seq_count, None, halves, piece_rows, width),
-                    lambda i, _: (0, prompt(i), 0, 0, 0),
-                ),
                 group_spec,
                 group_spec,
                 pl.BlockSpec(fresh.shape, lambda i, _: (0, 0)),
-            ],
+            ]
+            + [pl.BlockSpec(memory_space=pl.ANY)] * len(pieces),
             out_specs=[
                 pl.BlockSpec((None, rows, lat), lambda i, _: (prompt(i), 0, 0)),
                 pl.BlockSpec((decode_rows, lat), lambda i, _: (0, 0)),
                 pl.BlockSpec((decode_rows, 128), lambda i, _: (0, 0)),
             ],
-            scratch_shapes=[pltpu.VMEM((2, tile, keys), jnp.float32)],
+            scratch_shapes=[
+                pltpu.VMEM((2, tile, keys), jnp.float32),
+                pltpu.VMEM((2, holders, piece_rows, width), jnp.bfloat16),
+                pltpu.SemaphoreType.DMA((2, holders)),
+            ],
         ),
         out_shape=[
             jax.ShapeDtypeStruct((prompts, rows, lat), jnp.bfloat16),
@@ -214,7 +253,7 @@
             transcendentals=(prompts * rows + decode_rows) * keys,
         ),
         name="attend_all",
-    )(info, query, decode_query, past, near, far, fresh)
+    )(info, query, decode_query, near, far, fresh, *pieces)
 
 
 def dispatch_body(source, length, q_ref, out_ref):
@@ -377,7 +416,6 @@
 ):
     seq_count = lax.axis_size("seq")
     seq_place = lax.axis_index("seq")
-    tp_place = lax.axis_index("tp")
     core = lax.axis_index("grp")
     z_place, x_place = seq_place >> 2, seq_place & 3
     prompt_count, group_local, head_local, row_width = group_query.shape
@@ -391,10 +429,11 @@
     factor = (value_width + row_width - lat) ** (-0.5) * log2_e
 
     half = past_local // 2
-    past_part = lax.dynamic_slice(past_cache, (tp_place, core * half, 0), (1, half, row_width))
-    past_all = lax.all_gather(
-        past_part.reshape(half, row_width), ("seq", "tp", "grp"), axis=0, tiled=False
-    ).reshape(seq_count, prompt_count, 2, half, row_width)
+    past_half = lax.dynamic_slice_in_dim(past_cache, core * half, half, axis=1)
+    past_line = [past_half] + [fetch_ring(past_half, shift, 0) for shift in range(1, 4)]
+    past_line = jnp.stack(past_line)
+    past_lines = [past_line] + [fetch_ring(past_line, shift, 1) for shift in range(1, 4)]
+    past_lines = past_lines + [swap_core(piece) for piece in past_lines]
 
     half_tokens = group_local // 2
     pairs = 2 * request_local
@@ -417,6 +456,7 @@
     pair_sum = both(core).astype(jnp.float32) + swap_core(both(1 - core)).astype(jnp.float32)
     pair_sum = pair_sum.astype(jnp.bfloat16)
 
+    pair_sum, decode_query, _ = lax.optimization_barrier((pair_sum, decode_query, past_line))
     latent = pair_sum.astype(jnp.float32)
     for shift in range(1, 4):
         latent = latent + fetch_tp(pair_sum, shift).astype(jnp.float32)
@@ -504,7 +544,7 @@
         info,
         group_query.reshape(prompt_count, group_local * head_local, row_width),
         decode_query.reshape(request_local * query_pairs, row_width),
-        past_all,
+        past_lines,
         group_near,
         group_far,
         fresh,

time: 163 us -> 182 us (1.12)
  waiting for transfers between devices: 29.6 us -> 45.5 us
  starting transfers between devices: 35.7 us -> 51 us
  between operations: 15 us -> 1.69 us
  Pallas kernels: 53.3 us -> 50.8 us
  other arithmetic: 7.03 us -> 9.27 us
    ppermute x6 -> x12, waiting for transfers between devices: 7.66 us -> 45.5 us  [fetch_ring(): return lax.ppermute(value, ('seq', 'grp'), moves)]
    all_gather x1 -> x0, waiting for transfers between devices: 17 us -> none  [on_device(): lax.all_gather(past_part.reshape(half, row_width), ('seq', 'tp', 'grp'),...]
    ppermute x6 -> x12, starting transfers between devices: 9.9 us -> 24.6 us  [fetch_ring(): return lax.ppermute(value, ('seq', 'grp'), moves)]
    all_to_all x1, starting transfers between devices: 3.75 us -> 10.4 us  [on_device(): lax.all_to_all(back.reshape(seq_count, pair_limit * query_pairs, 2 * valu...]
    ppermute x3, waiting for transfers between devices: 4.93 us -> 0.01 us  [fetch_tp(): return lax.ppermute(value, 'tp', [((i + shift) % 4, i) for i in range(4)])]
    pallas_call x1, Pallas kernels: 13.7 us -> 9 us  [attend_cache(): pl.pallas_call(functools.partial(cache_body, lat, factor, batch), grid_sp...]
    all_to_all x1, starting transfers between devices: 7.82 us -> 4.84 us  [on_device(): lax.all_to_all(send_query.reshape(seq_count, pair_limit * query_pairs, ro...]
    another operation x3 -> x4, other arithmetic: 0.41 us -> 3.38 us  [the longest x1 2.98 us: on_device(): past_line = jnp.stack(past_line)]
  transfers between devices with their start and end apart: 14 -> 23, of which waited for: 6 -> 6; matrix products, arithmetic and copies ran while one was open for 16% -> 15% of each run, Pallas kernels for 31% -> 26%
where the time goes in v1:
time: 182 us; the launch traced here: 181 us
  starting transfers between devices  51 us (28%)
  Pallas kernels  50.8 us (28%)
  waiting for transfers between devices  45.5 us (25%)
  local copies, waits for them, and re-layouts  12.6 us (7%)
  matrix products  10.4 us (6%)
  other arithmetic  9.27 us (5%)
    ppermute x12, waiting for transfers between devices, fetch_ring(): return lax.ppermute(value, ('seq', 'grp'), moves)  45.5 us
    pallas_call x1, Pallas kernels, attend_all(): pl.pallas_call(functools.partial(attend_body, (lat, factor), chunk, head_...  36.5 us
    ppermute x12, starting transfers between devices, fetch_ring(): return lax.ppermute(value, ('seq', 'grp'), moves)  24.6 us
    all_to_all x1, starting transfers between devices, on_device(): lax.all_to_all(back.reshape(seq_count, pair_limit * query_pairs, 2 * valu...  10.4 us
    pallas_call x1, Pallas kernels, attend_cache(): pl.pallas_call(functools.partial(cache_body, lat, factor, batch), grid_sp...  9 us
    ppermute x6, starting transfers between devices, swap_core(): return lax.ppermute(value, 'grp', [(0, 1), (1, 0)])  6.21 us
    unnamed x31, local copies, waits for them, and re-layouts  6.07 us
    ppermute x3, starting transfers between devices, fetch_tp(): return lax.ppermute(value, 'tp', [((i + shift) % 4, i) for i in range(4)])  4.99 us
  transfers between devices with their start and end apart: 23, of which 6 were waited for; matrix products, arithmetic and copies ran while one was open for 15% of the time, Pallas kernels for 26%

profile of v1, /device:TPU:1, one launch (start us, length us, event | category | flops | bytes accessed | tf_op | source)
XLA Modules:
  0.0 181.3 jit_solution(5066062971581667072)
XLA Ops:
  0.7 2.0 %constant_dynamic-slice_fusion = bf16[4,96,576]{2,1,0:T(8,128)(2,1)} fusion(bf16[4,192,576]{2,1,0:T(8,128)(2,1)} %param.14, s32[]{:T(128)S(6)} %select_n.25), kind=kLoop, calls=%fused_computation.66 | loop fusion | bytes 884740 | tf_op jit(solution)/shard_map/dynamic_slice | solution.py:432
  2.7 4.4 %collective-permute-start.2 = (bf16[4,96,576]{2,1,0:T(8,128)(2,1)}, bf16[4,96,576]{2,1,0:T(8,128)(2,1)}, u32[]{:S(2)}, u32[]{:S(2)}) collective-permute-start(bf16[4,96,576]{2,1,0:T(8,128)(2,1)} %constant_dynamic-slice_fusion), channel_id=1, source_target_pairs={{16,0},{65,1},{24,8},{73,9},{0,16},{81,17},{8,24},{89,25},{48,32},... | collective-permute-start | bytes 1327112 | tf_op jit(solution)/shard_map/ppermute | solution.py:400
  7.1 0.4 collective-permute-start.1
  7.5 1.0 collective-permute-start.3
  8.6 0.8 reshape.171
  9.5 1.6 convolution_convert_fusion.1
  11.1 1.4 convolution_convert_fusion
  12.6 0.7 collective-permute-start
  13.3 1.1 fusion.48
  14.4 0.2 convert_reduce_fusion
  15.0 0.6 stack.46.info
  15.6 0.6 select_reduce_fusion.1
  16.3 3.5 %collective-permute-done.1 = bf16[4,96,576]{2,1,0:T(8,128)(2,1)} collective-permute-done((bf16[4,96,576]{2,1,0:T(8,128)(2,1)}, bf16[4,96,576]{2,1,0:T(8,128)(2,1)}, u32[]{:S(2)}, u32[]{:S(2)}) %collective-permute-start.1) | collective-permute-done | bytes 442400 | tf_op jit(solution)/shard_map/ppermute | solution.py:400
  19.8 3.0 %pad_maximum_fusion.rest_0_ = bf16[4,4,96,576]{3,2,1,0:T(8,128)(2,1)} fusion(bf16[1,4,96,576]{3,2,1,0:T(8,128)(2,1)} %bitcast.12, bf16[1,4,96,576]{3,2,1,0:T(8,128)(2,1)} %bitcast.11, bf16[1,4,96,576]{3,2,1,0:T(8,128)(2,1)} %bitcast.10, bf16[1,4,96,576]{3,2,1,0:T(8,128)(2,1)S(1)} %fusion.48), kind=kLoop, calls=%fused_computation.7 | loop fusion | flops 2654208 | bytes 3538944 | tf_op jit(solution)/shard_map/stack | solution.py:434
  22.8 1.3 collective-permute-start.6
  24.1 2.6 %collective-permute-start.5 = (bf16[96,576]{1,0:T(8,128)(2,1)S(1)}, bf16[96,576]{1,0:T(8,128)(2,1)}, u32[]{:S(2)}, u32[]{:S(2)}) collective-permute-start(bf16[96,576]{1,0:T(8,128)(2,1)S(1)} %add_convert_fusion), channel_id=1, source_target_pairs={{4,0},{6,2},{0,4},{2,6},{5,1},{7,3},{1,5},{3,7},{12,8},{14,10},{8,... | collective-permute-start | bytes 331784 | tf_op jit(solution)/shard_map/ppermute | solution.py:387
  26.7 1.1 collective-permute-start.4
  27.9 1.2 collective-permute-start.16
  29.0 2.4 %collective-permute-start.15 = (bf16[4,4,96,576]{3,2,1,0:T(8,128)(2,1)}, bf16[4,4,96,576]{3,2,1,0:T(8,128)(2,1)}, u32[]{:S(2)}, u32[]{:S(2)}) collective-permute-start(bf16[4,4,96,576]{3,2,1,0:T(8,128)(2,1)} %pad_maximum_fusion.rest_0_), channel_id=1, source_target_pairs={{64,0},{17,1},{72,8},{25,9},{80,16},{1,17},{88,24},{9,25},{96,32},... | collective-permute-start | bytes 5308424 | tf_op jit(solution)/shard_map/ppermute | solution.py:400
  31.4 2.3 %dispatch_queries.1 = bf16[32,32,640]{2,1,0:T(8,128)(2,1)} custom-call(s32[32]{0:T(128)} %get-tuple-element.27.source, s32[32]{0:T(128)} %get-tuple-element.26.length, bf16[16,32,576]{2,1,0:T(8,128)(2,1)} %bitcast.92), custom_call_target="tpu_custom_call" | custom-call | tf_op jit(solution)/shard_map/dispatch_queries/pallas_call | solution.py:275
  33.8 4.8 %all-to-all-start = ((bf16[16,64,640]{2,1,0:T(8,128)(2,1)}), bf16[16,64,640]{2,1,0:T(8,128)(2,1)S(1)}, u32[]{:S(2)}, u32[]{:S(2)}) async-start(bf16[16,64,640]{2,1,0:T(8,128)(2,1)} %bitcast.82), calls=%async_computation | async-start | bytes 2621440 | tf_op jit(solution)/shard_map/all_to_all | solution.py:499
  38.6 2.6 %collective-permute-start.14 = (bf16[4,4,96,576]{3,2,1,0:T(8,128)(2,1)}, bf16[4,4,96,576]{3,2,1,0:T(8,128)(2,1)}, u32[]{:S(2)}, u32[]{:S(2)}) collective-permute-start(bf16[4,4,96,576]{3,2,1,0:T(8,128)(2,1)} %pad_maximum_fusion.rest_0_), channel_id=1, source_target_pairs={{32,0},{9,1},{40,8},{17,9},{48,16},{25,17},{56,24},{1,25},{64,32},... | collective-permute-start | bytes 5308424 | tf_op jit(solution)/shard_map/ppermute | solution.py:400
  41.3 1.1 convert_add_fusion
  42.3 0.1 multiply_reduce_fusion
  42.6 0.3 fusion.39
  42.9 1.3 collective-permute-start.9
  44.2 2.4 %collective-permute-start.8 = (bf16[4,16,576]{2,1,0:T(8,128)(2,1)S(1)}, bf16[4,16,576]{2,1,0:T(8,128)(2,1)S(1)}, u32[]{:S(2)}, u32[]{:S(2)}) collective-permute-start(bf16[4,16,576]{2,1,0:T(8,128)(2,1)S(1)} %bitcast.88), channel_id=1, source_target_pairs={{16,0},{65,1},{24,8},{73,9},{0,16},{81,17},{8,24},{89,25},{48,32},... | collective-permute-start | bytes 221192 | tf_op jit(solution)/shard_map/ppermute | solution.py:400
  46.6 0.7 fusion.33.fresh_ref
  47.3 1.7 collective-permute-done.9
  49.0 2.6 %collective-permute-start.7 = (bf16[4,16,576]{2,1,0:T(8,128)(2,1)S(1)}, bf16[4,16,576]{2,1,0:T(8,128)(2,1)S(1)}, u32[]{:S(2)}, u32[]{:S(2)}) collective-permute-start(bf16[4,16,576]{2,1,0:T(8,128)(2,1)S(1)} %bitcast.89), channel_id=1, source_target_pairs={{8,0},{33,1},{16,8},{41,9},{24,16},{49,17},{0,24},{57,25},{40,32},... | collective-permute-start | bytes 221192 | tf_op jit(solution)/shard_map/ppermute | solution.py:400
  51.6 0.6 constant_dynamic-update-slice_fusion.6
  52.2 3.0 %collective-permute-done.8 = bf16[4,16,576]{2,1,0:T(8,128)(2,1)S(1)} collective-permute-done((bf16[4,16,576]{2,1,0:T(8,128)(2,1)S(1)}, bf16[4,16,576]{2,1,0:T(8,128)(2,1)S(1)}, u32[]{:S(2)}, u32[]{:S(2)}) %collective-permute-start.8) | collective-permute-done | bytes 73760 | tf_op jit(solution)/shard_map/ppermute | solution.py:400
  55.2 13.3 %collective-permute-done.7 = bf16[4,16,576]{2,1,0:T(8,128)(2,1)S(1)} collective-permute-done((bf16[4,16,576]{2,1,0:T(8,128)(2,1)S(1)}, bf16[4,16,576]{2,1,0:T(8,128)(2,1)S(1)}, u32[]{:S(2)}, u32[]{:S(2)}) %collective-permute-start.7) | collective-permute-done | bytes 73760 | tf_op jit(solution)/shard_map/ppermute | solution.py:400
  68.6 2.4 %collective-permute-start.12 = (bf16[4,4,16,576]{3,2,1,0:T(8,128)(2,1)S(1)}, bf16[4,4,16,576]{3,2,1,0:T(8,128)(2,1)S(1)}, u32[]{:S(2)}, u32[]{:S(2)}) collective-permute-start(bf16[4,4,16,576]{3,2,1,0:T(8,128)(2,1)S(1)} %pad_maximum_fusion.2), channel_id=1, source_target_pairs={{96,0},{25,1},{104,8},{1,9},{112,16},{9,17},{120,24},{17,25},{0,32... | collective-permute-start | bytes 884744 | tf_op jit(solution)/shard_map/ppermute | solution.py:400
  71.0 1.3 collective-permute-start.10
  72.3 0.6 constant_dynamic-update-slice_fusion.5
  72.9 0.7 constant_dynamic-update-slice_fusion.4
  73.6 20.5 %collective-permute-done.10 = bf16[4,4,16,576]{3,2,1,0:T(8,128)(2,1)S(1)} collective-permute-done((bf16[4,4,16,576]{3,2,1,0:T(8,128)(2,1)S(1)}, bf16[4,4,16,576]{3,2,1,0:T(8,128)(2,1)S(1)}, u32[]{:S(2)}, u32[]{:S(2)}) %collective-permute-start.10) | collective-permute-done | bytes 294944 | tf_op jit(solution)/shard_map/ppermute | solution.py:400
  94.1 2.6 %collective-permute-start.11 = (bf16[4,4,16,576]{3,2,1,0:T(8,128)(2,1)S(1)}, bf16[4,4,16,576]{3,2,1,0:T(8,128)(2,1)S(1)}, u32[]{:S(2)}, u32[]{:S(2)}) collective-permute-start(bf16[4,4,16,576]{3,2,1,0:T(8,128)(2,1)S(1)} %pad_maximum_fusion.2), channel_id=1, source_target_pairs={{64,0},{17,1},{72,8},{25,9},{80,16},{1,17},{88,24},{9,25},{96,32},... | collective-permute-start | bytes 884744 | tf_op jit(solution)/shard_map/ppermute | solution.py:400
  96.8 0.6 constant_dynamic-update-slice_fusion.3
  97.4 0.8 constant_dynamic-update-slice_fusion.2
  98.1 3.4 %collective-permute-done.11 = bf16[4,4,16,576]{3,2,1,0:T(8,128)(2,1)S(1)} collective-permute-done((bf16[4,4,16,576]{3,2,1,0:T(8,128)(2,1)S(1)}, bf16[4,4,16,576]{3,2,1,0:T(8,128)(2,1)S(1)}, u32[]{:S(2)}, u32[]{:S(2)}) %collective-permute-start.11) | collective-permute-done | bytes 294944 | tf_op jit(solution)/shard_map/ppermute | solution.py:400
  101.6 4.4 %collective-permute-start.17 = (bf16[4,4,96,576]{3,2,1,0:T(8,128)(2,1)}, bf16[4,4,96,576]{3,2,1,0:T(8,128)(2,1)}, u32[]{:S(2)}, u32[]{:S(2)}) collective-permute-start(bf16[4,4,96,576]{3,2,1,0:T(8,128)(2,1)} %pad_maximum_fusion.rest_0_), channel_id=1, source_target_pairs={{0,1},{1,0},{2,3},{3,2},{4,5},{5,4},{6,7},{7,6},{8,9},{9,8},{10,11... | collective-permute-start | bytes 5308424 | tf_op jit(solution)/shard_map/ppermute | solution.py:383
  105.9 0.8 constant_dynamic-update-slice_fusion.1
  106.7 0.8 constant_dynamic-update-slice_fusion.near_ref
  107.6 0.6 collective-permute-start.20
  108.1 0.1 collective-permute-start.19
  108.2 0.4 collective-permute-start.18
  108.7 0.2 fusion.44.length
  108.8 0.6 convert_reduce_fusion.1
  110.3 0.1 add_reduce_fusion
  110.4 0.7 select_reduce_fusion.order
  111.2 9.0 %attend_cache.1 = (bf16[32,32,512]{2,1,0:T(8,128)(2,1)}, bf16[32,32,128]{2,1,0:T(8,128)(2,1)}) custom-call(s32[32]{0:T(128)} %select_reduce_fusion.order, s32[32]{0:T(128)} %copy-done.6, s32[1]{0:T(128)} %bitcast.17.used, bf16[32,32,640]{2,1,0:T(8,128)(2,1)} %bitcast.81, bf16[32,576,384]{2,1,0:T(8,128)(2,1)} %bitcast.76, bf16[32,576,384]{2,1,0:T(8,128)(2,1)} %bitcast.77, ...), custom_call_target="tpu_custom_call" | custom-call | flops 3422552064 | bytes 14155776 | tf_op jit(solution)/shard_map/attend_cache/pallas_call | solution.py:328
  120.2 2.6 %fusion.23 = bf16[32,2,16,128]{3,0,1,2:T(8,128)(2,1)S(1)} fusion(bf16[16,512,128]{2,1,0:T(8,128)(2,1)S(1)} %copy-done, bf16[32,2,16,512]{3,2,1,0:T(8,128)(2,1)} %bitcast.84), kind=kOutput, calls=%fused_computation.12 | convolution fusion | flops 134348800 | bytes 3407872 | tf_op jit(solution)/shard_map/nshc,hcv->nshv/dot_general | solution.py:521
  122.7 0.2 copy.42
  122.9 0.9 pad_maximum_fusion.1
  123.8 10.4 %all-to-all-start.1 = ((bf16[16,64,256]{2,1,0:T(8,128)(2,1)}), bf16[16,64,256]{2,1,0:T(8,128)(2,1)S(1)}, u32[]{:S(2)}, u32[]{:S(2)}) async-start(bf16[16,64,256]{2,1,0:T(8,128)(2,1)} %pad_maximum_fusion.1), calls=%async_computation.1 | async-start | bytes 1048576 | tf_op jit(solution)/shard_map/all_to_all | solution.py:530
  134.3 36.5 %attend_all.1 = (bf16[4,512,512]{2,1,0:T(8,128)(2,1)}, bf16[512,512]{1,0:T(8,128)(2,1)}, f32[512,128]{1,0:T(8,128)}) custom-call(s32[8]{0:T(128)} %stack.46.info, bf16[4,512,576]{2,1,0:T(8,128)(2,1)} %bitcast.107, bf16[512,576]{1,0:T(8,128)(2,1)} %bitcast.93, bf16[16,4,16,576]{3,2,1,0:T(8,128)(2,1)} %constant_dynamic-update-slice_fusion.near_ref, ...), custom_call_target="tpu_custom_call" | custom-call | flops 24326963200 | bytes 21823488 | tf_op jit(solution)/shard_map/attend_all/pallas_call | solution.py:220
  170.8 4.1 %fusion.12 = bf16[4,32,16,128]{3,1,0,2:T(8,128)(2,1)S(1)} fusion(bf16[16,512,128]{2,1,0:T(8,128)(2,1)S(1)} %copy-done, bf16[4,32,16,512]{3,2,1,0:T(8,128)(2,1)} %bitcast.109), kind=kOutput, calls=%fused_computation.9 | convolution fusion | flops 268697600 | bytes 4718592 | tf_op jit(solution)/shard_map/pthc,hcv->pthv/dot_general | solution.py:568
  174.9 1.1 copy.45
  176.0 0.6 fusion.20
  176.6 0.9 copy.44
  177.5 0.8 copy-done.3
  178.3 3.0 %merge_decode.1 = bf16[16,32,128]{2,1,0:T(8,128)(2,1)} custom-call(s32[16]{0:T(128)} %copy-done.8, bf16[32,32,256]{2,1,0:T(8,128)(2,1)} %bitcast.83, f32[16,32,128]{2,1,0:T(8,128)} %bitcast.85, f32[16,32,128]{2,1,0:T(8,128)} %bitcast.103), custom_call_target="tpu_custom_call" | custom-call | tf_op jit(solution)/shard_map/merge_decode/pallas_call | solution.py:372
  (62 shorter events, 1.1 us)
Async XLA Ops:
  0.6 119.5 %copy-start = (bf16[16,512,128]{2,1,0:T(8,128)(2,1)S(1)}, bf16[16,512,128]{2,1,0:T(8,128)(2,1)}, u32[]{:S(2)}) copy-start(bf16[16,512,128]{2,1,0:T(8,128)(2,1)} %param.23) | copy-start | bytes 6291460
  0.6 10.5 %copy-start.2 = (bf16[896,576]{0,1:T(8,128)(2,1)S(1)}, bf16[896,576]{0,1:T(8,128)(2,1)}, u32[]{:S(2)}) copy-start(bf16[896,576]{0,1:T(8,128)(2,1)} %param.21) | copy-start | bytes 3096580
  2.7 13.6 %collective-permute-start.2 = (bf16[4,96,576]{2,1,0:T(8,128)(2,1)}, bf16[4,96,576]{2,1,0:T(8,128)(2,1)}, u32[]{:S(2)}, u32[]{:S(2)}) collective-permute-start(bf16[4,96,576]{2,1,0:T(8,128)(2,1)} %constant_dynamic-slice_fusion), channel_id=1, source_target_pairs={{16,0},{65,1},{24,8},{73,9},{0,16},{81,17},{8,24},{89,25},{48,32},... | collective-permute-start | bytes 1327112 | tf_op jit(solution)/shard_map/ppermute | solution.py:400
  7.1 12.7 %collective-permute-start.1 = (bf16[4,96,576]{2,1,0:T(8,128)(2,1)}, bf16[4,96,576]{2,1,0:T(8,128)(2,1)}, u32[]{:S(2)}, u32[]{:S(2)}) collective-permute-start(bf16[4,96,576]{2,1,0:T(8,128)(2,1)} %constant_dynamic-slice_fusion), channel_id=1, source_target_pairs={{8,0},{33,1},{16,8},{41,9},{24,16},{49,17},{0,24},{57,25},{40,32},... | collective-permute-start | bytes 1327112 | tf_op jit(solution)/shard_map/ppermute | solution.py:400
  7.5 12.3 %collective-permute-start.3 = (bf16[4,96,576]{2,1,0:T(8,128)(2,1)}, bf16[4,96,576]{2,1,0:T(8,128)(2,1)}, u32[]{:S(2)}, u32[]{:S(2)}) collective-permute-start(bf16[4,96,576]{2,1,0:T(8,128)(2,1)} %constant_dynamic-slice_fusion), channel_id=1, source_target_pairs={{24,0},{97,1},{0,8},{105,9},{8,16},{113,17},{16,24},{121,25},{56,3... | collective-permute-start | bytes 1327112 | tf_op jit(solution)/shard_map/ppermute | solution.py:400
  9.4 5.0 %copy-start.11 = (s32[16,1]{0,1:T(1,128)S(1)}, s32[16,1]{0,1:T(1,128)}, u32[]{:S(2)}) copy-start(s32[16,1]{0,1:T(1,128)} %param.19) | copy-start | bytes 196
  9.4 5.2 %copy-start.10 = (s32[4]{0:T(128)S(1)}, s32[4]{0:T(128)}, u32[]{:S(2)}) copy-start(s32[4]{0:T(128)} %param.15) | copy-start | bytes 52
  9.4 5.4 %copy-start.9 = (s32[16]{0:T(128)S(1)}, s32[16]{0:T(128)}, u32[]{:S(2)}) copy-start(s32[16]{0:T(128)} %param.20) | copy-start | bytes 196
  12.6 3.7 %collective-permute-start = (bf16[96,576]{1,0:T(8,128)(2,1)S(1)}, bf16[96,576]{1,0:T(8,128)(2,1)S(1)}, u32[]{:S(2)}, u32[]{:S(2)}) collective-permute-start(bf16[96,576]{1,0:T(8,128)(2,1)S(1)} %pad_maximum_fusion.3), channel_id=1, source_target_pairs={{0,1},{1,0},{2,3},{3,2},{4,5},{5,4},{6,7},{7,6},{8,9},{9,8},{10,11... | collective-permute-start | bytes 331784 | tf_op jit(solution)/shard_map/ppermute | solution.py:383
  14.6 8.2 %copy-start.8 = (s32[16]{0:T(128)}, s32[16]{0:T(128)S(1)}, u32[]{:S(2)}) copy-start(s32[16]{0:T(128)S(1)} %multiply_add_fusion.slot) | copy-start | bytes 196
  22.8 15.8 %collective-permute-start.6 = (bf16[96,576]{1,0:T(8,128)(2,1)S(1)}, bf16[96,576]{1,0:T(8,128)(2,1)}, u32[]{:S(2)}, u32[]{:S(2)}) collective-permute-start(bf16[96,576]{1,0:T(8,128)(2,1)S(1)} %add_convert_fusion), channel_id=1, source_target_pairs={{6,0},{0,2},{2,4},{4,6},{7,1},{1,3},{3,5},{5,7},{14,8},{8,10},{10,... | collective-permute-start | bytes 331784 | tf_op jit(solution)/shard_map/ppermute | solution.py:387
  24.1 17.1 %collective-permute-start.5 = (bf16[96,576]{1,0:T(8,128)(2,1)S(1)}, bf16[96,576]{1,0:T(8,128)(2,1)}, u32[]{:S(2)}, u32[]{:S(2)}) collective-permute-start(bf16[96,576]{1,0:T(8,128)(2,1)S(1)} %add_convert_fusion), channel_id=1, source_target_pairs={{4,0},{6,2},{0,4},{2,6},{5,1},{7,3},{1,5},{3,7},{12,8},{14,10},{8,... | collective-permute-start | bytes 331784 | tf_op jit(solution)/shard_map/ppermute | solution.py:387
  26.7 14.5 %collective-permute-start.4 = (bf16[96,576]{1,0:T(8,128)(2,1)S(1)}, bf16[96,576]{1,0:T(8,128)(2,1)}, u32[]{:S(2)}, u32[]{:S(2)}) collective-permute-start(bf16[96,576]{1,0:T(8,128)(2,1)S(1)} %add_convert_fusion), channel_id=1, source_target_pairs={{2,0},{4,2},{6,4},{0,6},{3,1},{5,3},{7,5},{1,7},{10,8},{12,10},{14... | collective-permute-start | bytes 331784 | tf_op jit(solution)/shard_map/ppermute | solution.py:387
  27.9 79.7 %collective-permute-start.16 = (bf16[4,4,96,576]{3,2,1,0:T(8,128)(2,1)}, bf16[4,4,96,576]{3,2,1,0:T(8,128)(2,1)}, u32[]{:S(2)}, u32[]{:S(2)}) collective-permute-start(bf16[4,4,96,576]{3,2,1,0:T(8,128)(2,1)} %pad_maximum_fusion.rest_0_), channel_id=1, source_target_pairs={{96,0},{25,1},{104,8},{1,9},{112,16},{9,17},{120,24},{17,25},{0,32... | collective-permute-start | bytes 5308424 | tf_op jit(solution)/shard_map/ppermute | solution.py:400
  29.0 79.1 %collective-permute-start.15 = (bf16[4,4,96,576]{3,2,1,0:T(8,128)(2,1)}, bf16[4,4,96,576]{3,2,1,0:T(8,128)(2,1)}, u32[]{:S(2)}, u32[]{:S(2)}) collective-permute-start(bf16[4,4,96,576]{3,2,1,0:T(8,128)(2,1)} %pad_maximum_fusion.rest_0_), channel_id=1, source_target_pairs={{64,0},{17,1},{72,8},{25,9},{80,16},{1,17},{88,24},{9,25},{96,32},... | collective-permute-start | bytes 5308424 | tf_op jit(solution)/shard_map/ppermute | solution.py:400
  33.8 8.7 %copy-start.7 = (f32[512]{0:T(512)S(1)}, f32[512]{0:T(512)}, u32[]{:S(2)}) copy-start(f32[512]{0:T(512)} %param.22) | copy-start | bytes 6148
  33.8 73.7 %all-to-all-start = ((bf16[16,64,640]{2,1,0:T(8,128)(2,1)}), bf16[16,64,640]{2,1,0:T(8,128)(2,1)S(1)}, u32[]{:S(2)}, u32[]{:S(2)}) async-start(bf16[16,64,640]{2,1,0:T(8,128)(2,1)} %bitcast.82), calls=%async_computation | async-start | bytes 2621440 | tf_op jit(solution)/shard_map/all_to_all | solution.py:499
  38.6 69.6 %collective-permute-start.14 = (bf16[4,4,96,576]{3,2,1,0:T(8,128)(2,1)}, bf16[4,4,96,576]{3,2,1,0:T(8,128)(2,1)}, u32[]{:S(2)}, u32[]{:S(2)}) collective-permute-start(bf16[4,4,96,576]{3,2,1,0:T(8,128)(2,1)} %pad_maximum_fusion.rest_0_), channel_id=1, source_target_pairs={{32,0},{9,1},{40,8},{17,9},{48,16},{25,17},{56,24},{1,25},{64,32},... | collective-permute-start | bytes 5308424 | tf_op jit(solution)/shard_map/ppermute | solution.py:400
  42.9 6.1 %collective-permute-start.9 = (bf16[4,16,576]{2,1,0:T(8,128)(2,1)S(1)}, bf16[4,16,576]{2,1,0:T(8,128)(2,1)S(1)}, u32[]{:S(2)}, u32[]{:S(2)}) collective-permute-start(bf16[4,16,576]{2,1,0:T(8,128)(2,1)S(1)} %bitcast.87), channel_id=1, source_target_pairs={{24,0},{97,1},{0,8},{105,9},{8,16},{113,17},{16,24},{121,25},{56,3... | collective-permute-start | bytes 221192 | tf_op jit(solution)/shard_map/ppermute | solution.py:400
  44.2 11.0 %collective-permute-start.8 = (bf16[4,16,576]{2,1,0:T(8,128)(2,1)S(1)}, bf16[4,16,576]{2,1,0:T(8,128)(2,1)S(1)}, u32[]{:S(2)}, u32[]{:S(2)}) collective-permute-start(bf16[4,16,576]{2,1,0:T(8,128)(2,1)S(1)} %bitcast.88), channel_id=1, source_target_pairs={{16,0},{65,1},{24,8},{73,9},{0,16},{81,17},{8,24},{89,25},{48,32},... | collective-permute-start | bytes 221192 | tf_op jit(solution)/shard_map/ppermute | solution.py:400
  49.0 19.5 %collective-permute-start.7 = (bf16[4,16,576]{2,1,0:T(8,128)(2,1)S(1)}, bf16[4,16,576]{2,1,0:T(8,128)(2,1)S(1)}, u32[]{:S(2)}, u32[]{:S(2)}) collective-permute-start(bf16[4,16,576]{2,1,0:T(8,128)(2,1)S(1)} %bitcast.89), channel_id=1, source_target_pairs={{8,0},{33,1},{16,8},{41,9},{24,16},{49,17},{0,24},{57,25},{40,32},... | collective-permute-start | bytes 221192 | tf_op jit(solution)/shard_map/ppermute | solution.py:400
  68.6 38.1 %collective-permute-start.12 = (bf16[4,4,16,576]{3,2,1,0:T(8,128)(2,1)S(1)}, bf16[4,4,16,576]{3,2,1,0:T(8,128)(2,1)S(1)}, u32[]{:S(2)}, u32[]{:S(2)}) collective-permute-start(bf16[4,4,16,576]{3,2,1,0:T(8,128)(2,1)S(1)} %pad_maximum_fusion.2), channel_id=1, source_target_pairs={{96,0},{25,1},{104,8},{1,9},{112,16},{9,17},{120,24},{17,25},{0,32... | collective-permute-start | bytes 884744 | tf_op jit(solution)/shard_map/ppermute | solution.py:400
  71.0 23.1 %collective-permute-start.10 = (bf16[4,4,16,576]{3,2,1,0:T(8,128)(2,1)S(1)}, bf16[4,4,16,576]{3,2,1,0:T(8,128)(2,1)S(1)}, u32[]{:S(2)}, u32[]{:S(2)}) collective-permute-start(bf16[4,4,16,576]{3,2,1,0:T(8,128)(2,1)S(1)} %pad_maximum_fusion.2), channel_id=1, source_target_pairs={{32,0},{9,1},{40,8},{17,9},{48,16},{25,17},{56,24},{1,25},{64,32},... | collective-permute-start | bytes 884744 | tf_op jit(solution)/shard_map/ppermute | solution.py:400
  94.1 7.4 %collective-permute-start.11 = (bf16[4,4,16,576]{3,2,1,0:T(8,128)(2,1)S(1)}, bf16[4,4,16,576]{3,2,1,0:T(8,128)(2,1)S(1)}, u32[]{:S(2)}, u32[]{:S(2)}) collective-permute-start(bf16[4,4,16,576]{3,2,1,0:T(8,128)(2,1)S(1)} %pad_maximum_fusion.2), channel_id=1, source_target_pairs={{64,0},{17,1},{72,8},{25,9},{80,16},{1,17},{88,24},{9,25},{96,32},... | collective-permute-start | bytes 884744 | tf_op jit(solution)/shard_map/ppermute | solution.py:400
  101.6 32.7 %collective-permute-start.17 = (bf16[4,4,96,576]{3,2,1,0:T(8,128)(2,1)}, bf16[4,4,96,576]{3,2,1,0:T(8,128)(2,1)}, u32[]{:S(2)}, u32[]{:S(2)}) collective-permute-start(bf16[4,4,96,576]{3,2,1,0:T(8,128)(2,1)} %pad_maximum_fusion.rest_0_), channel_id=1, source_target_pairs={{0,1},{1,0},{2,3},{3,2},{4,5},{5,4},{6,7},{7,6},{8,9},{9,8},{10,11... | collective-permute-start | bytes 5308424 | tf_op jit(solution)/shard_map/ppermute | solution.py:383
  107.4 26.8 %collective-permute-start.13 = (bf16[16,4,16,576]{3,2,1,0:T(8,128)(2,1)}, bf16[16,4,16,576]{3,2,1,0:T(8,128)(2,1)}, u32[]{:S(2)}, u32[]{:S(2)}) collective-permute-start(bf16[16,4,16,576]{3,2,1,0:T(8,128)(2,1)} %constant_dynamic-update-slice_fusion.near_ref), channel_id=1, source_target_pairs={{0,1},{1,0},{2,3},{3,2},{4,5},{5,4},{6,7},{7,6},{8,9},{9,8},{10,11... | collective-permute-start | bytes 3538952 | tf_op jit(solution)/shard_map/ppermute | solution.py:383
  107.5 3.7 %copy-start.1 = (bf16[16,64,640]{2,1,0:T(8,128)(2,1)}, bf16[16,64,640]{2,1,0:T(8,128)(2,1)S(1)}, u32[]{:S(2)}) copy-start(bf16[16,64,640]{2,1,0:T(8,128)(2,1)S(1)} %all-to-all-done) | copy-start | bytes 3932164
  107.6 26.7 %collective-permute-start.20 = (bf16[4,4,96,576]{3,2,1,0:T(8,128)(2,1)}, bf16[4,4,96,576]{3,2,1,0:T(8,128)(2,1)}, u32[]{:S(2)}, u32[]{:S(2)}) collective-permute-start(bf16[4,4,96,576]{3,2,1,0:T(8,128)(2,1)} %collective-permute-done.16.rest_3_), channel_id=1, source_target_pairs={{0,1},{1,0},{2,3},{3,2},{4,5},{5,4},{6,7},{7,6},{8,9},{9,8},{10,11... | collective-permute-start | bytes 5308424 | tf_op jit(solution)/shard_map/ppermute | solution.py:383
  108.1 26.1 %collective-permute-start.19 = (bf16[4,4,96,576]{3,2,1,0:T(8,128)(2,1)}, bf16[4,4,96,576]{3,2,1,0:T(8,128)(2,1)}, u32[]{:S(2)}, u32[]{:S(2)}) collective-permute-start(bf16[4,4,96,576]{3,2,1,0:T(8,128)(2,1)} %collective-permute-done.15.rest_2_), channel_id=1, source_target_pairs={{0,1},{1,0},{2,3},{3,2},{4,5},{5,4},{6,7},{7,6},{8,9},{9,8},{10,11... | collective-permute-start | bytes 5308424 | tf_op jit(solution)/shard_map/ppermute | solution.py:383
  108.2 26.0 %collective-permute-start.18 = (bf16[4,4,96,576]{3,2,1,0:T(8,128)(2,1)}, bf16[4,4,96,576]{3,2,1,0:T(8,128)(2,1)}, u32[]{:S(2)}, u32[]{:S(2)}) collective-permute-start(bf16[4,4,96,576]{3,2,1,0:T(8,128)(2,1)} %collective-permute-done.14.rest_1_), channel_id=1, source_target_pairs={{0,1},{1,0},{2,3},{3,2},{4,5},{5,4},{6,7},{7,6},{8,9},{9,8},{10,11... | collective-permute-start | bytes 5308424 | tf_op jit(solution)/shard_map/ppermute | solution.py:383
  108.8 2.3 %copy-start.6 = (s32[32]{0:T(128)}, s32[32]{0:T(128)S(1)}, u32[]{:S(2)}) copy-start(s32[32]{0:T(128)S(1)} %fusion.44.length) | copy-start | bytes 388
  120.2 2.8 %copy-start.5 = (bf16[32,32,128]{2,1,0:T(8,128)(2,1)S(1)}, bf16[32,32,128]{2,1,0:T(8,128)(2,1)}, u32[]{:S(2)}) copy-start(bf16[32,32,128]{2,1,0:T(8,128)(2,1)} %get-tuple-element.15) | copy-start | bytes 786436
  123.8 53.7 %all-to-all-start.1 = ((bf16[16,64,256]{2,1,0:T(8,128)(2,1)}), bf16[16,64,256]{2,1,0:T(8,128)(2,1)S(1)}, u32[]{:S(2)}, u32[]{:S(2)}) async-start(bf16[16,64,256]{2,1,0:T(8,128)(2,1)} %pad_maximum_fusion.1), calls=%async_computation.1 | async-start | bytes 1048576 | tf_op jit(solution)/shard_map/all_to_all | solution.py:530
  170.8 5.3 %copy-start.4 = (bf16[512,512]{1,0:T(8,128)(2,1)S(1)}, bf16[512,512]{1,0:T(8,128)(2,1)}, u32[]{:S(2)}) copy-start(bf16[512,512]{1,0:T(8,128)(2,1)} %get-tuple-element.16) | copy-start | bytes 1572868
  177.5 0.8 copy-start.3

commit v2 on v1

--- a/solution.py
+++ b/solution.py
@@ -86,7 +86,7 @@
         store(i, summed / total, peak * factor + jnp.log2(total))
 
 
-def attend_body(config, chunk, head_local, info, q_ref, dq_ref, near_ref, far_ref, fresh_ref, *rest):
+def first_body(config, chunk, head_local, info, q_ref, dq_ref, near_ref, far_ref, fresh_ref, *rest):
     pieces = rest[:8]
     out_ref, decode_ref, lse_ref, hold, past, arrive = rest[8:]
     step = pl.program_id(0)
@@ -201,8 +201,9 @@
         )
 
 
-def attend_all(info, query, decode_query, pieces, near, far, fresh, lat, factor, head_local):
-    prompts, rows, width = query.shape
+def attend_first(info, query, decode_query, pieces, near, far, fresh, lat, factor, head_local):
+    _, rows, width = query.shape
+    prompts = pieces[0].shape[1]
     decode_rows = decode_query.shape[0]
     piece_rows = pieces[0].shape[2]
     holders = 4 * len(pieces)
@@ -218,7 +219,7 @@
         (lines, None, half_tokens, width), lambda i, _: (0, prompt(i), 0, 0)
     )
     return pl.pallas_call(
-        functools.partial(attend_body, (lat, factor), chunk, head_local),
+        functools.partial(first_body, (lat, factor), chunk, head_local),
         grid_spec=pltpu.PrefetchScalarGridSpec(
             num_scalar_prefetch=1,
             grid=(prompts + 1,),
@@ -252,8 +253,111 @@
             bytes_accessed=2 * prompts * (keys + 2 * rows) * width,
             transcendentals=(prompts * rows + decode_rows) * keys,
         ),
-        name="attend_all",
+        name="attend_first",
     )(info, query, decode_query, near, far, fresh, *pieces)
+
+
+def later_body(config, chunk, head_local, first, info, q_ref, past_ref, near_ref, far_ref, out_ref, hold):
+    step = pl.program_id(0)
+    tile = hold.shape[1]
+    seq_count, _, piece_rows, width = past_ref.shape
+    lines, half_tokens, _ = near_ref.shape
+    held = chunk // (2 * piece_rows)
+    past_count = seq_count // held
+    past_len = info[step + first]
+    z_place, x_place, core = info[5], info[6], info[7]
+
+    def past_keys(j):
+        return lambda: past_ref[j * held : (j + 1) * held].reshape(chunk, width)
+
+    def past_mask(j):
+        def allowed(row):
+            if 2 * (j + 1) <= past_count:
+                return None
+            return lax.broadcasted_iota(jnp.int32, (1, chunk), 1) + j * chunk < past_len
+
+        return allowed
+
+    def group_mask(side):
+        def allowed(row):
+            place = lax.broadcasted_iota(jnp.int32, (1, lines * half_tokens), 1)
+            outer = place // (4 * half_tokens)
+            inner = (place // half_tokens) & 3
+            z_from = (z_place + outer + (inner - outer) * side) & 3
+            x_from = (x_place + inner + (outer - inner) * side) & 3
+            key_token = (z_from * 4 + x_from) * (2 * half_tokens) + side * half_tokens
+            key_token = key_token + (place & (half_tokens - 1))
+            return key_token <= info[4] + row // head_local
+
+        return allowed
+
+    keys = [past_keys(j) for j in range(past_count)]
+    keys += [
+        lambda: near_ref[...].reshape(lines * half_tokens, width),
+        lambda: far_ref[...].reshape(lines * half_tokens, width),
+    ]
+    masks = [past_mask(j) for j in range(past_count)]
+
+    def store(i, value, lse):
+        out_ref[i * tile : (i + 1) * tile, :] = value.astype(jnp.bfloat16)
+
+    def run(count):
+        attend_tiles(
+            config,
+            q_ref.shape[0] // tile,
+            lambda i: q_ref[i * tile : (i + 1) * tile, :],
+            store,
+            hold,
+            keys[:count] + keys[past_count:],
+            masks[:count] + [group_mask(core), group_mask(1 - core)],
+        )
+
+    short = past_len <= (past_count - 1) * chunk
+
+    @pl.when(short)
+    def _():
+        run(past_count - 1)
+
+    @pl.when(jnp.logical_not(short))
+    def _():
+        run(past_count)
+
+
+def attend_later(info, query, past, near, far, first, lat, factor, head_local):
+    prompts, rows, width = query.shape
+    count = prompts - first
+    seq_count, _, halves, piece_rows, _ = past.shape
+    lines, _, half_tokens, _ = near.shape
+    keys = seq_count * halves * piece_rows + 2 * lines * half_tokens
+    tile = 256
+    chunk = 768
+    group_spec = pl.BlockSpec((lines, None, half_tokens, width), lambda i, _: (0, i + first, 0, 0))
+    return pl.pallas_call(
+        functools.partial(later_body, (lat, factor), chunk, head_local, first),
+        grid_spec=pltpu.PrefetchScalarGridSpec(
+            num_scalar_prefetch=1,
+            grid=(count,),
+            in_specs=[
+                pl.BlockSpec((None, rows, width), lambda i, _: (i + first, 0, 0)),
+                pl.BlockSpec(
+                    (seq_count, None, halves, piece_rows, width),
+                    lambda i, _: (0, i + first, 0, 0, 0),
+                ),
+                group_spec,
+                group_spec,
+            ],
+            out_specs=pl.BlockSpec((None, rows, lat), lambda i, _: (i, 0, 0)),
+            scratch_shapes=[pltpu.VMEM((2, tile, keys), jnp.float32)],
+        ),
+        out_shape=jax.ShapeDtypeStruct((count, rows, lat), jnp.bfloat16),
+        compiler_params=pltpu.CompilerParams(vmem_limit_bytes=VMEM_BYTES),
+        cost_estimate=pl.CostEstimate(
+            flops=2 * count * rows * keys * (768 + lat),
+            bytes_accessed=2 * count * (keys + 2 * rows) * width,
+            transcendentals=count * rows * keys,
+        ),
+        name="attend_later",
+    )(info, query, past, near, far)
 
 
 def dispatch_body(source, length, q_ref, out_ref):
@@ -416,6 +520,7 @@
 ):
     seq_count = lax.axis_size("seq")
     seq_place = lax.axis_index("seq")
+    tp_place = lax.axis_index("tp")
     core = lax.axis_index("grp")
     z_place, x_place = seq_place >> 2, seq_place & 3
     prompt_count, group_local, head_local, row_width = group_query.shape
@@ -429,7 +534,12 @@
     factor = (value_width + row_width - lat) ** (-0.5) * log2_e
 
     half = past_local // 2
-    past_half = lax.dynamic_slice_in_dim(past_cache, core * half, half, axis=1)
+    past_part = lax.dynamic_slice(past_cache, (tp_place, core * half, 0), (1, half, row_width))
+    past_all = lax.all_gather(
+        past_part.reshape(half, row_width), ("seq", "tp", "grp"), axis=0, tiled=False
+    ).reshape(seq_count, prompt_count, 2, half, row_width)
+
+    past_half = lax.dynamic_slice(past_cache, (0, core * half, 0), (1, half, row_width))
     past_line = [past_half] + [fetch_ring(past_half, shift, 0) for shift in range(1, 4)]
     past_line = jnp.stack(past_line)
     past_lines = [past_line] + [fetch_ring(past_line, shift, 1) for shift in range(1, 4)]
@@ -456,7 +566,7 @@
     pair_sum = both(core).astype(jnp.float32) + swap_core(both(1 - core)).astype(jnp.float32)
     pair_sum = pair_sum.astype(jnp.bfloat16)
 
-    pair_sum, decode_query, _ = lax.optimization_barrier((pair_sum, decode_query, past_line))
+    pair_sum, _ = lax.optimization_barrier((pair_sum, past_line))
     latent = pair_sum.astype(jnp.float32)
     for shift in range(1, 4):
         latent = latent + fetch_tp(pair_sum, shift).astype(jnp.float32)
@@ -539,11 +649,12 @@
         [past_len[p] for p in range(prompt_count)]
         + [seq_place * group_local, z_place, x_place, core]
     ).astype(jnp.int32)
-    group_query, _ = lax.optimization_barrier((group_query, cache_value))
-    prefill_latent, near_latent, near_lse = attend_all(
+    queries = group_query.reshape(prompt_count, group_local * head_local, row_width)
+    decode_rows, _ = lax.optimization_barrier((decode_query, cache_value))
+    first_latent, near_latent, near_lse = attend_first(
         info,
-        group_query.reshape(prompt_count, group_local * head_local, row_width),
-        decode_query.reshape(request_local * query_pairs, row_width),
+        queries,
+        decode_rows.reshape(request_local * query_pairs, row_width),
         past_lines,
         group_near,
         group_far,
@@ -565,12 +676,21 @@
         near_lse.reshape(request_local, query_pairs, 128),
     ).reshape(request_local, 2, head_local, value_width)
 
-    prefill_out = jnp.einsum(
-        "pthc,hcv->pthv",
-        prefill_latent.reshape(prompt_count, group_local, head_local, lat),
-        w_value,
-        preferred_element_type=jnp.float32,
-    ).astype(jnp.bfloat16)
+    queries, _ = lax.optimization_barrier((queries, decode_out))
+    later_latent = attend_later(
+        info, queries, past_all, group_near, group_far, 1, lat, factor, head_local
+    )
+    prefill_out = jnp.concatenate(
+        [
+            jnp.einsum(
+                "pthc,hcv->pthv",
+                value.reshape(-1, group_local, head_local, lat),
+                w_value,
+                preferred_element_type=jnp.float32,
+            ).astype(jnp.bfloat16)
+            for value in (first_latent, later_latent)
+        ]
+    )
     return (prefill_out, decode_out)
 
 

time: 182 us -> 161 us (0.88)
  waiting for transfers between devices: 45.5 us -> 17.9 us
  between operations: 1.69 us -> 15.1 us
  starting transfers between devices: 51 us -> 40.4 us
  Pallas kernels: 50.8 us -> 55.1 us
    ppermute x12, waiting for transfers between devices: 45.5 us -> 12.7 us  [fetch_ring(): return lax.ppermute(value, ('seq', 'grp'), moves)]
    ppermute x12, starting transfers between devices: 24.6 us -> 18.8 us  [fetch_ring(): return lax.ppermute(value, ('seq', 'grp'), moves)]
    ppermute x3, waiting for transfers between devices: 0.01 us -> 5.11 us  [fetch_tp(): return lax.ppermute(value, 'tp', [((i + shift) % 4, i) for i in range(4)])]
    all_to_all x1, starting transfers between devices: 10.4 us -> 6.11 us  [on_device(): lax.all_to_all(back.reshape(seq_count, pair_limit * query_pairs, 2 * valu...]
    pallas_call x1 -> x2, Pallas kernels: 36.5 us -> 39.8 us  [the longest x1 21.5 us: attend_later(): pl.pallas_call(functools.partial(later_body, (lat, factor), chunk, head_l...]
    all_to_all x1, starting transfers between devices: 4.84 us -> 6.94 us  [on_device(): lax.all_to_all(send_query.reshape(seq_count, pair_limit * query_pairs, ro...]
    dot_general x1 -> x2, matrix products: 4.12 us -> 3.89 us  [on_device(): jnp.einsum('pthc,hcv->pthv', value.reshape(-1, group_local, head_local, l...]
    unnamed x31 -> x35, local copies, waits for them, and re-layouts: 6.07 us -> 6.08 us
  transfers between devices with their start and end apart: 23 -> 24, of which waited for: 6 -> 8; matrix products, arithmetic and copies ran while one was open for 15% -> 15% of each run, Pallas kernels for 26% -> 21%
where the time goes in v2:
time: 161 us; the launch traced here: 160 us
  Pallas kernels  55.1 us (34%)
  starting transfers between devices  40.4 us (25%)
  waiting for transfers between devices  17.9 us (11%)
  between operations  15.1 us (9%)
  local copies, waits for them, and re-layouts  12.6 us (8%)
  matrix products  10.3 us (6%)
  other arithmetic  8.91 us (6%)
    pallas_call x1, Pallas kernels, attend_later(): pl.pallas_call(functools.partial(later_body, (lat, factor), chunk, head_l...  21.5 us
    ppermute x12, starting transfers between devices, fetch_ring(): return lax.ppermute(value, ('seq', 'grp'), moves)  18.8 us
    pallas_call x1, Pallas kernels, attend_first(): pl.pallas_call(functools.partial(first_body, (lat, factor), chunk, head_l...  18.3 us
    ppermute x12, waiting for transfers between devices, fetch_ring(): return lax.ppermute(value, ('seq', 'grp'), moves)  12.7 us
    pallas_call x1, Pallas kernels, attend_cache(): pl.pallas_call(functools.partial(cache_body, lat, factor, batch), grid_sp...  9.91 us
    all_to_all x1, starting transfers between devices, on_device(): lax.all_to_all(send_query.reshape(seq_count, pair_limit * query_pairs, ro...  6.94 us
    all_to_all x1, starting transfers between devices, on_device(): lax.all_to_all(back.reshape(seq_count, pair_limit * query_pairs, 2 * valu...  6.11 us
    unnamed x35, local copies, waits for them, and re-layouts  6.08 us
  transfers between devices with their start and end apart: 24, of which 8 were waited for; matrix products, arithmetic and copies ran while one was open for 15% of the time, Pallas kernels for 21%

profile of v2, /device:TPU:1, one launch (start us, length us, event | category | flops | bytes accessed | tf_op | source)
XLA Modules:
  0.0 160.2 jit_solution(4387477197308747923)
XLA Ops:
  7.2 1.8 %constant_dynamic-slice_fusion = (bf16[1,96,576]{2,1,0:T(8,128)(2,1)}, bf16[1,96,576]{2,1,0:T(8,128)(2,1)S(1)}) fusion(bf16[4,192,576]{2,1,0:T(8,128)(2,1)} %param.14, s32[]{:T(128)S(6)} %select_n.31, s32[]{:T(128)S(6)} %select_n.30), kind=kLoop, calls=%fused_computation.70 | loop fusion | bytes 442376 | tf_op jit(solution)/shard_map/dynamic_slice | solution.py:537
  9.1 4.7 %collective-permute-start.1 = (bf16[1,96,576]{2,1,0:T(8,128)(2,1)S(1)}, bf16[1,96,576]{2,1,0:T(8,128)(2,1)}, u32[]{:S(2)}, u32[]{:S(2)}) collective-permute-start(bf16[1,96,576]{2,1,0:T(8,128)(2,1)S(1)} %get-tuple-element.31), channel_id=1, source_target_pairs={{8,0},{33,1},{16,8},{41,9},{24,16},{49,17},{0,24},{57,25},{40,32},... | collective-permute-start | bytes 331784 | tf_op jit(solution)/shard_map/ppermute | solution.py:504
  13.7 0.7 collective-permute-start.3
  14.4 1.5 reshape.188
  15.9 1.8 %convolution_convert_fusion = bf16[4,32,576]{2,1,0:T(8,128)(2,1)S(1)} fusion(bf16[4,32,896]{2,1,0:T(8,128)(2,1)} %param.12, bf16[896,576]{0,1:T(8,128)(2,1)} %param.21), kind=kOutput, calls=%fused_computation.12 | convolution fusion | flops 132194304 | bytes 1409024 | tf_op jit(solution)/shard_map/ptd,dc->ptc/dot_general | solution.py:550
  17.7 0.7 constant_dynamic-slice_fusion.3
  18.4 0.4 convolution_convert_fusion.2
  18.8 0.7 pad_maximum_fusion.4
  19.5 0.7 collective-permute-start
  20.2 0.2 convert_reduce_fusion
  20.4 0.6 select_reduce_fusion.1
  21.0 2.4 %dispatch_queries.1 = bf16[32,32,640]{2,1,0:T(8,128)(2,1)} custom-call(s32[32]{0:T(128)} %get-tuple-element.29.source, s32[32]{0:T(128)} %get-tuple-element.28.length, bf16[16,32,576]{2,1,0:T(8,128)(2,1)} %bitcast.102), custom_call_target="tpu_custom_call" | custom-call | tf_op jit(solution)/shard_map/dispatch_queries/pallas_call | solution.py:379
  23.4 6.9 %all-to-all-start = ((bf16[16,64,640]{2,1,0:T(8,128)(2,1)}), bf16[16,64,640]{2,1,0:T(8,128)(2,1)S(1)}, u32[]{:S(2)}, u32[]{:S(2)}) async-start(bf16[16,64,640]{2,1,0:T(8,128)(2,1)} %bitcast.92), calls=%async_computation | async-start | bytes 2621440 | tf_op jit(solution)/shard_map/all_to_all | solution.py:609
  30.7 0.6 stack.46.info
  31.3 1.9 %pad_maximum_fusion.2.rest_0_ = bf16[4,1,96,576]{3,2,1,0:T(8,128)(2,1)} fusion(bf16[1,1,96,576]{3,2,1,0:T(8,128)(2,1)} %bitcast.24, bf16[1,1,96,576]{3,2,1,0:T(8,128)(2,1)} %bitcast.23, bf16[1,1,96,576]{3,2,1,0:T(8,128)(2,1)} %bitcast.22, bf16[1,1,96,576]{3,2,1,0:T(8,128)(2,1)S(1)} %bitcast.107), kind=kLoop, calls=%fused_computation.22 | loop fusion | flops 663552 | bytes 884736 | tf_op jit(solution)/shard_map/stack | solution.py:544
  33.2 1.0 add_convert_fusion
  34.2 2.8 %collective-permute-start.4 = (bf16[96,576]{1,0:T(8,128)(2,1)S(1)}, bf16[96,576]{1,0:T(8,128)(2,1)S(1)}, u32[]{:S(2)}, u32[]{:S(2)}) collective-permute-start(bf16[96,576]{1,0:T(8,128)(2,1)S(1)} %add_convert_fusion), channel_id=1, source_target_pairs={{2,0},{4,2},{6,4},{0,6},{3,1},{5,3},{7,5},{1,7},{10,8},{12,10},{14... | collective-permute-start | bytes 331784 | tf_op jit(solution)/shard_map/ppermute | solution.py:491
  37.1 0.3 collective-permute-start.5
  37.4 0.7 collective-permute-start.6
  38.2 2.6 %collective-permute-start.14 = (bf16[4,1,96,576]{3,2,1,0:T(8,128)(2,1)}, bf16[4,1,96,576]{3,2,1,0:T(8,128)(2,1)}, u32[]{:S(2)}, u32[]{:S(2)}) collective-permute-start(bf16[4,1,96,576]{3,2,1,0:T(8,128)(2,1)} %pad_maximum_fusion.2.rest_0_), channel_id=1, source_target_pairs={{32,0},{9,1},{40,8},{17,9},{48,16},{25,17},{56,24},{1,25},{64,32},... | collective-permute-start | bytes 1327112 | tf_op jit(solution)/shard_map/ppermute | solution.py:504
  40.7 0.6 collective-permute-start.15
  41.3 0.7 collective-permute-done.4
  42.0 0.8 collective-permute-done.5
  42.9 3.5 %collective-permute-done.6 = bf16[96,576]{1,0:T(8,128)(2,1)S(1)} collective-permute-done((bf16[96,576]{1,0:T(8,128)(2,1)S(1)}, bf16[96,576]{1,0:T(8,128)(2,1)S(1)}, u32[]{:S(2)}, u32[]{:S(2)}) %collective-permute-start.6) | collective-permute-done | bytes 110624 | tf_op jit(solution)/shard_map/ppermute | solution.py:491
  46.6 0.3 fusion.41
  47.1 2.7 %collective-permute-start.7 = (bf16[4,16,576]{2,1,0:T(8,128)(2,1)S(1)}, bf16[4,16,576]{2,1,0:T(8,128)(2,1)S(1)}, u32[]{:S(2)}, u32[]{:S(2)}) collective-permute-start(bf16[4,16,576]{2,1,0:T(8,128)(2,1)S(1)} %bitcast.97), channel_id=1, source_target_pairs={{8,0},{33,1},{16,8},{41,9},{24,16},{49,17},{0,24},{57,25},{40,32},... | collective-permute-start | bytes 221192 | tf_op jit(solution)/shard_map/ppermute | solution.py:504
  49.8 0.4 collective-permute-start.8
  50.2 0.6 collective-permute-start.9
  50.8 0.8 fusion.35.fresh_ref
  51.6 0.6 constant_dynamic-update-slice_fusion.6
  52.2 0.4 collective-permute-done.7
  52.6 1.1 collective-permute-start.16
  53.8 2.2 %collective-permute-done.8 = bf16[4,16,576]{2,1,0:T(8,128)(2,1)S(1)} collective-permute-done((bf16[4,16,576]{2,1,0:T(8,128)(2,1)S(1)}, bf16[4,16,576]{2,1,0:T(8,128)(2,1)S(1)}, u32[]{:S(2)}, u32[]{:S(2)}) %collective-permute-start.8) | collective-permute-done | bytes 73760 | tf_op jit(solution)/shard_map/ppermute | solution.py:504
  55.9 0.9 collective-permute-done.9
  56.9 1.8 %collective-permute-start.10 = (bf16[4,4,16,576]{3,2,1,0:T(8,128)(2,1)S(1)}, bf16[4,4,16,576]{3,2,1,0:T(8,128)(2,1)S(1)}, u32[]{:S(2)}, u32[]{:S(2)}) collective-permute-start(bf16[4,4,16,576]{3,2,1,0:T(8,128)(2,1)S(1)} %pad_maximum_fusion.3), channel_id=1, source_target_pairs={{32,0},{9,1},{40,8},{17,9},{48,16},{25,17},{56,24},{1,25},{64,32},... | collective-permute-start | bytes 884744 | tf_op jit(solution)/shard_map/ppermute | solution.py:504
  58.7 0.9 collective-permute-start.11
  59.6 0.6 constant_dynamic-update-slice_fusion.5
  60.2 0.6 constant_dynamic-update-slice_fusion.4
  60.9 5.5 %collective-permute-done.10 = bf16[4,4,16,576]{3,2,1,0:T(8,128)(2,1)S(1)} collective-permute-done((bf16[4,4,16,576]{3,2,1,0:T(8,128)(2,1)S(1)}, bf16[4,4,16,576]{3,2,1,0:T(8,128)(2,1)S(1)}, u32[]{:S(2)}, u32[]{:S(2)}) %collective-permute-start.10) | collective-permute-done | bytes 294944 | tf_op jit(solution)/shard_map/ppermute | solution.py:504
  66.4 2.8 %collective-permute-start.12 = (bf16[4,4,16,576]{3,2,1,0:T(8,128)(2,1)S(1)}, bf16[4,4,16,576]{3,2,1,0:T(8,128)(2,1)S(1)}, u32[]{:S(2)}, u32[]{:S(2)}) collective-permute-start(bf16[4,4,16,576]{3,2,1,0:T(8,128)(2,1)S(1)} %pad_maximum_fusion.3), channel_id=1, source_target_pairs={{96,0},{25,1},{104,8},{1,9},{112,16},{9,17},{120,24},{17,25},{0,32... | collective-permute-start | bytes 884744 | tf_op jit(solution)/shard_map/ppermute | solution.py:504
  69.1 0.6 constant_dynamic-update-slice_fusion.3
  69.8 0.8 constant_dynamic-update-slice_fusion.2
  70.6 1.8 %collective-permute-start.17 = (bf16[4,1,96,576]{3,2,1,0:T(8,128)(2,1)}, bf16[4,1,96,576]{3,2,1,0:T(8,128)(2,1)}, u32[]{:S(2)}, u32[]{:S(2)}) collective-permute-start(bf16[4,1,96,576]{3,2,1,0:T(8,128)(2,1)} %pad_maximum_fusion.2.rest_0_), channel_id=1, source_target_pairs={{0,1},{1,0},{2,3},{3,2},{4,5},{5,4},{6,7},{7,6},{8,9},{9,8},{10,11... | collective-permute-start | bytes 1327112 | tf_op jit(solution)/shard_map/ppermute | solution.py:487
  72.5 0.4 collective-permute-start.19
  72.9 0.3 collective-permute-start.20
  73.2 0.8 constant_dynamic-update-slice_fusion.1
  73.9 3.7 %collective-permute-done.12 = bf16[4,4,16,576]{3,2,1,0:T(8,128)(2,1)S(1)} collective-permute-done((bf16[4,4,16,576]{3,2,1,0:T(8,128)(2,1)S(1)}, bf16[4,4,16,576]{3,2,1,0:T(8,128)(2,1)S(1)}, u32[]{:S(2)}, u32[]{:S(2)}) %collective-permute-start.12) | collective-permute-done | bytes 294944 | tf_op jit(solution)/shard_map/ppermute | solution.py:504
  77.6 0.8 constant_dynamic-update-slice_fusion.near_ref
  78.4 1.3 collective-permute-start.13
  80.0 0.7 convert_reduce_fusion.1
  81.6 0.7 select_reduce_fusion.order
  82.3 9.9 %attend_cache.1 = (bf16[32,32,512]{2,1,0:T(8,128)(2,1)}, bf16[32,32,128]{2,1,0:T(8,128)(2,1)}) custom-call(s32[32]{0:T(128)} %select_reduce_fusion.order, s32[32]{0:T(128)} %copy-done.8, s32[1]{0:T(128)} %bitcast.10.used, bf16[32,32,640]{2,1,0:T(8,128)(2,1)} %bitcast.91, bf16[32,576,384]{2,1,0:T(8,128)(2,1)} %bitcast.86, bf16[32,576,384]{2,1,0:T(8,128)(2,1)} %bitcast.87, ...), custom_call_target="tpu_custom_call" | custom-call | flops 3422552064 | bytes 14155776 | tf_op jit(solution)/shard_map/attend_cache/pallas_call | solution.py:432
  92.2 2.6 %fusion.23 = bf16[32,2,16,128]{3,0,1,2:T(8,128)(2,1)S(1)} fusion(bf16[16,512,128]{2,1,0:T(8,128)(2,1)S(1)} %copy-done, bf16[32,2,16,512]{3,2,1,0:T(8,128)(2,1)} %bitcast.94), kind=kOutput, calls=%fused_computation.11 | convolution fusion | flops 134348800 | bytes 3407872 | tf_op jit(solution)/shard_map/nshc,hcv->nshv/dot_general | solution.py:631
  95.0 0.9 pad_maximum_fusion
  95.9 6.1 %all-to-all-start.1 = ((bf16[16,64,256]{2,1,0:T(8,128)(2,1)}), bf16[16,64,256]{2,1,0:T(8,128)(2,1)S(1)}, u32[]{:S(2)}, u32[]{:S(2)}) async-start(bf16[16,64,256]{2,1,0:T(8,128)(2,1)} %pad_maximum_fusion), calls=%async_computation.1 | async-start | bytes 1048576 | tf_op jit(solution)/shard_map/all_to_all | solution.py:640
  102.1 18.3 %attend_first.1 = (bf16[1,512,512]{2,1,0:T(8,128)(2,1)}, bf16[512,512]{1,0:T(8,128)(2,1)}, f32[512,128]{1,0:T(8,128)}) custom-call(s32[8]{0:T(128)} %stack.46.info, bf16[4,512,576]{2,1,0:T(8,128)(2,1)} %bitcast.120, bf16[512,576]{1,0:T(8,128)(2,1)} %bitcast.103, bf16[16,4,16,576]{3,2,1,0:T(8,128)(2,1)} %constant_dynamic-update-slice_fusion.near_ref, ...), custom_call_target="tpu_custom_call" | custom-call | flops 9730785280 | bytes 5455872 | tf_op jit(solution)/shard_map/attend_first/pallas_call | solution.py:221
  120.4 1.6 fusion.20
  122.0 0.9 copy.60
  122.9 0.8 copy-done.3
  123.7 3.0 %merge_decode.1 = bf16[16,32,128]{2,1,0:T(8,128)(2,1)} custom-call(s32[16]{0:T(128)} %copy-done.10, bf16[32,32,256]{2,1,0:T(8,128)(2,1)} %bitcast.93, f32[16,32,128]{2,1,0:T(8,128)} %bitcast.95, f32[16,32,128]{2,1,0:T(8,128)} %bitcast.115), custom_call_target="tpu_custom_call" | custom-call | tf_op jit(solution)/shard_map/merge_decode/pallas_call | solution.py:476
  126.7 0.6 fusion.26
  127.3 21.5 %attend_later.1 = bf16[3,512,512]{2,1,0:T(8,128)(2,1)} custom-call(s32[8]{0:T(128)} %stack.46.info, bf16[4,512,576]{2,1,0:T(8,128)(2,1)} %bitcast.121, bf16[16,4,2,96,576]{4,3,2,1,0:T(8,128)(2,1)} %bitcast.119, bf16[16,4,16,576]{3,2,1,0:T(8,128)(2,1)} %constant_dynamic-update-slice_fusion.near_ref, bf16[16,4,16,576]{3,2,1,0:T(8,128)(2,1)} %collective-permute-done.13.far_ref), custom_call_target="tpu_custom_call" | custom-call | flops 14092861440 | bytes 15925248 | tf_op jit(solution)/shard_map/attend_later/pallas_call | solution.py:335
  148.8 3.3 %fusion.12 = bf16[3,32,16,128]{3,1,0,2:T(8,128)(2,1)S(1)} fusion(bf16[16,512,128]{2,1,0:T(8,128)(2,1)S(1)} %copy-done, bf16[3,32,16,512]{3,2,1,0:T(8,128)(2,1)} %bitcast.123), kind=kOutput, calls=%fused_computation.8 | convolution fusion | flops 201523200 | bytes 4063232 | tf_op jit(solution)/shard_map/pthc,hcv->pthv/dot_general | solution.py:685
  152.2 1.1 copy.63
  (71 shorter events, 1.9 us)
Async XLA Ops:
  7.2 85.1 %copy-start = (bf16[16,512,128]{2,1,0:T(8,128)(2,1)S(1)}, bf16[16,512,128]{2,1,0:T(8,128)(2,1)}, u32[]{:S(2)}) copy-start(bf16[16,512,128]{2,1,0:T(8,128)(2,1)} %param.23) | copy-start | bytes 6291460
  7.2 11.2 %copy-start.2 = (bf16[896,576]{0,1:T(8,128)(2,1)S(1)}, bf16[896,576]{0,1:T(8,128)(2,1)}, u32[]{:S(2)}) copy-start(bf16[896,576]{0,1:T(8,128)(2,1)} %param.21) | copy-start | bytes 3096580
  7.2 120.1 %all-gather.2.cloned.1.call-start = ((), (), s32[]{:S(2)}) async-start(), calls=%async_computation.2 | async-start | bytes 15851520 | tf_op jit(solution)/shard_map/all_gather | solution.py:538
  9.1 22.3 %collective-permute-start.1 = (bf16[1,96,576]{2,1,0:T(8,128)(2,1)S(1)}, bf16[1,96,576]{2,1,0:T(8,128)(2,1)}, u32[]{:S(2)}, u32[]{:S(2)}) collective-permute-start(bf16[1,96,576]{2,1,0:T(8,128)(2,1)S(1)} %get-tuple-element.31), channel_id=1, source_target_pairs={{8,0},{33,1},{16,8},{41,9},{24,16},{49,17},{0,24},{57,25},{40,32},... | collective-permute-start | bytes 331784 | tf_op jit(solution)/shard_map/ppermute | solution.py:504
  13.7 17.6 %collective-permute-start.2 = (bf16[1,96,576]{2,1,0:T(8,128)(2,1)S(1)}, bf16[1,96,576]{2,1,0:T(8,128)(2,1)}, u32[]{:S(2)}, u32[]{:S(2)}) collective-permute-start(bf16[1,96,576]{2,1,0:T(8,128)(2,1)S(1)} %get-tuple-element.31), channel_id=1, source_target_pairs={{16,0},{65,1},{24,8},{73,9},{0,16},{81,17},{8,24},{89,25},{48,32},... | collective-permute-start | bytes 331784 | tf_op jit(solution)/shard_map/ppermute | solution.py:504
  13.7 17.6 %collective-permute-start.3 = (bf16[1,96,576]{2,1,0:T(8,128)(2,1)S(1)}, bf16[1,96,576]{2,1,0:T(8,128)(2,1)}, u32[]{:S(2)}, u32[]{:S(2)}) collective-permute-start(bf16[1,96,576]{2,1,0:T(8,128)(2,1)S(1)} %get-tuple-element.31), channel_id=1, source_target_pairs={{24,0},{97,1},{0,8},{105,9},{8,16},{113,17},{16,24},{121,25},{56,3... | collective-permute-start | bytes 331784 | tf_op jit(solution)/shard_map/ppermute | solution.py:504
  15.9 2.5 %copy-start.7 = (bf16[32,896]{1,0:T(8,128)(2,1)S(1)}, bf16[32,896]{1,0:T(8,128)(2,1)}, u32[]{:S(2)}) copy-start(bf16[32,896]{1,0:T(8,128)(2,1)} %reshape.188) | copy-start | bytes 172036
  15.9 4.2 %copy-start.13 = (s32[16,1]{0,1:T(1,128)S(1)}, s32[16,1]{0,1:T(1,128)}, u32[]{:S(2)}) copy-start(s32[16,1]{0,1:T(1,128)} %param.19) | copy-start | bytes 196
  15.9 4.4 %copy-start.11 = (s32[16]{0:T(128)S(1)}, s32[16]{0:T(128)}, u32[]{:S(2)}) copy-start(s32[16]{0:T(128)} %param.20) | copy-start | bytes 196
  18.8 4.5 %copy-start.5 = (bf16[32,576]{1,0:T(8,128)(2,1)}, bf16[32,576]{1,0:T(8,128)(2,1)S(1)}, u32[]{:S(2)}) copy-start(bf16[32,576]{1,0:T(8,128)(2,1)S(1)} %convolution_convert_fusion.2) | copy-start | bytes 110596
  19.5 13.7 %collective-permute-start = (bf16[96,576]{1,0:T(8,128)(2,1)}, bf16[96,576]{1,0:T(8,128)(2,1)}, u32[]{:S(2)}, u32[]{:S(2)}) collective-permute-start(bf16[96,576]{1,0:T(8,128)(2,1)} %pad_maximum_fusion.4), channel_id=1, source_target_pairs={{0,1},{1,0},{2,3},{3,2},{4,5},{5,4},{6,7},{7,6},{8,9},{9,8},{10,11... | collective-permute-start | bytes 331784 | tf_op jit(solution)/shard_map/ppermute | solution.py:487
  20.3 3.0 %copy-start.10 = (s32[16]{0:T(128)}, s32[16]{0:T(128)S(1)}, u32[]{:S(2)}) copy-start(s32[16]{0:T(128)S(1)} %multiply_add_fusion.slot) | copy-start | bytes 196
  23.3 7.0 %copy-start.12 = (s32[4]{0:T(128)S(1)}, s32[4]{0:T(128)}, u32[]{:S(2)}) copy-start(s32[4]{0:T(128)} %param.15) | copy-start | bytes 52
  23.4 56.3 %all-to-all-start = ((bf16[16,64,640]{2,1,0:T(8,128)(2,1)}), bf16[16,64,640]{2,1,0:T(8,128)(2,1)S(1)}, u32[]{:S(2)}, u32[]{:S(2)}) async-start(bf16[16,64,640]{2,1,0:T(8,128)(2,1)} %bitcast.92), calls=%async_computation | async-start | bytes 2621440 | tf_op jit(solution)/shard_map/all_to_all | solution.py:609
  30.3 16.6 %copy-start.9 = (f32[512]{0:T(512)S(1)}, f32[512]{0:T(512)}, u32[]{:S(2)}) copy-start(f32[512]{0:T(512)} %param.22) | copy-start | bytes 6148
  34.2 7.8 %collective-permute-start.4 = (bf16[96,576]{1,0:T(8,128)(2,1)S(1)}, bf16[96,576]{1,0:T(8,128)(2,1)S(1)}, u32[]{:S(2)}, u32[]{:S(2)}) collective-permute-start(bf16[96,576]{1,0:T(8,128)(2,1)S(1)} %add_convert_fusion), channel_id=1, source_target_pairs={{2,0},{4,2},{6,4},{0,6},{3,1},{5,3},{7,5},{1,7},{10,8},{12,10},{14... | collective-permute-start | bytes 331784 | tf_op jit(solution)/shard_map/ppermute | solution.py:491
  37.1 5.8 %collective-permute-start.5 = (bf16[96,576]{1,0:T(8,128)(2,1)S(1)}, bf16[96,576]{1,0:T(8,128)(2,1)S(1)}, u32[]{:S(2)}, u32[]{:S(2)}) collective-permute-start(bf16[96,576]{1,0:T(8,128)(2,1)S(1)} %add_convert_fusion), channel_id=1, source_target_pairs={{4,0},{6,2},{0,4},{2,6},{5,1},{7,3},{1,5},{3,7},{12,8},{14,10},{8,... | collective-permute-start | bytes 331784 | tf_op jit(solution)/shard_map/ppermute | solution.py:491
  37.4 9.0 %collective-permute-start.6 = (bf16[96,576]{1,0:T(8,128)(2,1)S(1)}, bf16[96,576]{1,0:T(8,128)(2,1)S(1)}, u32[]{:S(2)}, u32[]{:S(2)}) collective-permute-start(bf16[96,576]{1,0:T(8,128)(2,1)S(1)} %add_convert_fusion), channel_id=1, source_target_pairs={{6,0},{0,2},{2,4},{4,6},{7,1},{1,3},{3,5},{5,7},{14,8},{8,10},{10,... | collective-permute-start | bytes 331784 | tf_op jit(solution)/shard_map/ppermute | solution.py:491
  38.2 32.4 %collective-permute-start.14 = (bf16[4,1,96,576]{3,2,1,0:T(8,128)(2,1)}, bf16[4,1,96,576]{3,2,1,0:T(8,128)(2,1)}, u32[]{:S(2)}, u32[]{:S(2)}) collective-permute-start(bf16[4,1,96,576]{3,2,1,0:T(8,128)(2,1)} %pad_maximum_fusion.2.rest_0_), channel_id=1, source_target_pairs={{32,0},{9,1},{40,8},{17,9},{48,16},{25,17},{56,24},{1,25},{64,32},... | collective-permute-start | bytes 1327112 | tf_op jit(solution)/shard_map/ppermute | solution.py:504
  40.7 31.6 %collective-permute-start.15 = (bf16[4,1,96,576]{3,2,1,0:T(8,128)(2,1)}, bf16[4,1,96,576]{3,2,1,0:T(8,128)(2,1)}, u32[]{:S(2)}, u32[]{:S(2)}) collective-permute-start(bf16[4,1,96,576]{3,2,1,0:T(8,128)(2,1)} %pad_maximum_fusion.2.rest_0_), channel_id=1, source_target_pairs={{64,0},{17,1},{72,8},{25,9},{80,16},{1,17},{88,24},{9,25},{96,32},... | collective-permute-start | bytes 1327112 | tf_op jit(solution)/shard_map/ppermute | solution.py:504
  47.1 5.5 %collective-permute-start.7 = (bf16[4,16,576]{2,1,0:T(8,128)(2,1)S(1)}, bf16[4,16,576]{2,1,0:T(8,128)(2,1)S(1)}, u32[]{:S(2)}, u32[]{:S(2)}) collective-permute-start(bf16[4,16,576]{2,1,0:T(8,128)(2,1)S(1)} %bitcast.97), channel_id=1, source_target_pairs={{8,0},{33,1},{16,8},{41,9},{24,16},{49,17},{0,24},{57,25},{40,32},... | collective-permute-start | bytes 221192 | tf_op jit(solution)/shard_map/ppermute | solution.py:504
  49.8 6.2 %collective-permute-start.8 = (bf16[4,16,576]{2,1,0:T(8,128)(2,1)S(1)}, bf16[4,16,576]{2,1,0:T(8,128)(2,1)S(1)}, u32[]{:S(2)}, u32[]{:S(2)}) collective-permute-start(bf16[4,16,576]{2,1,0:T(8,128)(2,1)S(1)} %bitcast.98), channel_id=1, source_target_pairs={{16,0},{65,1},{24,8},{73,9},{0,16},{81,17},{8,24},{89,25},{48,32},... | collective-permute-start | bytes 221192 | tf_op jit(solution)/shard_map/ppermute | solution.py:504
  50.2 6.6 %collective-permute-start.9 = (bf16[4,16,576]{2,1,0:T(8,128)(2,1)S(1)}, bf16[4,16,576]{2,1,0:T(8,128)(2,1)S(1)}, u32[]{:S(2)}, u32[]{:S(2)}) collective-permute-start(bf16[4,16,576]{2,1,0:T(8,128)(2,1)S(1)} %bitcast.99), channel_id=1, source_target_pairs={{24,0},{97,1},{0,8},{105,9},{8,16},{113,17},{16,24},{121,25},{56,3... | collective-permute-start | bytes 221192 | tf_op jit(solution)/shard_map/ppermute | solution.py:504
  52.6 19.8 %collective-permute-start.16 = (bf16[4,1,96,576]{3,2,1,0:T(8,128)(2,1)}, bf16[4,1,96,576]{3,2,1,0:T(8,128)(2,1)}, u32[]{:S(2)}, u32[]{:S(2)}) collective-permute-start(bf16[4,1,96,576]{3,2,1,0:T(8,128)(2,1)} %pad_maximum_fusion.2.rest_0_), channel_id=1, source_target_pairs={{96,0},{25,1},{104,8},{1,9},{112,16},{9,17},{120,24},{17,25},{0,32... | collective-permute-start | bytes 1327112 | tf_op jit(solution)/shard_map/ppermute | solution.py:504
  56.9 9.5 %collective-permute-start.10 = (bf16[4,4,16,576]{3,2,1,0:T(8,128)(2,1)S(1)}, bf16[4,4,16,576]{3,2,1,0:T(8,128)(2,1)S(1)}, u32[]{:S(2)}, u32[]{:S(2)}) collective-permute-start(bf16[4,4,16,576]{3,2,1,0:T(8,128)(2,1)S(1)} %pad_maximum_fusion.3), channel_id=1, source_target_pairs={{32,0},{9,1},{40,8},{17,9},{48,16},{25,17},{56,24},{1,25},{64,32},... | collective-permute-start | bytes 884744 | tf_op jit(solution)/shard_map/ppermute | solution.py:504
  58.7 14.2 %collective-permute-start.11 = (bf16[4,4,16,576]{3,2,1,0:T(8,128)(2,1)S(1)}, bf16[4,4,16,576]{3,2,1,0:T(8,128)(2,1)S(1)}, u32[]{:S(2)}, u32[]{:S(2)}) collective-permute-start(bf16[4,4,16,576]{3,2,1,0:T(8,128)(2,1)S(1)} %pad_maximum_fusion.3), channel_id=1, source_target_pairs={{64,0},{17,1},{72,8},{25,9},{80,16},{1,17},{88,24},{9,25},{96,32},... | collective-permute-start | bytes 884744 | tf_op jit(solution)/shard_map/ppermute | solution.py:504
  66.4 11.2 %collective-permute-start.12 = (bf16[4,4,16,576]{3,2,1,0:T(8,128)(2,1)S(1)}, bf16[4,4,16,576]{3,2,1,0:T(8,128)(2,1)S(1)}, u32[]{:S(2)}, u32[]{:S(2)}) collective-permute-start(bf16[4,4,16,576]{3,2,1,0:T(8,128)(2,1)S(1)} %pad_maximum_fusion.3), channel_id=1, source_target_pairs={{96,0},{25,1},{104,8},{1,9},{112,16},{9,17},{120,24},{17,25},{0,32... | collective-permute-start | bytes 884744 | tf_op jit(solution)/shard_map/ppermute | solution.py:504
  70.6 31.5 %collective-permute-start.17 = (bf16[4,1,96,576]{3,2,1,0:T(8,128)(2,1)}, bf16[4,1,96,576]{3,2,1,0:T(8,128)(2,1)}, u32[]{:S(2)}, u32[]{:S(2)}) collective-permute-start(bf16[4,1,96,576]{3,2,1,0:T(8,128)(2,1)} %pad_maximum_fusion.2.rest_0_), channel_id=1, source_target_pairs={{0,1},{1,0},{2,3},{3,2},{4,5},{5,4},{6,7},{7,6},{8,9},{9,8},{10,11... | collective-permute-start | bytes 1327112 | tf_op jit(solution)/shard_map/ppermute | solution.py:487
  72.4 29.7 %collective-permute-start.18 = (bf16[4,1,96,576]{3,2,1,0:T(8,128)(2,1)}, bf16[4,1,96,576]{3,2,1,0:T(8,128)(2,1)}, u32[]{:S(2)}, u32[]{:S(2)}) collective-permute-start(bf16[4,1,96,576]{3,2,1,0:T(8,128)(2,1)} %collective-permute-done.14.rest_1_), channel_id=1, source_target_pairs={{0,1},{1,0},{2,3},{3,2},{4,5},{5,4},{6,7},{7,6},{8,9},{9,8},{10,11... | collective-permute-start | bytes 1327112 | tf_op jit(solution)/shard_map/ppermute | solution.py:487
  72.5 29.6 %collective-permute-start.19 = (bf16[4,1,96,576]{3,2,1,0:T(8,128)(2,1)}, bf16[4,1,96,576]{3,2,1,0:T(8,128)(2,1)}, u32[]{:S(2)}, u32[]{:S(2)}) collective-permute-start(bf16[4,1,96,576]{3,2,1,0:T(8,128)(2,1)} %collective-permute-done.15.rest_2_), channel_id=1, source_target_pairs={{0,1},{1,0},{2,3},{3,2},{4,5},{5,4},{6,7},{7,6},{8,9},{9,8},{10,11... | collective-permute-start | bytes 1327112 | tf_op jit(solution)/shard_map/ppermute | solution.py:487
  72.9 29.2 %collective-permute-start.20 = (bf16[4,1,96,576]{3,2,1,0:T(8,128)(2,1)}, bf16[4,1,96,576]{3,2,1,0:T(8,128)(2,1)}, u32[]{:S(2)}, u32[]{:S(2)}) collective-permute-start(bf16[4,1,96,576]{3,2,1,0:T(8,128)(2,1)} %collective-permute-done.16.rest_3_), channel_id=1, source_target_pairs={{0,1},{1,0},{2,3},{3,2},{4,5},{5,4},{6,7},{7,6},{8,9},{9,8},{10,11... | collective-permute-start | bytes 1327112 | tf_op jit(solution)/shard_map/ppermute | solution.py:487
  78.4 23.7 %collective-permute-start.13 = (bf16[16,4,16,576]{3,2,1,0:T(8,128)(2,1)}, bf16[16,4,16,576]{3,2,1,0:T(8,128)(2,1)}, u32[]{:S(2)}, u32[]{:S(2)}) collective-permute-start(bf16[16,4,16,576]{3,2,1,0:T(8,128)(2,1)} %constant_dynamic-update-slice_fusion.near_ref), channel_id=1, source_target_pairs={{0,1},{1,0},{2,3},{3,2},{4,5},{5,4},{6,7},{7,6},{8,9},{9,8},{10,11... | collective-permute-start | bytes 3538952 | tf_op jit(solution)/shard_map/ppermute | solution.py:487
  79.7 2.6 %copy-start.1 = (bf16[16,64,640]{2,1,0:T(8,128)(2,1)}, bf16[16,64,640]{2,1,0:T(8,128)(2,1)S(1)}, u32[]{:S(2)}) copy-start(bf16[16,64,640]{2,1,0:T(8,128)(2,1)S(1)} %all-to-all-done) | copy-start | bytes 3932164
  80.0 2.3 %copy-start.8 = (s32[32]{0:T(128)}, s32[32]{0:T(128)S(1)}, u32[]{:S(2)}) copy-start(s32[32]{0:T(128)S(1)} %fusion.46.length) | copy-start | bytes 388
  92.2 2.8 %copy-start.6 = (bf16[32,32,128]{2,1,0:T(8,128)(2,1)S(1)}, bf16[32,32,128]{2,1,0:T(8,128)(2,1)}, u32[]{:S(2)}) copy-start(bf16[32,32,128]{2,1,0:T(8,128)(2,1)} %get-tuple-element.14) | copy-start | bytes 786436
  95.9 27.0 %all-to-all-start.1 = ((bf16[16,64,256]{2,1,0:T(8,128)(2,1)}), bf16[16,64,256]{2,1,0:T(8,128)(2,1)S(1)}, u32[]{:S(2)}, u32[]{:S(2)}) async-start(bf16[16,64,256]{2,1,0:T(8,128)(2,1)} %pad_maximum_fusion), calls=%async_computation.1 | async-start | bytes 1048576 | tf_op jit(solution)/shard_map/all_to_all | solution.py:640
  122.0 4.7 %copy-start.4 = (bf16[1,512,512]{2,1,0:T(8,128)(2,1)S(1)}, bf16[1,512,512]{2,1,0:T(8,128)(2,1)}, u32[]{:S(2)}) copy-start(bf16[1,512,512]{2,1,0:T(8,128)(2,1)} %get-tuple-element.13) | copy-start | bytes 1572868
  122.9 0.8 copy-start.3
Sparse Core Ops, SparseCore 0:
  11.1 103.9 all-gather.1

commit v3 on v2

--- a/solution.py
+++ b/solution.py
@@ -86,23 +86,28 @@
         store(i, summed / total, peak * factor + jnp.log2(total))
 
 
-def first_body(config, chunk, head_local, info, q_ref, dq_ref, near_ref, far_ref, fresh_ref, *rest):
+def gather_group(piece_refs, group):
+    for c in range(2):
+        for s in range(4):
+            group[c, s] = piece_refs[c * 4 + s][...].reshape(group.shape[2:])
+
+
+def first_body(config, chunk, head_local, info, q_ref, dq_ref, fresh_ref, *rest):
     pieces = rest[:8]
-    out_ref, decode_ref, lse_ref, hold, past, arrive = rest[8:]
+    group_refs = rest[8:16]
+    out_ref, decode_ref, lse_ref, hold, past, group, arrive = rest[16:]
     step = pl.program_id(0)
-    prompts = pl.num_programs(0) - 1
     tile = hold.shape[1]
-    _, holders, piece_rows, width = past.shape
-    lines, half_tokens, _ = near_ref.shape
-    held = chunk // piece_rows
+    holders, piece_blocks, half_tokens, width = past.shape
+    lines = 16
+    held = chunk // (piece_blocks * half_tokens)
     past_count = holders // held
-    prompt = jnp.maximum(step - 1, 0)
-    slot = prompt & 1
-    past_len = info[prompt]
+    past_len = info[0]
     z_place, x_place, core = info[5], info[6], info[7]
 
-    def copies(p):
-        made = []
+    @pl.when(step == 0)
+    def _():
+        copies = []
         for c in range(2):
             side = core if c == 0 else 1 - core
             for s in range(4):
@@ -110,32 +115,21 @@
                     dz = s + (j - s) * side
                     dx = j + (s - j) * side
                     holder = ((z_place + dz) & 3) * 4 + ((x_place + dx) & 3)
-                    made.append(
+                    copies.append(
                         pltpu.make_async_copy(
-                            pieces[c * 4 + s].at[j, p],
-                            past.at[p & 1, holder * 2 + side],
-                            arrive.at[p & 1, c * 16 + s * 4 + j],
+                            pieces[c * 4 + s].at[j, pl.ds(0, piece_blocks)],
+                            past.at[holder * 2 + side],
+                            arrive.at[c * 16 + s * 4 + j],
                         )
                     )
-        return made
-
-    @pl.when(step == 0)
-    def _():
-        for copy in copies(0):
+        for copy in copies:
             copy.start()
-
-    @pl.when((step > 0) & (step < prompts))
-    def _():
-        for copy in copies(step):
-            copy.start()
-
-    @pl.when(step != 1)
-    def _():
-        for copy in copies(prompt):
+        gather_group(group_refs, group)
+        for copy in copies:
             copy.wait()
 
     def past_keys(j):
-        return lambda: past[slot, j * held : (j + 1) * held].reshape(chunk, width)
+        return lambda: past[j * held : (j + 1) * held].reshape(chunk, width)
 
     def past_mask(j):
         def allowed(row):
@@ -164,8 +158,8 @@
 
     keys = [past_keys(j) for j in range(past_count)]
     keys += [
-        lambda: near_ref[...].reshape(lines * half_tokens, width),
-        lambda: far_ref[...].reshape(lines * half_tokens, width),
+        lambda: group[0].reshape(lines * half_tokens, width),
+        lambda: group[1].reshape(lines * half_tokens, width),
     ]
     masks = [past_mask(j) for j in range(past_count)]
 
@@ -201,67 +195,67 @@
         )
 
 
-def attend_first(info, query, decode_query, pieces, near, far, fresh, lat, factor, head_local):
+def group_specs(pieces, block):
+    count, _, half_tokens, width = pieces[0].shape
+    return [pl.BlockSpec((count, None, half_tokens, width), block) for _ in pieces]
+
+
+def attend_first(info, query, decode_query, pieces, piece_blocks, fresh, lat, factor, head_local):
     _, rows, width = query.shape
-    prompts = pieces[0].shape[1]
     decode_rows = decode_query.shape[0]
-    piece_rows = pieces[0].shape[2]
+    half_tokens = pieces[0].shape[2]
     holders = 4 * len(pieces)
-    lines, _, half_tokens, _ = near.shape
-    keys = holders * piece_rows + 2 * lines * half_tokens + fresh.shape[0]
+    keys = holders * (piece_blocks + 1) * half_tokens + fresh.shape[0]
     tile = 256
     chunk = 768
-
-    def prompt(i):
-        return jnp.maximum(i - 1, 0)
-
-    group_spec = pl.BlockSpec(
-        (lines, None, half_tokens, width), lambda i, _: (0, prompt(i), 0, 0)
-    )
     return pl.pallas_call(
         functools.partial(first_body, (lat, factor), chunk, head_local),
         grid_spec=pltpu.PrefetchScalarGridSpec(
             num_scalar_prefetch=1,
-            grid=(prompts + 1,),
+            grid=(2,),
             in_specs=[
-                pl.BlockSpec((None, rows, width), lambda i, _: (prompt(i), 0, 0)),
+                pl.BlockSpec((None, rows, width), lambda i, _: (0, 0, 0)),
                 pl.BlockSpec((decode_rows, width), lambda i, _: (0, 0)),
-                group_spec,
-                group_spec,
                 pl.BlockSpec(fresh.shape, lambda i, _: (0, 0)),
             ]
-            + [pl.BlockSpec(memory_space=pl.ANY)] * len(pieces),
+            + [pl.BlockSpec(memory_space=pl.ANY)] * len(pieces)
+            + group_specs(pieces, lambda i, _: (0, piece_blocks, 0, 0)),
             out_specs=[
-                pl.BlockSpec((None, rows, lat), lambda i, _: (prompt(i), 0, 0)),
+                pl.BlockSpec((None, rows, lat), lambda i, _: (0, 0, 0)),
                 pl.BlockSpec((decode_rows, lat), lambda i, _: (0, 0)),
                 pl.BlockSpec((decode_rows, 128), lambda i, _: (0, 0)),
             ],
             scratch_shapes=[
                 pltpu.VMEM((2, tile, keys), jnp.float32),
-                pltpu.VMEM((2, holders, piece_rows, width), jnp.bfloat16),
-                pltpu.SemaphoreType.DMA((2, holders)),
+                pltpu.VMEM((holders, piece_blocks, half_tokens, width), jnp.bfloat16),
+                pltpu.VMEM((2, 4, 4 * half_tokens, width), jnp.bfloat16),
+                pltpu.SemaphoreType.DMA((holders,)),
             ],
         ),
         out_shape=[
-            jax.ShapeDtypeStruct((prompts, rows, lat), jnp.bfloat16),
+            jax.ShapeDtypeStruct((1, rows, lat), jnp.bfloat16),
             jax.ShapeDtypeStruct((decode_rows, lat), jnp.bfloat16),
             jax.ShapeDtypeStruct((decode_rows, 128), jnp.float32),
         ],
         compiler_params=pltpu.CompilerParams(vmem_limit_bytes=VMEM_BYTES),
         cost_estimate=pl.CostEstimate(
-            flops=2 * (prompts * rows + decode_rows) * keys * (768 + lat),
-            bytes_accessed=2 * prompts * (keys + 2 * rows) * width,
-            transcendentals=(prompts * rows + decode_rows) * keys,
+            flops=2 * (rows + decode_rows) * keys * (768 + lat),
+            bytes_accessed=2 * (keys + 2 * rows + 2 * decode_rows) * width,
+            transcendentals=(rows + decode_rows) * keys,
         ),
         name="attend_first",
-    )(info, query, decode_query, near, far, fresh, *pieces)
-
-
-def later_body(config, chunk, head_local, first, info, q_ref, past_ref, near_ref, far_ref, out_ref, hold):
+    )(info, query, decode_query, fresh, *pieces, *pieces)
+
+
+def later_body(config, chunk, head_local, first, info, q_ref, past_ref, *rest):
+    group_refs = rest[:8]
+    out_ref, hold, group = rest[8:]
     step = pl.program_id(0)
     tile = hold.shape[1]
     seq_count, _, piece_rows, width = past_ref.shape
-    lines, half_tokens, _ = near_ref.shape
+    lines = 16
+    half_tokens = group_refs[0].shape[1]
+    gather_group(group_refs, group)
     held = chunk // (2 * piece_rows)
     past_count = seq_count // held
     past_len = info[step + first]
@@ -293,8 +287,8 @@
 
     keys = [past_keys(j) for j in range(past_count)]
     keys += [
-        lambda: near_ref[...].reshape(lines * half_tokens, width),
-        lambda: far_ref[...].reshape(lines * half_tokens, width),
+        lambda: group[0].reshape(lines * half_tokens, width),
+        lambda: group[1].reshape(lines * half_tokens, width),
     ]
     masks = [past_mask(j) for j in range(past_count)]
 
@@ -323,15 +317,14 @@
         run(past_count)
 
 
-def attend_later(info, query, past, near, far, first, lat, factor, head_local):
+def attend_later(info, query, past, pieces, piece_blocks, first, lat, factor, head_local):
     prompts, rows, width = query.shape
     count = prompts - first
     seq_count, _, halves, piece_rows, _ = past.shape
-    lines, _, half_tokens, _ = near.shape
-    keys = seq_count * halves * piece_rows + 2 * lines * half_tokens
+    half_tokens = pieces[0].shape[2]
+    keys = seq_count * halves * (piece_rows + half_tokens)
     tile = 256
     chunk = 768
-    group_spec = pl.BlockSpec((lines, None, half_tokens, width), lambda i, _: (0, i + first, 0, 0))
     return pl.pallas_call(
         functools.partial(later_body, (lat, factor), chunk, head_local, first),
         grid_spec=pltpu.PrefetchScalarGridSpec(
@@ -343,11 +336,13 @@
                     (seq_count, None, halves, piece_rows, width),
                     lambda i, _: (0, i + first, 0, 0, 0),
                 ),
-                group_spec,
-                group_spec,
+            ]
+            + group_specs(pieces, lambda i, _: (0, piece_blocks + i + first, 0, 0)),
+            out_specs=pl.BlockSpec((None, rows, lat), lambda i, _: (i, 0, 0)),
+            scratch_shapes=[
+                pltpu.VMEM((2, tile, keys), jnp.float32),
+                pltpu.VMEM((2, 4, 4 * half_tokens, width), jnp.bfloat16),
             ],
-            out_specs=pl.BlockSpec((None, rows, lat), lambda i, _: (i, 0, 0)),
-            scratch_shapes=[pltpu.VMEM((2, tile, keys), jnp.float32)],
         ),
         out_shape=jax.ShapeDtypeStruct((count, rows, lat), jnp.bfloat16),
         compiler_params=pltpu.CompilerParams(vmem_limit_bytes=VMEM_BYTES),
@@ -357,7 +352,7 @@
             transcendentals=count * rows * keys,
         ),
         name="attend_later",
-    )(info, query, past, near, far)
+    )(info, query, past, *pieces)
 
 
 def dispatch_body(source, length, q_ref, out_ref):
@@ -539,12 +534,6 @@
         past_part.reshape(half, row_width), ("seq", "tp", "grp"), axis=0, tiled=False
     ).reshape(seq_count, prompt_count, 2, half, row_width)
 
-    past_half = lax.dynamic_slice(past_cache, (0, core * half, 0), (1, half, row_width))
-    past_line = [past_half] + [fetch_ring(past_half, shift, 0) for shift in range(1, 4)]
-    past_line = jnp.stack(past_line)
-    past_lines = [past_line] + [fetch_ring(past_line, shift, 1) for shift in range(1, 4)]
-    past_lines = past_lines + [swap_core(piece) for piece in past_lines]
-
     half_tokens = group_local // 2
     pairs = 2 * request_local
     partial_group = jnp.einsum(
@@ -566,7 +555,6 @@
     pair_sum = both(core).astype(jnp.float32) + swap_core(both(1 - core)).astype(jnp.float32)
     pair_sum = pair_sum.astype(jnp.bfloat16)
 
-    pair_sum, _ = lax.optimization_barrier((pair_sum, past_line))
     latent = pair_sum.astype(jnp.float32)
     for shift in range(1, 4):
         latent = latent + fetch_tp(pair_sum, shift).astype(jnp.float32)
@@ -583,12 +571,12 @@
     rows_own = make_rows(latent, kv_gain, positions)
     fresh = jnp.pad(rows_own[group_part:], ((0, 128 - pairs), (0, 0)))
 
-    group_own = rows_own[:group_part].reshape(prompt_count, half_tokens, row_width)
-    group_line = [group_own] + [fetch_ring(group_own, shift, 0) for shift in range(1, 4)]
-    group_line = jnp.stack(group_line)
-    group_lines = [group_line] + [fetch_ring(group_line, shift, 1) for shift in range(1, 4)]
-    group_near = jnp.concatenate(group_lines)
-    group_far = swap_core(group_near)
+    past_zero = lax.dynamic_slice(past_cache, (0, core * half, 0), (1, half, row_width))
+    piece_blocks = half // half_tokens
+    line = jnp.concatenate([past_zero.reshape(half, row_width), rows_own[:group_part]])
+    line = line.reshape(-1, half_tokens, row_width)
+    line = jnp.stack([line] + [fetch_ring(line, shift, 0) for shift in range(1, 4)])
+    lines = [line] + [fetch_ring(line, shift, 1) for shift in range(1, 4)]
 
     targets = owner[:, 0]
     request_order = jnp.arange(request_local, dtype=jnp.int32)
@@ -628,6 +616,8 @@
     cache_latent, cache_lse = attend_cache(
         order, slot_length, used.reshape(1), arrived, jnp.swapaxes(decode_pool, 1, 2), lat, factor
     )
+    lines[1:], cache_latent = lax.optimization_barrier((lines[1:], cache_latent))
+    pieces = lines + [swap_core(piece) for piece in lines]
     cache_value = jnp.einsum(
         "nshc,hcv->nshv",
         cache_latent.reshape(slot_count, 2, head_local, lat),
@@ -655,9 +645,8 @@
         info,
         queries,
         decode_rows.reshape(request_local * query_pairs, row_width),
-        past_lines,
-        group_near,
-        group_far,
+        pieces,
+        piece_blocks,
         fresh,
         lat,
         factor,
@@ -678,7 +667,7 @@
 
     queries, _ = lax.optimization_barrier((queries, decode_out))
     later_latent = attend_later(
-        info, queries, past_all, group_near, group_far, 1, lat, factor, head_local
+        info, queries, past_all, pieces, piece_blocks, 1, lat, factor, head_local
     )
     prefill_out = jnp.concatenate(
         [

time: 161 us -> 155 us (0.963)
  starting transfers between devices: 40.4 us -> 32 us
  waiting for transfers between devices: 17.9 us -> 24.2 us
  local copies, waits for them, and re-layouts: 12.6 us -> 8.32 us
  Pallas kernels: 55.1 us -> 52.6 us
    ppermute x12 -> x6, starting transfers between devices: 18.8 us -> 7.81 us  [fetch_ring(): return lax.ppermute(value, ('seq', 'grp'), moves)]
    ppermute x12 -> x6, waiting for transfers between devices: 12.7 us -> 16.6 us  [fetch_ring(): return lax.ppermute(value, ('seq', 'grp'), moves)]
    unnamed x35 -> x29, local copies, waits for them, and re-layouts: 6.08 us -> 3.07 us
    all_gather x1, waiting for transfers between devices: 0.02 us -> 2.43 us  [on_device(): lax.all_gather(past_part.reshape(half, row_width), ('seq', 'tp', 'grp'),...]
    ppermute x6 -> x5, starting transfers between devices: 4.59 us -> 6 us  [swap_core(): return lax.ppermute(value, 'grp', [(0, 1), (1, 0)])]
  transfers between devices with their start and end apart: 24 -> 17, of which waited for: 8 -> 6; matrix products, arithmetic and copies ran while one was open for 15% -> 13% of each run, Pallas kernels for 21% -> 21%
where the time goes in v3:
time: 155 us; the launch traced here: 153 us
  Pallas kernels  52.6 us (34%)
  starting transfers between devices  32 us (21%)
  waiting for transfers between devices  24.2 us (16%)
  between operations  15.1 us (10%)
  matrix products  10.3 us (7%)
  other arithmetic  10.2 us (7%)
  local copies, waits for them, and re-layouts  8.32 us (5%)
    pallas_call x1, Pallas kernels, attend_later(): pl.pallas_call(functools.partial(later_body, (lat, factor), chunk, head_l...  19.9 us
    pallas_call x1, Pallas kernels, attend_first(): pl.pallas_call(functools.partial(first_body, (lat, factor), chunk, head_l...  18.4 us
    ppermute x6, waiting for transfers between devices, fetch_ring(): return lax.ppermute(value, ('seq', 'grp'), moves)  16.6 us
    pallas_call x1, Pallas kernels, attend_cache(): pl.pallas_call(functools.partial(cache_body, lat, factor, batch), grid_sp...  8.99 us
    all_to_all x1, starting transfers between devices, on_device(): lax.all_to_all(send_query.reshape(seq_count, pair_limit * query_pairs, ro...  7.81 us
    ppermute x6, starting transfers between devices, fetch_ring(): return lax.ppermute(value, ('seq', 'grp'), moves)  7.81 us
    ppermute x5, starting transfers between devices, swap_core(): return lax.ppermute(value, 'grp', [(0, 1), (1, 0)])  6 us
    all_to_all x1, starting transfers between devices, on_device(): lax.all_to_all(back.reshape(seq_count, pair_limit * query_pairs, 2 * valu...  5.29 us
  transfers between devices with their start and end apart: 17, of which 6 were waited for; matrix products, arithmetic and copies ran while one was open for 13% of the time, Pallas kernels for 21%

profile of v3, /device:TPU:1, one launch (start us, length us, event | category | flops | bytes accessed | tf_op | source)
XLA Modules:
  0.0 152.8 jit_solution(17395153318562921381)
XLA Ops:
  7.3 1.8 %constant_dynamic-slice_fusion = (bf16[1,96,576]{2,1,0:T(8,128)(2,1)}, bf16[96,576]{1,0:T(8,128)(2,1)}) fusion(bf16[4,192,576]{2,1,0:T(8,128)(2,1)} %param.14, s32[]{:T(128)S(6)} %select_n.31, s32[]{:T(128)S(6)} %select_n.25), kind=kLoop, calls=%fused_computation.64 | loop fusion | bytes 442376 | tf_op jit(solution)/shard_map/dynamic_slice | solution.py:532
  9.1 0.8 reshape.186
  10.0 1.8 %convolution_convert_fusion = bf16[4,32,576]{2,1,0:T(8,128)(2,1)S(1)} fusion(bf16[4,32,896]{2,1,0:T(8,128)(2,1)} %param.12, bf16[896,576]{0,1:T(8,128)(2,1)} %param.21), kind=kOutput, calls=%fused_computation.12 | convolution fusion | flops 132194304 | bytes 1409024 | tf_op jit(solution)/shard_map/ptd,dc->ptc/dot_general | solution.py:539
  11.8 0.4 convolution_convert_fusion.2
  12.2 0.7 pad_maximum_fusion.4
  12.9 1.4 collective-permute-start
  14.3 0.2 convert_reduce_fusion
  14.5 0.6 copy-done.10
  15.1 0.6 select_reduce_fusion.1
  15.7 2.3 %dispatch_queries.1 = bf16[32,32,640]{2,1,0:T(8,128)(2,1)} custom-call(s32[32]{0:T(128)} %get-tuple-element.35.source, s32[32]{0:T(128)} %get-tuple-element.34.length, bf16[16,32,576]{2,1,0:T(8,128)(2,1)} %bitcast.96), custom_call_target="tpu_custom_call" | custom-call | tf_op jit(solution)/shard_map/dispatch_queries/pallas_call | solution.py:374
  18.0 7.8 %all-to-all-start = ((bf16[16,64,640]{2,1,0:T(8,128)(2,1)}), bf16[16,64,640]{2,1,0:T(8,128)(2,1)S(1)}, u32[]{:S(2)}, u32[]{:S(2)}) async-start(bf16[16,64,640]{2,1,0:T(8,128)(2,1)} %bitcast.87), calls=%async_computation | async-start | bytes 2621440 | tf_op jit(solution)/shard_map/all_to_all | solution.py:597
  25.9 0.1 iota_add_fusion
  26.0 0.1 add.145
  26.1 0.1 add_add_fusion
  26.2 0.1 add.153
  26.3 0.9 add_convert_fusion
  27.2 1.4 collective-permute-start.3
  28.6 2.6 %collective-permute-start.2 = (bf16[96,576]{1,0:T(8,128)(2,1)S(1)}, bf16[96,576]{1,0:T(8,128)(2,1)S(1)}, u32[]{:S(2)}, u32[]{:S(2)}) collective-permute-start(bf16[96,576]{1,0:T(8,128)(2,1)S(1)} %add_convert_fusion), channel_id=1, source_target_pairs={{4,0},{6,2},{0,4},{2,6},{5,1},{7,3},{1,5},{3,7},{12,8},{14,10},{8,... | collective-permute-start | bytes 331784 | tf_op jit(solution)/shard_map/ppermute | solution.py:486
  31.2 1.1 collective-permute-start.1
  32.3 0.1 add_convert_fusion.1
  32.4 1.1 collective-permute-done.3
  33.4 4.1 %collective-permute-done.2 = bf16[96,576]{1,0:T(8,128)(2,1)S(1)} collective-permute-done((bf16[96,576]{1,0:T(8,128)(2,1)S(1)}, bf16[96,576]{1,0:T(8,128)(2,1)S(1)}, u32[]{:S(2)}, u32[]{:S(2)}) %collective-permute-start.2) | collective-permute-done | bytes 110624 | tf_op jit(solution)/shard_map/ppermute | solution.py:486
  37.6 0.1 multiply_reduce_fusion
  37.7 0.3 fusion.41
  38.0 0.1 multiply_convert_fusion
  38.1 0.5 copy-done.6
  38.6 0.1 pad_maximum_fusion.6
  38.7 0.9 pad_maximum_fusion.3
  39.6 1.3 collective-permute-start.6
  40.9 2.3 %collective-permute-start.5 = (bf16[10,16,576]{2,1,0:T(8,128)(2,1)S(1)}, bf16[10,16,576]{2,1,0:T(8,128)(2,1)S(1)}, u32[]{:S(2)}, u32[]{:S(2)}) collective-permute-start(bf16[10,16,576]{2,1,0:T(8,128)(2,1)S(1)} %bitcast.93), channel_id=1, source_target_pairs={{16,0},{65,1},{24,8},{73,9},{0,16},{81,17},{8,24},{89,25},{48,32},... | collective-permute-start | bytes 552968 | tf_op jit(solution)/shard_map/ppermute | solution.py:499
  43.2 1.2 collective-permute-start.4
  44.4 1.5 collective-permute-done.6
  45.9 4.1 %collective-permute-done.5 = bf16[10,16,576]{2,1,0:T(8,128)(2,1)S(1)} collective-permute-done((bf16[10,16,576]{2,1,0:T(8,128)(2,1)S(1)}, bf16[10,16,576]{2,1,0:T(8,128)(2,1)S(1)}, u32[]{:S(2)}, u32[]{:S(2)}) %collective-permute-start.5) | collective-permute-done | bytes 184352 | tf_op jit(solution)/shard_map/ppermute | solution.py:499
  50.0 1.1 pad_maximum_fusion.rest_0_.rest_8_
  51.1 2.9 %collective-permute-start.10 = (bf16[4,10,16,576]{3,2,1,0:T(8,128)(2,1)}, bf16[4,10,16,576]{3,2,1,0:T(8,128)(2,1)}, u32[]{:S(2)}, u32[]{:S(2)}) collective-permute-start(bf16[4,10,16,576]{3,2,1,0:T(8,128)(2,1)} %pad_maximum_fusion.rest_0_.rest_8_), channel_id=1, source_target_pairs={{0,1},{1,0},{2,3},{3,2},{4,5},{5,4},{6,7},{7,6},{8,9},{9,8},{10,11... | collective-permute-start | bytes 2211848 | tf_op jit(solution)/shard_map/ppermute | solution.py:482
  54.0 1.7 %collective-permute-start.8 = (bf16[4,10,16,576]{3,2,1,0:T(8,128)(2,1)}, bf16[4,10,16,576]{3,2,1,0:T(8,128)(2,1)}, u32[]{:S(2)}, u32[]{:S(2)}) collective-permute-start(bf16[4,10,16,576]{3,2,1,0:T(8,128)(2,1)} %pad_maximum_fusion.rest_0_.rest_8_), channel_id=1, source_target_pairs={{64,0},{17,1},{72,8},{25,9},{80,16},{1,17},{88,24},{9,25},{96,32},... | collective-permute-start | bytes 2211848 | tf_op jit(solution)/shard_map/ppermute | solution.py:499
  55.7 1.4 collective-permute-start.7
  57.0 0.1 slice_convert_fusion
  57.1 0.2 fusion.46.length
  57.3 0.7 convert_reduce_fusion.1
  58.7 0.7 compare_convert_fusion
  59.4 0.8 reduce-window.8
  60.1 0.1 add_reduce_fusion
  60.3 0.7 select_reduce_fusion.order
  61.0 9.0 %attend_cache.1 = (bf16[32,32,512]{2,1,0:T(8,128)(2,1)}, bf16[32,32,128]{2,1,0:T(8,128)(2,1)}) custom-call(s32[32]{0:T(128)} %select_reduce_fusion.order, s32[32]{0:T(128)} %copy-done.8, s32[1]{0:T(128)} %bitcast.21.used, bf16[32,32,640]{2,1,0:T(8,128)(2,1)} %bitcast.86, bf16[32,576,384]{2,1,0:T(8,128)(2,1)} %bitcast.81, bf16[32,576,384]{2,1,0:T(8,128)(2,1)} %bitcast.82, ...), custom_call_target="tpu_custom_call" | custom-call | flops 3422552064 | bytes 14155776 | tf_op jit(solution)/shard_map/attend_cache/pallas_call | solution.py:427
  70.0 11.0 %collective-permute-done.9.rest_3_.rest_11_ = bf16[4,10,16,576]{3,2,1,0:T(8,128)(2,1)} collective-permute-done((bf16[4,10,16,576]{3,2,1,0:T(8,128)(2,1)}, bf16[4,10,16,576]{3,2,1,0:T(8,128)(2,1)}, u32[]{:S(2)}, u32[]{:S(2)}) %collective-permute-start.9) | collective-permute-done | bytes 737312 | tf_op jit(solution)/shard_map/ppermute | solution.py:499
  81.0 1.1 collective-permute-start.11
  82.2 0.5 collective-permute-start.13
  82.7 1.3 stack.31.info
  84.0 0.7 fusion.35.fresh_ref
  84.7 2.5 %fusion.23 = bf16[32,2,16,128]{3,0,1,2:T(8,128)(2,1)S(1)} fusion(bf16[16,512,128]{2,1,0:T(8,128)(2,1)S(1)} %copy-done, bf16[32,2,16,512]{3,2,1,0:T(8,128)(2,1)} %bitcast.89), kind=kOutput, calls=%fused_computation.11 | convolution fusion | flops 134348800 | bytes 3407872 | tf_op jit(solution)/shard_map/nshc,hcv->nshv/dot_general | solution.py:621
  87.3 0.2 copy.58
  87.5 0.9 pad_maximum_fusion.1
  88.3 5.3 %all-to-all-start.1 = ((bf16[16,64,256]{2,1,0:T(8,128)(2,1)}), bf16[16,64,256]{2,1,0:T(8,128)(2,1)S(1)}, u32[]{:S(2)}, u32[]{:S(2)}) async-start(bf16[16,64,256]{2,1,0:T(8,128)(2,1)} %pad_maximum_fusion.1), calls=%async_computation.1 | async-start | bytes 1048576 | tf_op jit(solution)/shard_map/all_to_all | solution.py:630
  93.7 18.4 %attend_first.1 = (bf16[1,512,512]{2,1,0:T(8,128)(2,1)}, bf16[512,512]{1,0:T(8,128)(2,1)}, f32[512,128]{1,0:T(8,128)}) custom-call(s32[8]{0:T(128)} %stack.31.info, bf16[4,512,576]{2,1,0:T(8,128)(2,1)} %bitcast.113, bf16[512,576]{1,0:T(8,128)(2,1)} %bitcast.97, bf16[128,576]{1,0:T(8,128)(2,1)} %fusion.35.fresh_ref, ...), custom_call_target="tpu_custom_call" | custom-call | flops 9730785280 | bytes 6635520 | tf_op jit(solution)/shard_map/attend_first/pallas_call | solution.py:211
  112.1 1.7 %fusion.20 = f32[16,2,16,128]{3,0,1,2:T(8,128)S(1)} fusion(bf16[16,512,128]{2,1,0:T(8,128)(2,1)S(1)} %copy-done, bf16[16,2,16,512]{3,2,1,0:T(8,128)(2,1)} %bitcast.100), kind=kOutput, calls=%fused_computation.10 | convolution fusion | flops 67108864 | bytes 2883584 | tf_op jit(solution)/shard_map/rshc,hcv->rshv/dot_general | solution.py:655
  113.8 0.9 copy.60
  114.7 0.8 copy-done.3
  115.5 3.0 %merge_decode.1 = bf16[16,32,128]{2,1,0:T(8,128)(2,1)} custom-call(s32[16]{0:T(128)} %copy-done.10, bf16[32,32,256]{2,1,0:T(8,128)(2,1)} %bitcast.88, f32[16,32,128]{2,1,0:T(8,128)} %bitcast.90, f32[16,32,128]{2,1,0:T(8,128)} %bitcast.106), custom_call_target="tpu_custom_call" | custom-call | tf_op jit(solution)/shard_map/merge_decode/pallas_call | solution.py:471
  118.5 0.6 fusion.26
  119.1 2.4 %all-gather.2.cloned.1.call-done = bf16[128,96,576]{2,1,0:T(8,128)(2,1)} async-done(((bf16[1,96,576]{2,1,0:T(8,128)(2,1)}), bf16[128,96,576]{2,1,0:T(8,128)(2,1)}) %all-gather.2.cloned.1.call-update) | async-done | bytes 14155792 | tf_op jit(solution)/shard_map/all_gather | solution.py:533
  121.5 19.9 %attend_later.1 = bf16[3,512,512]{2,1,0:T(8,128)(2,1)} custom-call(s32[8]{0:T(128)} %stack.31.info, bf16[4,512,576]{2,1,0:T(8,128)(2,1)} %bitcast.114, bf16[16,4,2,96,576]{4,3,2,1,0:T(8,128)(2,1)} %bitcast.112, bf16[4,10,16,576]{3,2,1,0:T(8,128)(2,1)} %pad_maximum_fusion.rest_0_.rest_8_, bf16[4,10,16,576]{3,2,1,0:T(8,128)(2,1)} %collective-permute-done.7.rest_1_.rest_9_, ...), custom_call_target="tpu_custom_call" | custom-call | flops 14092861440 | bytes 15925248 | tf_op jit(solution)/shard_map/attend_later/pallas_call | solution.py:328
  141.4 3.3 %fusion.12 = bf16[3,32,16,128]{3,1,0,2:T(8,128)(2,1)S(1)} fusion(bf16[16,512,128]{2,1,0:T(8,128)(2,1)S(1)} %copy-done, bf16[3,32,16,512]{3,2,1,0:T(8,128)(2,1)} %bitcast.116), kind=kOutput, calls=%fused_computation.8 | convolution fusion | flops 201523200 | bytes 4063232 | tf_op jit(solution)/shard_map/pthc,hcv->pthv/dot_general | solution.py:674
  144.8 1.1 copy.63
  (50 shorter events, 0.3 us)
Async XLA Ops:
  7.2 77.6 %copy-start = (bf16[16,512,128]{2,1,0:T(8,128)(2,1)S(1)}, bf16[16,512,128]{2,1,0:T(8,128)(2,1)}, u32[]{:S(2)}) copy-start(bf16[16,512,128]{2,1,0:T(8,128)(2,1)} %param.23) | copy-start | bytes 6291460
  7.2 4.6 %copy-start.2 = (bf16[896,576]{0,1:T(8,128)(2,1)S(1)}, bf16[896,576]{0,1:T(8,128)(2,1)}, u32[]{:S(2)}) copy-start(bf16[896,576]{0,1:T(8,128)(2,1)} %param.21) | copy-start | bytes 3096580
  7.2 7.1 %copy-start.13 = (s32[16,1]{0,1:T(1,128)S(1)}, s32[16,1]{0,1:T(1,128)}, u32[]{:S(2)}) copy-start(s32[16,1]{0,1:T(1,128)} %param.19) | copy-start | bytes 196
  7.2 7.9 %copy-start.11 = (s32[16]{0:T(128)S(1)}, s32[16]{0:T(128)}, u32[]{:S(2)}) copy-start(s32[16]{0:T(128)} %param.20) | copy-start | bytes 196
  7.2 114.3 %all-gather.2.cloned.1.call-start = ((), (), s32[]{:S(2)}) async-start(), calls=%async_computation.2 | async-start | bytes 15851520 | tf_op jit(solution)/shard_map/all_gather | solution.py:533
  12.9 13.4 %collective-permute-start = (bf16[96,576]{1,0:T(8,128)(2,1)}, bf16[96,576]{1,0:T(8,128)(2,1)}, u32[]{:S(2)}, u32[]{:S(2)}) collective-permute-start(bf16[96,576]{1,0:T(8,128)(2,1)} %pad_maximum_fusion.4), channel_id=1, source_target_pairs={{0,1},{1,0},{2,3},{3,2},{4,5},{5,4},{6,7},{7,6},{8,9},{9,8},{10,11... | collective-permute-start | bytes 331784 | tf_op jit(solution)/shard_map/ppermute | solution.py:482
  14.5 0.6 copy-start.10
  15.7 10.2 %copy-start.12 = (s32[4]{0:T(128)S(1)}, s32[4]{0:T(128)}, u32[]{:S(2)}) copy-start(s32[4]{0:T(128)} %param.15) | copy-start | bytes 52
  18.0 19.9 %copy-start.9 = (f32[512]{0:T(512)S(1)}, f32[512]{0:T(512)}, u32[]{:S(2)}) copy-start(f32[512]{0:T(512)} %param.22) | copy-start | bytes 6148
  18.0 39.0 %all-to-all-start = ((bf16[16,64,640]{2,1,0:T(8,128)(2,1)}), bf16[16,64,640]{2,1,0:T(8,128)(2,1)S(1)}, u32[]{:S(2)}, u32[]{:S(2)}) async-start(bf16[16,64,640]{2,1,0:T(8,128)(2,1)} %bitcast.87), calls=%async_computation | async-start | bytes 2621440 | tf_op jit(solution)/shard_map/all_to_all | solution.py:597
  27.2 6.2 %collective-permute-start.3 = (bf16[96,576]{1,0:T(8,128)(2,1)S(1)}, bf16[96,576]{1,0:T(8,128)(2,1)S(1)}, u32[]{:S(2)}, u32[]{:S(2)}) collective-permute-start(bf16[96,576]{1,0:T(8,128)(2,1)S(1)} %add_convert_fusion), channel_id=1, source_target_pairs={{6,0},{0,2},{2,4},{4,6},{7,1},{1,3},{3,5},{5,7},{14,8},{8,10},{10,... | collective-permute-start | bytes 331784 | tf_op jit(solution)/shard_map/ppermute | solution.py:486
  28.6 8.9 %collective-permute-start.2 = (bf16[96,576]{1,0:T(8,128)(2,1)S(1)}, bf16[96,576]{1,0:T(8,128)(2,1)S(1)}, u32[]{:S(2)}, u32[]{:S(2)}) collective-permute-start(bf16[96,576]{1,0:T(8,128)(2,1)S(1)} %add_convert_fusion), channel_id=1, source_target_pairs={{4,0},{6,2},{0,4},{2,6},{5,1},{7,3},{1,5},{3,7},{12,8},{14,10},{8,... | collective-permute-start | bytes 331784 | tf_op jit(solution)/shard_map/ppermute | solution.py:486
  31.2 6.3 %collective-permute-start.1 = (bf16[96,576]{1,0:T(8,128)(2,1)S(1)}, bf16[96,576]{1,0:T(8,128)(2,1)S(1)}, u32[]{:S(2)}, u32[]{:S(2)}) collective-permute-start(bf16[96,576]{1,0:T(8,128)(2,1)S(1)} %add_convert_fusion), channel_id=1, source_target_pairs={{2,0},{4,2},{6,4},{0,6},{3,1},{5,3},{7,5},{1,7},{10,8},{12,10},{14... | collective-permute-start | bytes 331784 | tf_op jit(solution)/shard_map/ppermute | solution.py:486
  38.0 0.6 copy-start.6
  39.6 6.3 %collective-permute-start.6 = (bf16[10,16,576]{2,1,0:T(8,128)(2,1)S(1)}, bf16[10,16,576]{2,1,0:T(8,128)(2,1)S(1)}, u32[]{:S(2)}, u32[]{:S(2)}) collective-permute-start(bf16[10,16,576]{2,1,0:T(8,128)(2,1)S(1)} %bitcast.92), channel_id=1, source_target_pairs={{24,0},{97,1},{0,8},{105,9},{8,16},{113,17},{16,24},{121,25},{56,3... | collective-permute-start | bytes 552968 | tf_op jit(solution)/shard_map/ppermute | solution.py:499
  40.9 9.1 %collective-permute-start.5 = (bf16[10,16,576]{2,1,0:T(8,128)(2,1)S(1)}, bf16[10,16,576]{2,1,0:T(8,128)(2,1)S(1)}, u32[]{:S(2)}, u32[]{:S(2)}) collective-permute-start(bf16[10,16,576]{2,1,0:T(8,128)(2,1)S(1)} %bitcast.93), channel_id=1, source_target_pairs={{16,0},{65,1},{24,8},{73,9},{0,16},{81,17},{8,24},{89,25},{48,32},... | collective-permute-start | bytes 552968 | tf_op jit(solution)/shard_map/ppermute | solution.py:499
  43.2 6.8 %collective-permute-start.4 = (bf16[10,16,576]{2,1,0:T(8,128)(2,1)S(1)}, bf16[10,16,576]{2,1,0:T(8,128)(2,1)S(1)}, u32[]{:S(2)}, u32[]{:S(2)}) collective-permute-start(bf16[10,16,576]{2,1,0:T(8,128)(2,1)S(1)} %bitcast.94), channel_id=1, source_target_pairs={{8,0},{33,1},{16,8},{41,9},{24,16},{49,17},{0,24},{57,25},{40,32},... | collective-permute-start | bytes 552968 | tf_op jit(solution)/shard_map/ppermute | solution.py:499
  51.1 42.6 %collective-permute-start.10 = (bf16[4,10,16,576]{3,2,1,0:T(8,128)(2,1)}, bf16[4,10,16,576]{3,2,1,0:T(8,128)(2,1)}, u32[]{:S(2)}, u32[]{:S(2)}) collective-permute-start(bf16[4,10,16,576]{3,2,1,0:T(8,128)(2,1)} %pad_maximum_fusion.rest_0_.rest_8_), channel_id=1, source_target_pairs={{0,1},{1,0},{2,3},{3,2},{4,5},{5,4},{6,7},{7,6},{8,9},{9,8},{10,11... | collective-permute-start | bytes 2211848 | tf_op jit(solution)/shard_map/ppermute | solution.py:482
  54.0 27.0 %collective-permute-start.9 = (bf16[4,10,16,576]{3,2,1,0:T(8,128)(2,1)}, bf16[4,10,16,576]{3,2,1,0:T(8,128)(2,1)}, u32[]{:S(2)}, u32[]{:S(2)}) collective-permute-start(bf16[4,10,16,576]{3,2,1,0:T(8,128)(2,1)} %pad_maximum_fusion.rest_0_.rest_8_), channel_id=1, source_target_pairs={{96,0},{25,1},{104,8},{1,9},{112,16},{9,17},{120,24},{17,25},{0,32... | collective-permute-start | bytes 2211848 | tf_op jit(solution)/shard_map/ppermute | solution.py:499
  54.0 27.0 %collective-permute-start.8 = (bf16[4,10,16,576]{3,2,1,0:T(8,128)(2,1)}, bf16[4,10,16,576]{3,2,1,0:T(8,128)(2,1)}, u32[]{:S(2)}, u32[]{:S(2)}) collective-permute-start(bf16[4,10,16,576]{3,2,1,0:T(8,128)(2,1)} %pad_maximum_fusion.rest_0_.rest_8_), channel_id=1, source_target_pairs={{64,0},{17,1},{72,8},{25,9},{80,16},{1,17},{88,24},{9,25},{96,32},... | collective-permute-start | bytes 2211848 | tf_op jit(solution)/shard_map/ppermute | solution.py:499
  55.7 25.3 %collective-permute-start.7 = (bf16[4,10,16,576]{3,2,1,0:T(8,128)(2,1)}, bf16[4,10,16,576]{3,2,1,0:T(8,128)(2,1)}, u32[]{:S(2)}, u32[]{:S(2)}) collective-permute-start(bf16[4,10,16,576]{3,2,1,0:T(8,128)(2,1)} %pad_maximum_fusion.rest_0_.rest_8_), channel_id=1, source_target_pairs={{32,0},{9,1},{40,8},{17,9},{48,16},{25,17},{56,24},{1,25},{64,32},... | collective-permute-start | bytes 2211848 | tf_op jit(solution)/shard_map/ppermute | solution.py:499
  57.0 4.0 %copy-start.1 = (bf16[16,64,640]{2,1,0:T(8,128)(2,1)}, bf16[16,64,640]{2,1,0:T(8,128)(2,1)S(1)}, u32[]{:S(2)}) copy-start(bf16[16,64,640]{2,1,0:T(8,128)(2,1)S(1)} %all-to-all-done) | copy-start | bytes 3932164
  57.3 3.7 %copy-start.8 = (s32[32]{0:T(128)}, s32[32]{0:T(128)S(1)}, u32[]{:S(2)}) copy-start(s32[32]{0:T(128)S(1)} %fusion.46.length) | copy-start | bytes 388
  61.0 23.0 %copy-start.7 = (bf16[96,32]{1,0:T(8,128)(2,1)S(1)}, bf16[96,32]{1,0:T(8,128)(2,1)}, u32[]{:S(2)}) copy-start(bf16[96,32]{1,0:T(8,128)(2,1)} %copy-done.6) | copy-start | bytes 18436
  81.0 12.7 %collective-permute-start.11 = (bf16[4,10,16,576]{3,2,1,0:T(8,128)(2,1)}, bf16[4,10,16,576]{3,2,1,0:T(8,128)(2,1)}, u32[]{:S(2)}, u32[]{:S(2)}) collective-permute-start(bf16[4,10,16,576]{3,2,1,0:T(8,128)(2,1)} %collective-permute-done.7.rest_1_.rest_9_), channel_id=1, source_target_pairs={{0,1},{1,0},{2,3},{3,2},{4,5},{5,4},{6,7},{7,6},{8,9},{9,8},{10,11... | collective-permute-start | bytes 2211848 | tf_op jit(solution)/shard_map/ppermute | solution.py:482
  82.1 11.5 %collective-permute-start.12 = (bf16[4,10,16,576]{3,2,1,0:T(8,128)(2,1)}, bf16[4,10,16,576]{3,2,1,0:T(8,128)(2,1)}, u32[]{:S(2)}, u32[]{:S(2)}) collective-permute-start(bf16[4,10,16,576]{3,2,1,0:T(8,128)(2,1)} %collective-permute-done.8.rest_2_.rest_10_), channel_id=1, source_target_pairs={{0,1},{1,0},{2,3},{3,2},{4,5},{5,4},{6,7},{7,6},{8,9},{9,8},{10,11... | collective-permute-start | bytes 2211848 | tf_op jit(solution)/shard_map/ppermute | solution.py:482
  82.2 11.5 %collective-permute-start.13 = (bf16[4,10,16,576]{3,2,1,0:T(8,128)(2,1)}, bf16[4,10,16,576]{3,2,1,0:T(8,128)(2,1)}, u32[]{:S(2)}, u32[]{:S(2)}) collective-permute-start(bf16[4,10,16,576]{3,2,1,0:T(8,128)(2,1)} %collective-permute-done.9.rest_3_.rest_11_), channel_id=1, source_target_pairs={{0,1},{1,0},{2,3},{3,2},{4,5},{5,4},{6,7},{7,6},{8,9},{9,8},{10,11... | collective-permute-start | bytes 2211848 | tf_op jit(solution)/shard_map/ppermute | solution.py:482
  84.0 3.5 %copy-start.5 = (bf16[32,32,128]{2,1,0:T(8,128)(2,1)S(1)}, bf16[32,32,128]{2,1,0:T(8,128)(2,1)}, u32[]{:S(2)}) copy-start(bf16[32,32,128]{2,1,0:T(8,128)(2,1)} %get-tuple-element.20) | copy-start | bytes 786436
  88.3 26.3 %all-to-all-start.1 = ((bf16[16,64,256]{2,1,0:T(8,128)(2,1)}), bf16[16,64,256]{2,1,0:T(8,128)(2,1)S(1)}, u32[]{:S(2)}, u32[]{:S(2)}) async-start(bf16[16,64,256]{2,1,0:T(8,128)(2,1)} %pad_maximum_fusion.1), calls=%async_computation.1 | async-start | bytes 1048576 | tf_op jit(solution)/shard_map/all_to_all | solution.py:630
  112.1 6.4 %copy-start.4 = (bf16[1,512,512]{2,1,0:T(8,128)(2,1)S(1)}, bf16[1,512,512]{2,1,0:T(8,128)(2,1)}, u32[]{:S(2)}) copy-start(bf16[1,512,512]{2,1,0:T(8,128)(2,1)} %get-tuple-element.19) | copy-start | bytes 1572868
  114.7 0.8 copy-start.3
Sparse Core Ops, SparseCore 0:
  11.2 110.3 all-gather.1

commit v4 on v3

--- a/solution.py
+++ b/solution.py
@@ -252,11 +252,11 @@
     out_ref, hold, group = rest[8:]
     step = pl.program_id(0)
     tile = hold.shape[1]
-    seq_count, _, piece_rows, width = past_ref.shape
+    seq_count, piece_rows, width = past_ref.shape
     lines = 16
     half_tokens = group_refs[0].shape[1]
     gather_group(group_refs, group)
-    held = chunk // (2 * piece_rows)
+    held = chunk // piece_rows
     past_count = seq_count // held
     past_len = info[step + first]
     z_place, x_place, core = info[5], info[6], info[7]
@@ -320,9 +320,9 @@
 def attend_later(info, query, past, pieces, piece_blocks, first, lat, factor, head_local):
     prompts, rows, width = query.shape
     count = prompts - first
-    seq_count, _, halves, piece_rows, _ = past.shape
+    seq_count, _, piece_rows, _ = past.shape
     half_tokens = pieces[0].shape[2]
-    keys = seq_count * halves * (piece_rows + half_tokens)
+    keys = seq_count * (piece_rows + 2 * half_tokens)
     tile = 256
     chunk = 768
     return pl.pallas_call(
@@ -333,8 +333,7 @@
             in_specs=[
                 pl.BlockSpec((None, rows, width), lambda i, _: (i + first, 0, 0)),
                 pl.BlockSpec(
-                    (seq_count, None, halves, piece_rows, width),
-                    lambda i, _: (0, i + first, 0, 0, 0),
+                    (seq_count, None, piece_rows, width), lambda i, _: (0, i, 0, 0)
                 ),
             ]
             + group_specs(pieces, lambda i, _: (0, piece_blocks + i + first, 0, 0)),
@@ -388,13 +387,14 @@
     rows = q_ref.shape[1]
     width, cache_rows = pool_refs[0].shape
 
-    @pl.when(step * batch < used[0])
-    def _():
-        place = lax.broadcasted_iota(jnp.int32, (1, cache_rows), 1)
+    slots = [order[step * batch + b] for b in range(batch)]
+    longest = length[slots[0]]
+
+    def run(columns):
+        place = lax.broadcasted_iota(jnp.int32, (1, columns), 1)
         lane = lax.broadcasted_iota(jnp.int32, (rows, lse_ref.shape[2]), 1)
-        slots = [order[step * batch + b] for b in range(batch)]
         scores = [
-            key_scores(q_ref[slots[b], :, :width], pool_refs[b][...], lat, NN)
+            key_scores(q_ref[slots[b], :, :width], pool_refs[b][:, :columns], lat, NN)
             for b in range(batch)
         ]
         for b in range(batch):
@@ -402,7 +402,7 @@
             peak = jnp.max(masked, axis=1, keepdims=True)
             weights = jnp.exp2((masked - peak) * factor)
             total = jnp.sum(weights, axis=1, keepdims=True)
-            summed = dot(weights.astype(jnp.bfloat16), pool_refs[b][:lat], NT)
+            summed = dot(weights.astype(jnp.bfloat16), pool_refs[b][:lat, :columns], NT)
             out_ref[slots[b]] = (summed / total).astype(jnp.bfloat16)
             lse = peak * factor + jnp.log2(total)
             high = lse.astype(jnp.bfloat16).astype(jnp.float32)
@@ -411,6 +411,14 @@
             lse_ref[slots[b]] = jnp.where(
                 lane == 0, high, jnp.where(lane == 1, middle, low)
             ).astype(jnp.bfloat16)
+
+    for columns in range(128, cache_rows + 1, 128):
+
+        @pl.when(
+            (step * batch < used[0]) & (longest > columns - 128) & (longest <= columns)
+        )
+        def _(columns=columns):
+            run(columns)
 
 
 def attend_cache(order, length, used, query, pool, lat, factor):
@@ -529,10 +537,15 @@
     factor = (value_width + row_width - lat) ** (-0.5) * log2_e
 
     half = past_local // 2
-    past_part = lax.dynamic_slice(past_cache, (tp_place, core * half, 0), (1, half, row_width))
-    past_all = lax.all_gather(
-        past_part.reshape(half, row_width), ("seq", "tp", "grp"), axis=0, tiled=False
-    ).reshape(seq_count, prompt_count, 2, half, row_width)
+    eighth = (prompt_count - 1) * past_local // 8
+    past_part = lax.dynamic_slice_in_dim(
+        past_cache.reshape(prompt_count * past_local, row_width),
+        past_local + (tp_place * 2 + core) * eighth,
+        eighth,
+        axis=0,
+    )
+    past_all = lax.all_gather(past_part, ("seq", "tp", "grp"), axis=0, tiled=True)
+    past_all = past_all.reshape(seq_count, prompt_count - 1, past_local, row_width)
 
     half_tokens = group_local // 2
     pairs = 2 * request_local
@@ -604,15 +617,14 @@
     marks = arrived[:, 0, row_width:].astype(jnp.float32)
     slot_length = (marks[:, 0] * 16 + marks[:, 32]).astype(jnp.int32)
 
-    is_used = slot_length > 0
-    used_rank = jnp.cumsum(is_used.astype(jnp.int32)) - 1
-    used = jnp.sum(is_used.astype(jnp.int32))
     slots = jnp.arange(slot_count, dtype=jnp.int32)
+    longer = (slot_length[None, :] > slot_length[:, None]) | (
+        (slot_length[None, :] == slot_length[:, None]) & (slots[None, :] < slots[:, None])
+    )
+    rank = jnp.sum(longer.astype(jnp.int32), axis=1)
+    used = jnp.sum((slot_length > 0).astype(jnp.int32))
     wanted = jnp.minimum(slots, jnp.maximum(used - 1, 0))
-    order = jnp.sum(
-        jnp.where(is_used[None, :] & (used_rank[None, :] == wanted[:, None]), slots[None, :], 0),
-        axis=1,
-    )
+    order = jnp.sum(jnp.where(rank[None, :] == wanted[:, None], slots[None, :], 0), axis=1)
     cache_latent, cache_lse = attend_cache(
         order, slot_length, used.reshape(1), arrived, jnp.swapaxes(decode_pool, 1, 2), lat, factor
     )

time: 155 us -> 150 us (0.968)
  waiting for transfers between devices: 24.2 us -> 21.7 us
    all_gather x1, waiting for transfers between devices: 2.43 us -> 0.02 us  [on_device(): lax.all_gather(past_part, ('seq', 'tp', 'grp'), axis=0, tiled=True)]
    unnamed x29 -> x23, local copies, waits for them, and re-layouts: 3.07 us -> 3.14 us
  transfers between devices with their start and end apart: 17 -> 17, of which waited for: 6 -> 5; matrix products, arithmetic and copies ran while one was open for 13% -> 14% of each run, Pallas kernels for 21% -> 22%
where the time goes in v4:
time: 150 us; the launch traced here: 148 us
  Pallas kernels  52 us (35%)
  starting transfers between devices  30.8 us (21%)
  waiting for transfers between devices  21.7 us (14%)
  between operations  15.1 us (10%)
  matrix products  10.3 us (7%)
  other arithmetic  9.23 us (6%)
  local copies, waits for them, and re-layouts  9.17 us (6%)
    pallas_call x1, Pallas kernels, attend_later(): pl.pallas_call(functools.partial(later_body, (lat, factor), chunk, head_l...  20 us
    pallas_call x1, Pallas kernels, attend_first(): pl.pallas_call(functools.partial(first_body, (lat, factor), chunk, head_l...  18.2 us
    ppermute x6, waiting for transfers between devices, fetch_ring(): return lax.ppermute(value, ('seq', 'grp'), moves)  16.7 us
    pallas_call x1, Pallas kernels, attend_cache(): pl.pallas_call(functools.partial(cache_body, lat, factor, batch), grid_sp...  8.56 us
    ppermute x6, starting transfers between devices, fetch_ring(): return lax.ppermute(value, ('seq', 'grp'), moves)  7.76 us
    all_to_all x1, starting transfers between devices, on_device(): lax.all_to_all(send_query.reshape(seq_count, pair_limit * query_pairs, ro...  7.68 us
    all_to_all x1, starting transfers between devices, on_device(): lax.all_to_all(back.reshape(seq_count, pair_limit * query_pairs, 2 * valu...  5.19 us
    ppermute x5, starting transfers between devices, swap_core(): return lax.ppermute(value, 'grp', [(0, 1), (1, 0)])  5.08 us
  transfers between devices with their start and end apart: 17, of which 5 were waited for; matrix products, arithmetic and copies ran while one was open for 14% of the time, Pallas kernels for 22%

profile of v4, /device:TPU:1, one launch (start us, length us, event | category | flops | bytes accessed | tf_op | source)
XLA Modules:
  0.0 148.3 jit_solution(2657132198796256447)
XLA Ops:
  7.2 0.0 all-gather.2.cloned.1.call-start
  7.3 1.7 %constant_dynamic-slice_fusion = bf16[72,576]{1,0:T(8,128)(2,1)} fusion(bf16[768,576]{1,0:T(8,128)(2,1)} %bitcast.111, s32[]{:T(128)S(6)} %select_n.30), kind=kLoop, calls=%fused_computation.67 | loop fusion | bytes 165892 | tf_op jit(solution)/shard_map/dynamic_slice | solution.py:541
  9.0 0.8 reshape.167
  9.8 1.8 %convolution_convert_fusion = bf16[4,32,576]{2,1,0:T(8,128)(2,1)S(1)} fusion(bf16[4,32,896]{2,1,0:T(8,128)(2,1)} %param.12, bf16[896,576]{0,1:T(8,128)(2,1)} %param.21), kind=kOutput, calls=%fused_computation.12 | convolution fusion | flops 132194304 | bytes 1409024 | tf_op jit(solution)/shard_map/ptd,dc->ptc/dot_general | solution.py:552
  11.7 0.4 convolution_convert_fusion.2
  12.1 0.7 pad_maximum_fusion.4
  12.8 1.4 collective-permute-start
  14.2 0.2 convert_reduce_fusion.1
  14.4 0.5 copy-done.7
  14.9 0.6 select_reduce_fusion.1
  15.5 2.3 %dispatch_queries.1 = bf16[32,32,640]{2,1,0:T(8,128)(2,1)} custom-call(s32[32]{0:T(128)} %get-tuple-element.33.source, s32[32]{0:T(128)} %get-tuple-element.32.length, bf16[16,32,576]{2,1,0:T(8,128)(2,1)} %bitcast.97), custom_call_target="tpu_custom_call" | custom-call | tf_op jit(solution)/shard_map/dispatch_queries/pallas_call | solution.py:373
  17.8 7.7 %all-to-all-start = ((bf16[16,64,640]{2,1,0:T(8,128)(2,1)}), bf16[16,64,640]{2,1,0:T(8,128)(2,1)S(1)}, u32[]{:S(2)}, u32[]{:S(2)}) async-start(bf16[16,64,640]{2,1,0:T(8,128)(2,1)} %bitcast.88), calls=%async_computation | async-start | bytes 2621440 | tf_op jit(solution)/shard_map/all_to_all | solution.py:610
  25.5 0.1 iota_add_fusion
  25.6 0.1 add.146
  25.7 0.1 add_add_fusion
  25.8 0.1 add.154
  25.9 0.9 dynamic-slice_bitcast_fusion
  26.9 0.9 add_convert_fusion
  27.8 1.4 collective-permute-start.3
  29.2 2.6 %collective-permute-start.2 = (bf16[96,576]{1,0:T(8,128)(2,1)S(1)}, bf16[96,576]{1,0:T(8,128)(2,1)S(1)}, u32[]{:S(2)}, u32[]{:S(2)}) collective-permute-start(bf16[96,576]{1,0:T(8,128)(2,1)S(1)} %add_convert_fusion), channel_id=1, source_target_pairs={{4,0},{6,2},{0,4},{2,6},{5,1},{7,3},{1,5},{3,7},{12,8},{14,10},{8,... | collective-permute-start | bytes 331784 | tf_op jit(solution)/shard_map/ppermute | solution.py:494
  31.8 1.1 collective-permute-start.1
  32.9 0.1 add_convert_fusion.1
  32.9 1.2 collective-permute-done.3
  34.2 3.8 %collective-permute-done.2 = bf16[96,576]{1,0:T(8,128)(2,1)S(1)} collective-permute-done((bf16[96,576]{1,0:T(8,128)(2,1)S(1)}, bf16[96,576]{1,0:T(8,128)(2,1)S(1)}, u32[]{:S(2)}, u32[]{:S(2)}) %collective-permute-start.2) | collective-permute-done | bytes 110624 | tf_op jit(solution)/shard_map/ppermute | solution.py:494
  37.9 0.1 convert_add_fusion
  38.0 0.1 multiply_reduce_fusion
  38.1 0.3 fusion.41
  38.4 0.8 multiply_convert_fusion
  39.2 0.1 pad_maximum_fusion.6
  39.3 1.3 collective-permute-start.6
  40.6 2.4 %collective-permute-start.5 = (bf16[10,16,576]{2,1,0:T(8,128)(2,1)S(1)}, bf16[10,16,576]{2,1,0:T(8,128)(2,1)S(1)}, u32[]{:S(2)}, u32[]{:S(2)}) collective-permute-start(bf16[10,16,576]{2,1,0:T(8,128)(2,1)S(1)} %bitcast.94), channel_id=1, source_target_pairs={{16,0},{65,1},{24,8},{73,9},{0,16},{81,17},{8,24},{89,25},{48,32},... | collective-permute-start | bytes 552968 | tf_op jit(solution)/shard_map/ppermute | solution.py:507
  43.0 1.1 collective-permute-start.4
  44.1 1.3 collective-permute-done.6
  45.5 5.0 %collective-permute-done.5 = bf16[10,16,576]{2,1,0:T(8,128)(2,1)S(1)} collective-permute-done((bf16[10,16,576]{2,1,0:T(8,128)(2,1)S(1)}, bf16[10,16,576]{2,1,0:T(8,128)(2,1)S(1)}, u32[]{:S(2)}, u32[]{:S(2)}) %collective-permute-start.5) | collective-permute-done | bytes 184352 | tf_op jit(solution)/shard_map/ppermute | solution.py:507
  50.4 1.1 pad_maximum_fusion.rest_0_.rest_8_
  51.5 2.2 %collective-permute-start.10 = (bf16[4,10,16,576]{3,2,1,0:T(8,128)(2,1)}, bf16[4,10,16,576]{3,2,1,0:T(8,128)(2,1)}, u32[]{:S(2)}, u32[]{:S(2)}) collective-permute-start(bf16[4,10,16,576]{3,2,1,0:T(8,128)(2,1)} %pad_maximum_fusion.rest_0_.rest_8_), channel_id=1, source_target_pairs={{0,1},{1,0},{2,3},{3,2},{4,5},{5,4},{6,7},{7,6},{8,9},{9,8},{10,11... | collective-permute-start | bytes 2211848 | tf_op jit(solution)/shard_map/ppermute | solution.py:490
  53.8 1.6 %collective-permute-start.8 = (bf16[4,10,16,576]{3,2,1,0:T(8,128)(2,1)}, bf16[4,10,16,576]{3,2,1,0:T(8,128)(2,1)}, u32[]{:S(2)}, u32[]{:S(2)}) collective-permute-start(bf16[4,10,16,576]{3,2,1,0:T(8,128)(2,1)} %pad_maximum_fusion.rest_0_.rest_8_), channel_id=1, source_target_pairs={{64,0},{17,1},{72,8},{25,9},{80,16},{1,17},{88,24},{9,25},{96,32},... | collective-permute-start | bytes 2211848 | tf_op jit(solution)/shard_map/ppermute | solution.py:507
  55.3 1.4 collective-permute-start.7
  56.7 0.1 slice_convert_fusion
  56.8 0.2 fusion.45.length
  57.0 0.7 copy-done.6
  57.6 0.7 fusion.49
  59.0 0.9 convert_reduce_fusion
  59.9 0.7 select_reduce_fusion.order
  60.6 8.6 %attend_cache.1 = (bf16[32,32,512]{2,1,0:T(8,128)(2,1)}, bf16[32,32,128]{2,1,0:T(8,128)(2,1)}) custom-call(s32[32]{0:T(128)} %select_reduce_fusion.order, s32[32]{0:T(128)} %copy-done.6, s32[1]{0:T(128)} %bitcast.21.used, bf16[32,32,640]{2,1,0:T(8,128)(2,1)} %bitcast.87, bf16[32,576,384]{2,1,0:T(8,128)(2,1)} %bitcast.82, bf16[32,576,384]{2,1,0:T(8,128)(2,1)} %bitcast.83, ...), custom_call_target="tpu_custom_call" | custom-call | flops 3422552064 | bytes 14155776 | tf_op jit(solution)/shard_map/attend_cache/pallas_call | solution.py:435
  69.2 10.3 %collective-permute-done.9.rest_3_.rest_11_ = bf16[4,10,16,576]{3,2,1,0:T(8,128)(2,1)} collective-permute-done((bf16[4,10,16,576]{3,2,1,0:T(8,128)(2,1)}, bf16[4,10,16,576]{3,2,1,0:T(8,128)(2,1)}, u32[]{:S(2)}, u32[]{:S(2)}) %collective-permute-start.9) | collective-permute-done | bytes 737312 | tf_op jit(solution)/shard_map/ppermute | solution.py:507
  79.5 0.9 collective-permute-start.11
  80.4 0.5 collective-permute-start.13
  80.9 1.3 stack.31.info
  82.2 0.7 fusion.35.fresh_ref
  83.0 2.5 %fusion.23 = bf16[32,2,16,128]{3,0,1,2:T(8,128)(2,1)S(1)} fusion(bf16[16,512,128]{2,1,0:T(8,128)(2,1)S(1)} %copy-done, bf16[32,2,16,512]{3,2,1,0:T(8,128)(2,1)} %bitcast.90), kind=kOutput, calls=%fused_computation.11 | convolution fusion | flops 134348800 | bytes 3407872 | tf_op jit(solution)/shard_map/nshc,hcv->nshv/dot_general | solution.py:633
  85.5 0.2 copy.48
  85.7 0.9 pad_maximum_fusion.1
  86.6 5.2 %all-to-all-start.1 = ((bf16[16,64,256]{2,1,0:T(8,128)(2,1)}), bf16[16,64,256]{2,1,0:T(8,128)(2,1)S(1)}, u32[]{:S(2)}, u32[]{:S(2)}) async-start(bf16[16,64,256]{2,1,0:T(8,128)(2,1)} %pad_maximum_fusion.1), calls=%async_computation.1 | async-start | bytes 1048576 | tf_op jit(solution)/shard_map/all_to_all | solution.py:642
  91.8 18.2 %attend_first.1 = (bf16[1,512,512]{2,1,0:T(8,128)(2,1)}, bf16[512,512]{1,0:T(8,128)(2,1)}, f32[512,128]{1,0:T(8,128)}) custom-call(s32[8]{0:T(128)} %stack.31.info, bf16[4,512,576]{2,1,0:T(8,128)(2,1)} %bitcast.114, bf16[512,576]{1,0:T(8,128)(2,1)} %bitcast.98, bf16[128,576]{1,0:T(8,128)(2,1)} %fusion.35.fresh_ref, ...), custom_call_target="tpu_custom_call" | custom-call | flops 9730785280 | bytes 6635520 | tf_op jit(solution)/shard_map/attend_first/pallas_call | solution.py:211
  110.0 1.6 %fusion.20 = f32[16,2,16,128]{3,0,1,2:T(8,128)S(1)} fusion(bf16[16,512,128]{2,1,0:T(8,128)(2,1)S(1)} %copy-done, bf16[16,2,16,512]{3,2,1,0:T(8,128)(2,1)} %bitcast.101), kind=kOutput, calls=%fused_computation.10 | convolution fusion | flops 67108864 | bytes 2883584 | tf_op jit(solution)/shard_map/rshc,hcv->rshv/dot_general | solution.py:667
  111.7 0.9 copy.50
  112.5 0.8 copy-done.3
  113.3 3.0 %merge_decode.1 = bf16[16,32,128]{2,1,0:T(8,128)(2,1)} custom-call(s32[16]{0:T(128)} %copy-done.7, bf16[32,32,256]{2,1,0:T(8,128)(2,1)} %bitcast.89, f32[16,32,128]{2,1,0:T(8,128)} %bitcast.91, f32[16,32,128]{2,1,0:T(8,128)} %bitcast.105), custom_call_target="tpu_custom_call" | custom-call | tf_op jit(solution)/shard_map/merge_decode/pallas_call | solution.py:479
  116.3 0.6 fusion.26
  116.9 20.0 %attend_later.1 = bf16[3,512,512]{2,1,0:T(8,128)(2,1)} custom-call(s32[8]{0:T(128)} %stack.31.info, bf16[4,512,576]{2,1,0:T(8,128)(2,1)} %bitcast.115, bf16[16,3,192,576]{3,2,1,0:T(8,128)(2,1)} %bitcast.113, bf16[4,10,16,576]{3,2,1,0:T(8,128)(2,1)} %pad_maximum_fusion.rest_0_.rest_8_, bf16[4,10,16,576]{3,2,1,0:T(8,128)(2,1)} %collective-permute-done.7.rest_1_.rest_9_, ...), custom_call_target="tpu_custom_call" | custom-call | flops 14092861440 | bytes 15925248 | tf_op jit(solution)/shard_map/attend_later/pallas_call | solution.py:328
  136.9 3.3 %fusion.12 = bf16[3,32,16,128]{3,1,0,2:T(8,128)(2,1)S(1)} fusion(bf16[16,512,128]{2,1,0:T(8,128)(2,1)S(1)} %copy-done, bf16[3,32,16,512]{3,2,1,0:T(8,128)(2,1)} %bitcast.117), kind=kOutput, calls=%fused_computation.8 | convolution fusion | flops 201523200 | bytes 4063232 | tf_op jit(solution)/shard_map/pthc,hcv->pthv/dot_general | solution.py:686
  140.2 0.1 pad_maximum_fusion.2
  140.3 1.1 copy.53
  (42 shorter events, 0.2 us)
Async XLA Ops:
  7.2 75.8 %copy-start = (bf16[16,512,128]{2,1,0:T(8,128)(2,1)S(1)}, bf16[16,512,128]{2,1,0:T(8,128)(2,1)}, u32[]{:S(2)}) copy-start(bf16[16,512,128]{2,1,0:T(8,128)(2,1)} %param.23) | copy-start | bytes 6291460
  7.2 4.5 %copy-start.2 = (bf16[896,576]{0,1:T(8,128)(2,1)S(1)}, bf16[896,576]{0,1:T(8,128)(2,1)}, u32[]{:S(2)}) copy-start(bf16[896,576]{0,1:T(8,128)(2,1)} %param.21) | copy-start | bytes 3096580
  7.2 7.0 %copy-start.10 = (s32[16,1]{0,1:T(1,128)S(1)}, s32[16,1]{0,1:T(1,128)}, u32[]{:S(2)}) copy-start(s32[16,1]{0,1:T(1,128)} %param.19) | copy-start | bytes 196
  7.2 7.7 %copy-start.8 = (s32[16]{0:T(128)S(1)}, s32[16]{0:T(128)}, u32[]{:S(2)}) copy-start(s32[16]{0:T(128)} %param.20) | copy-start | bytes 196
  7.2 109.7 %all-gather.2.cloned.1.call-start = ((), (), s32[]{:S(2)}) async-start(), calls=%async_computation.2 | async-start | bytes 11888640 | tf_op jit(solution)/shard_map/all_gather | solution.py:547
  12.8 14.1 %collective-permute-start = (bf16[96,576]{1,0:T(8,128)(2,1)}, bf16[96,576]{1,0:T(8,128)(2,1)}, u32[]{:S(2)}, u32[]{:S(2)}) collective-permute-start(bf16[96,576]{1,0:T(8,128)(2,1)} %pad_maximum_fusion.4), channel_id=1, source_target_pairs={{0,1},{1,0},{2,3},{3,2},{4,5},{5,4},{6,7},{7,6},{8,9},{9,8},{10,11... | collective-permute-start | bytes 331784 | tf_op jit(solution)/shard_map/ppermute | solution.py:490
  14.4 0.5 copy-start.7
  15.5 10.0 %copy-start.9 = (s32[4]{0:T(128)S(1)}, s32[4]{0:T(128)}, u32[]{:S(2)}) copy-start(s32[4]{0:T(128)} %param.15) | copy-start | bytes 52
  17.8 38.9 %all-to-all-start = ((bf16[16,64,640]{2,1,0:T(8,128)(2,1)}), bf16[16,64,640]{2,1,0:T(8,128)(2,1)S(1)}, u32[]{:S(2)}, u32[]{:S(2)}) async-start(bf16[16,64,640]{2,1,0:T(8,128)(2,1)} %bitcast.88), calls=%async_computation | async-start | bytes 2621440 | tf_op jit(solution)/shard_map/all_to_all | solution.py:610
  27.8 6.4 %collective-permute-start.3 = (bf16[96,576]{1,0:T(8,128)(2,1)S(1)}, bf16[96,576]{1,0:T(8,128)(2,1)S(1)}, u32[]{:S(2)}, u32[]{:S(2)}) collective-permute-start(bf16[96,576]{1,0:T(8,128)(2,1)S(1)} %add_convert_fusion), channel_id=1, source_target_pairs={{6,0},{0,2},{2,4},{4,6},{7,1},{1,3},{3,5},{5,7},{14,8},{8,10},{10,... | collective-permute-start | bytes 331784 | tf_op jit(solution)/shard_map/ppermute | solution.py:494
  29.2 8.8 %collective-permute-start.2 = (bf16[96,576]{1,0:T(8,128)(2,1)S(1)}, bf16[96,576]{1,0:T(8,128)(2,1)S(1)}, u32[]{:S(2)}, u32[]{:S(2)}) collective-permute-start(bf16[96,576]{1,0:T(8,128)(2,1)S(1)} %add_convert_fusion), channel_id=1, source_target_pairs={{4,0},{6,2},{0,4},{2,6},{5,1},{7,3},{1,5},{3,7},{12,8},{14,10},{8,... | collective-permute-start | bytes 331784 | tf_op jit(solution)/shard_map/ppermute | solution.py:494
  31.8 6.1 %collective-permute-start.1 = (bf16[96,576]{1,0:T(8,128)(2,1)S(1)}, bf16[96,576]{1,0:T(8,128)(2,1)S(1)}, u32[]{:S(2)}, u32[]{:S(2)}) collective-permute-start(bf16[96,576]{1,0:T(8,128)(2,1)S(1)} %add_convert_fusion), channel_id=1, source_target_pairs={{2,0},{4,2},{6,4},{0,6},{3,1},{5,3},{7,5},{1,7},{10,8},{12,10},{14... | collective-permute-start | bytes 331784 | tf_op jit(solution)/shard_map/ppermute | solution.py:494
  39.3 6.2 %collective-permute-start.6 = (bf16[10,16,576]{2,1,0:T(8,128)(2,1)S(1)}, bf16[10,16,576]{2,1,0:T(8,128)(2,1)S(1)}, u32[]{:S(2)}, u32[]{:S(2)}) collective-permute-start(bf16[10,16,576]{2,1,0:T(8,128)(2,1)S(1)} %bitcast.93), channel_id=1, source_target_pairs={{24,0},{97,1},{0,8},{105,9},{8,16},{113,17},{16,24},{121,25},{56,3... | collective-permute-start | bytes 552968 | tf_op jit(solution)/shard_map/ppermute | solution.py:507
  40.6 9.8 %collective-permute-start.5 = (bf16[10,16,576]{2,1,0:T(8,128)(2,1)S(1)}, bf16[10,16,576]{2,1,0:T(8,128)(2,1)S(1)}, u32[]{:S(2)}, u32[]{:S(2)}) collective-permute-start(bf16[10,16,576]{2,1,0:T(8,128)(2,1)S(1)} %bitcast.94), channel_id=1, source_target_pairs={{16,0},{65,1},{24,8},{73,9},{0,16},{81,17},{8,24},{89,25},{48,32},... | collective-permute-start | bytes 552968 | tf_op jit(solution)/shard_map/ppermute | solution.py:507
  43.0 7.4 %collective-permute-start.4 = (bf16[10,16,576]{2,1,0:T(8,128)(2,1)S(1)}, bf16[10,16,576]{2,1,0:T(8,128)(2,1)S(1)}, u32[]{:S(2)}, u32[]{:S(2)}) collective-permute-start(bf16[10,16,576]{2,1,0:T(8,128)(2,1)S(1)} %bitcast.95), channel_id=1, source_target_pairs={{8,0},{33,1},{16,8},{41,9},{24,16},{49,17},{0,24},{57,25},{40,32},... | collective-permute-start | bytes 552968 | tf_op jit(solution)/shard_map/ppermute | solution.py:507
  51.5 40.3 %collective-permute-start.10 = (bf16[4,10,16,576]{3,2,1,0:T(8,128)(2,1)}, bf16[4,10,16,576]{3,2,1,0:T(8,128)(2,1)}, u32[]{:S(2)}, u32[]{:S(2)}) collective-permute-start(bf16[4,10,16,576]{3,2,1,0:T(8,128)(2,1)} %pad_maximum_fusion.rest_0_.rest_8_), channel_id=1, source_target_pairs={{0,1},{1,0},{2,3},{3,2},{4,5},{5,4},{6,7},{7,6},{8,9},{9,8},{10,11... | collective-permute-start | bytes 2211848 | tf_op jit(solution)/shard_map/ppermute | solution.py:490
  53.8 25.7 %collective-permute-start.9 = (bf16[4,10,16,576]{3,2,1,0:T(8,128)(2,1)}, bf16[4,10,16,576]{3,2,1,0:T(8,128)(2,1)}, u32[]{:S(2)}, u32[]{:S(2)}) collective-permute-start(bf16[4,10,16,576]{3,2,1,0:T(8,128)(2,1)} %pad_maximum_fusion.rest_0_.rest_8_), channel_id=1, source_target_pairs={{96,0},{25,1},{104,8},{1,9},{112,16},{9,17},{120,24},{17,25},{0,32... | collective-permute-start | bytes 2211848 | tf_op jit(solution)/shard_map/ppermute | solution.py:507
  53.8 25.7 %collective-permute-start.8 = (bf16[4,10,16,576]{3,2,1,0:T(8,128)(2,1)}, bf16[4,10,16,576]{3,2,1,0:T(8,128)(2,1)}, u32[]{:S(2)}, u32[]{:S(2)}) collective-permute-start(bf16[4,10,16,576]{3,2,1,0:T(8,128)(2,1)} %pad_maximum_fusion.rest_0_.rest_8_), channel_id=1, source_target_pairs={{64,0},{17,1},{72,8},{25,9},{80,16},{1,17},{88,24},{9,25},{96,32},... | collective-permute-start | bytes 2211848 | tf_op jit(solution)/shard_map/ppermute | solution.py:507
  55.3 24.2 %collective-permute-start.7 = (bf16[4,10,16,576]{3,2,1,0:T(8,128)(2,1)}, bf16[4,10,16,576]{3,2,1,0:T(8,128)(2,1)}, u32[]{:S(2)}, u32[]{:S(2)}) collective-permute-start(bf16[4,10,16,576]{3,2,1,0:T(8,128)(2,1)} %pad_maximum_fusion.rest_0_.rest_8_), channel_id=1, source_target_pairs={{32,0},{9,1},{40,8},{17,9},{48,16},{25,17},{56,24},{1,25},{64,32},... | collective-permute-start | bytes 2211848 | tf_op jit(solution)/shard_map/ppermute | solution.py:507
  56.7 3.9 %copy-start.1 = (bf16[16,64,640]{2,1,0:T(8,128)(2,1)}, bf16[16,64,640]{2,1,0:T(8,128)(2,1)S(1)}, u32[]{:S(2)}) copy-start(bf16[16,64,640]{2,1,0:T(8,128)(2,1)S(1)} %all-to-all-done) | copy-start | bytes 3932164
  57.0 0.7 copy-start.6
  79.5 12.3 %collective-permute-start.11 = (bf16[4,10,16,576]{3,2,1,0:T(8,128)(2,1)}, bf16[4,10,16,576]{3,2,1,0:T(8,128)(2,1)}, u32[]{:S(2)}, u32[]{:S(2)}) collective-permute-start(bf16[4,10,16,576]{3,2,1,0:T(8,128)(2,1)} %collective-permute-done.7.rest_1_.rest_9_), channel_id=1, source_target_pairs={{0,1},{1,0},{2,3},{3,2},{4,5},{5,4},{6,7},{7,6},{8,9},{9,8},{10,11... | collective-permute-start | bytes 2211848 | tf_op jit(solution)/shard_map/ppermute | solution.py:490
  80.4 11.4 %collective-permute-start.12 = (bf16[4,10,16,576]{3,2,1,0:T(8,128)(2,1)}, bf16[4,10,16,576]{3,2,1,0:T(8,128)(2,1)}, u32[]{:S(2)}, u32[]{:S(2)}) collective-permute-start(bf16[4,10,16,576]{3,2,1,0:T(8,128)(2,1)} %collective-permute-done.8.rest_2_.rest_10_), channel_id=1, source_target_pairs={{0,1},{1,0},{2,3},{3,2},{4,5},{5,4},{6,7},{7,6},{8,9},{9,8},{10,11... | collective-permute-start | bytes 2211848 | tf_op jit(solution)/shard_map/ppermute | solution.py:490
  80.4 11.4 %collective-permute-start.13 = (bf16[4,10,16,576]{3,2,1,0:T(8,128)(2,1)}, bf16[4,10,16,576]{3,2,1,0:T(8,128)(2,1)}, u32[]{:S(2)}, u32[]{:S(2)}) collective-permute-start(bf16[4,10,16,576]{3,2,1,0:T(8,128)(2,1)} %collective-permute-done.9.rest_3_.rest_11_), channel_id=1, source_target_pairs={{0,1},{1,0},{2,3},{3,2},{4,5},{5,4},{6,7},{7,6},{8,9},{9,8},{10,11... | collective-permute-start | bytes 2211848 | tf_op jit(solution)/shard_map/ppermute | solution.py:490
  82.2 3.5 %copy-start.5 = (bf16[32,32,128]{2,1,0:T(8,128)(2,1)S(1)}, bf16[32,32,128]{2,1,0:T(8,128)(2,1)}, u32[]{:S(2)}) copy-start(bf16[32,32,128]{2,1,0:T(8,128)(2,1)} %get-tuple-element.20) | copy-start | bytes 786436
  86.6 25.9 %all-to-all-start.1 = ((bf16[16,64,256]{2,1,0:T(8,128)(2,1)}), bf16[16,64,256]{2,1,0:T(8,128)(2,1)S(1)}, u32[]{:S(2)}, u32[]{:S(2)}) async-start(bf16[16,64,256]{2,1,0:T(8,128)(2,1)} %pad_maximum_fusion.1), calls=%async_computation.1 | async-start | bytes 1048576 | tf_op jit(solution)/shard_map/all_to_all | solution.py:642
  110.0 6.3 %copy-start.4 = (bf16[1,512,512]{2,1,0:T(8,128)(2,1)S(1)}, bf16[1,512,512]{2,1,0:T(8,128)(2,1)}, u32[]{:S(2)}) copy-start(bf16[1,512,512]{2,1,0:T(8,128)(2,1)} %get-tuple-element.19) | copy-start | bytes 1572868
  112.5 0.8 copy-start.3
Sparse Core Ops, SparseCore 0:
  11.0 103.1 all-gather.1

commit v5 on v4

--- a/solution.py
+++ b/solution.py
@@ -628,8 +628,6 @@
     cache_latent, cache_lse = attend_cache(
         order, slot_length, used.reshape(1), arrived, jnp.swapaxes(decode_pool, 1, 2), lat, factor
     )
-    lines[1:], cache_latent = lax.optimization_barrier((lines[1:], cache_latent))
-    pieces = lines + [swap_core(piece) for piece in lines]
     cache_value = jnp.einsum(
         "nshc,hcv->nshv",
         cache_latent.reshape(slot_count, 2, head_local, lat),
@@ -639,6 +637,8 @@
     back = jnp.concatenate(
         [cache_value.reshape(slot_count, query_pairs, value_width), cache_lse], axis=-1
     )
+    lines[1:], _ = lax.optimization_barrier((lines[1:], back))
+    pieces = lines + [swap_core(piece) for piece in lines]
     back = lax.all_to_all(
         back.reshape(seq_count, pair_limit * query_pairs, 2 * value_width),
         "seq",

time: 150 us -> 163 us (1.087); the launches traced: 148 us -> 163 us
  waiting for transfers between devices: 21.7 us -> 35.7 us
  starting transfers between devices: 30.8 us -> 32.7 us
    ppermute x6, waiting for transfers between devices: 16.7 us -> 27 us  [fetch_ring(): return lax.ppermute(value, ('seq', 'grp'), moves)]
    ppermute x3, waiting for transfers between devices: 5 us -> 8.64 us  [fetch_tp(): return lax.ppermute(value, 'tp', [((i + shift) % 4, i) for i in range(4)])]
    all_to_all x1, starting transfers between devices: 5.19 us -> 8.02 us  [on_device(): lax.all_to_all(back.reshape(seq_count, pair_limit * query_pairs, 2 * valu...]
    ppermute x5, starting transfers between devices: 5.08 us -> 6.86 us  [swap_core(): return lax.ppermute(value, 'grp', [(0, 1), (1, 0)])]
    ppermute x6, starting transfers between devices: 7.76 us -> 6.09 us  [fetch_ring(): return lax.ppermute(value, ('seq', 'grp'), moves)]
  transfers between devices with their start and end apart: 17 -> 17, of which waited for: 5 -> 9; matrix products, arithmetic and copies ran while one was open for 14% -> 12% of each run, Pallas kernels for 22% -> 19%
where the time goes in v5:
time: 163 us
  Pallas kernels  52.6 us (32%)
  waiting for transfers between devices  35.7 us (22%)
  starting transfers between devices  32.7 us (20%)
  between operations  15 us (9%)
  matrix products  10.4 us (6%)
  local copies, waits for them, and re-layouts  8.6 us (5%)
  other arithmetic  7.92 us (5%)
    ppermute x6, waiting for transfers between devices, fetch_ring(): return lax.ppermute(value, ('seq', 'grp'), moves)  27 us
    pallas_call x1, Pallas kernels, attend_later(): pl.pallas_call(functools.partial(later_body, (lat, factor), chunk, head_l...  20.9 us
    pallas_call x1, Pallas kernels, attend_first(): pl.pallas_call(functools.partial(first_body, (lat, factor), chunk, head_l...  17.9 us
    ppermute x3, waiting for transfers between devices, fetch_tp(): return lax.ppermute(value, 'tp', [((i + shift) % 4, i) for i in range(4)])  8.64 us
    pallas_call x1, Pallas kernels, attend_cache(): pl.pallas_call(functools.partial(cache_body, lat, factor, batch), grid_sp...  8.46 us
    all_to_all x1, starting transfers between devices, on_device(): lax.all_to_all(back.reshape(seq_count, pair_limit * query_pairs, 2 * valu...  8.02 us
    all_to_all x1, starting transfers between devices, on_device(): lax.all_to_all(send_query.reshape(seq_count, pair_limit * query_pairs, ro...  7.81 us
    ppermute x5, starting transfers between devices, swap_core(): return lax.ppermute(value, 'grp', [(0, 1), (1, 0)])  6.86 us
  transfers between devices with their start and end apart: 17, of which 9 were waited for; matrix products, arithmetic and copies ran while one was open for 12% of the time, Pallas kernels for 19%

profile of v5, /device:TPU:1, one launch (start us, length us, event | category | flops | bytes accessed | tf_op | source)
XLA Modules:
  0.0 163.0 jit_solution(2396779223290025182)
XLA Ops:
  7.3 1.7 %constant_dynamic-slice_fusion = bf16[72,576]{1,0:T(8,128)(2,1)} fusion(bf16[768,576]{1,0:T(8,128)(2,1)} %bitcast.111, s32[]{:T(128)S(6)} %select_n.30), kind=kLoop, calls=%fused_computation.68 | loop fusion | bytes 165892 | tf_op jit(solution)/shard_map/dynamic_slice | solution.py:541
  9.0 0.8 reshape.172
  9.8 1.8 %convolution_convert_fusion = bf16[4,32,576]{2,1,0:T(8,128)(2,1)S(1)} fusion(bf16[4,32,896]{2,1,0:T(8,128)(2,1)} %param.12, bf16[896,576]{0,1:T(8,128)(2,1)} %param.21), kind=kOutput, calls=%fused_computation.12 | convolution fusion | flops 132194304 | bytes 1409024 | tf_op jit(solution)/shard_map/ptd,dc->ptc/dot_general | solution.py:552
  11.7 0.4 convolution_convert_fusion.2
  12.1 0.7 pad_maximum_fusion.5
  12.8 1.4 collective-permute-start
  14.2 0.2 convert_reduce_fusion.1
  14.4 0.6 copy-done.8
  15.0 0.7 select_reduce_fusion.1
  15.6 2.4 %dispatch_queries.1 = bf16[32,32,640]{2,1,0:T(8,128)(2,1)} custom-call(s32[32]{0:T(128)} %get-tuple-element.31.source, s32[32]{0:T(128)} %get-tuple-element.30.length, bf16[16,32,576]{2,1,0:T(8,128)(2,1)} %bitcast.97), custom_call_target="tpu_custom_call" | custom-call | tf_op jit(solution)/shard_map/dispatch_queries/pallas_call | solution.py:373
  18.1 7.8 %all-to-all-start = ((bf16[16,64,640]{2,1,0:T(8,128)(2,1)}), bf16[16,64,640]{2,1,0:T(8,128)(2,1)S(1)}, u32[]{:S(2)}, u32[]{:S(2)}) async-start(bf16[16,64,640]{2,1,0:T(8,128)(2,1)} %bitcast.88), calls=%async_computation | async-start | bytes 2621440 | tf_op jit(solution)/shard_map/all_to_all | solution.py:610
  26.0 0.1 add.147
  26.1 0.1 add_add_fusion
  26.2 0.1 add.155
  26.3 0.9 dynamic-slice_bitcast_fusion
  27.2 0.9 add_convert_fusion
  28.2 2.8 %collective-permute-start.1 = (bf16[96,576]{1,0:T(8,128)(2,1)S(1)}, bf16[96,576]{1,0:T(8,128)(2,1)S(1)}, u32[]{:S(2)}, u32[]{:S(2)}) collective-permute-start(bf16[96,576]{1,0:T(8,128)(2,1)S(1)} %add_convert_fusion), channel_id=1, source_target_pairs={{2,0},{4,2},{6,4},{0,6},{3,1},{5,3},{7,5},{1,7},{10,8},{12,10},{14... | collective-permute-start | bytes 331784 | tf_op jit(solution)/shard_map/ppermute | solution.py:494
  31.0 0.3 collective-permute-start.2
  31.3 0.7 collective-permute-start.3
  32.0 0.1 add_convert_fusion.1
  32.1 3.8 %collective-permute-done.1 = bf16[96,576]{1,0:T(8,128)(2,1)S(1)} collective-permute-done((bf16[96,576]{1,0:T(8,128)(2,1)S(1)}, bf16[96,576]{1,0:T(8,128)(2,1)S(1)}, u32[]{:S(2)}, u32[]{:S(2)}) %collective-permute-start.1) | collective-permute-done | bytes 110624 | tf_op jit(solution)/shard_map/ppermute | solution.py:494
  35.9 0.9 collective-permute-done.2
  36.8 3.9 %collective-permute-done.3 = bf16[96,576]{1,0:T(8,128)(2,1)S(1)} collective-permute-done((bf16[96,576]{1,0:T(8,128)(2,1)S(1)}, bf16[96,576]{1,0:T(8,128)(2,1)S(1)}, u32[]{:S(2)}, u32[]{:S(2)}) %collective-permute-start.3) | collective-permute-done | bytes 110624 | tf_op jit(solution)/shard_map/ppermute | solution.py:494
  40.8 0.1 multiply_reduce_fusion
  40.9 0.1 multiply_convert_fusion
  41.0 0.3 fusion.42
  41.3 0.1 fusion.34
  41.4 2.5 %collective-permute-start.4 = (bf16[10,16,576]{2,1,0:T(8,128)(2,1)S(1)}, bf16[10,16,576]{2,1,0:T(8,128)(2,1)S(1)}, u32[]{:S(2)}, u32[]{:S(2)}) collective-permute-start(bf16[10,16,576]{2,1,0:T(8,128)(2,1)S(1)} %bitcast.93), channel_id=1, source_target_pairs={{8,0},{33,1},{16,8},{41,9},{24,16},{49,17},{0,24},{57,25},{40,32},... | collective-permute-start | bytes 552968 | tf_op jit(solution)/shard_map/ppermute | solution.py:507
  43.9 0.6 collective-permute-start.5
  44.5 0.6 collective-permute-start.6
  45.1 3.7 %collective-permute-done.4 = bf16[10,16,576]{2,1,0:T(8,128)(2,1)S(1)} collective-permute-done((bf16[10,16,576]{2,1,0:T(8,128)(2,1)S(1)}, bf16[10,16,576]{2,1,0:T(8,128)(2,1)S(1)}, u32[]{:S(2)}, u32[]{:S(2)}) %collective-permute-start.4) | collective-permute-done | bytes 184352 | tf_op jit(solution)/shard_map/ppermute | solution.py:507
  48.8 2.8 %collective-permute-done.5 = bf16[10,16,576]{2,1,0:T(8,128)(2,1)S(1)} collective-permute-done((bf16[10,16,576]{2,1,0:T(8,128)(2,1)S(1)}, bf16[10,16,576]{2,1,0:T(8,128)(2,1)S(1)}, u32[]{:S(2)}, u32[]{:S(2)}) %collective-permute-start.5) | collective-permute-done | bytes 184352 | tf_op jit(solution)/shard_map/ppermute | solution.py:507
  51.6 1.8 %collective-permute-done.6 = bf16[10,16,576]{2,1,0:T(8,128)(2,1)S(1)} collective-permute-done((bf16[10,16,576]{2,1,0:T(8,128)(2,1)S(1)}, bf16[10,16,576]{2,1,0:T(8,128)(2,1)S(1)}, u32[]{:S(2)}, u32[]{:S(2)}) %collective-permute-start.6) | collective-permute-done | bytes 184352 | tf_op jit(solution)/shard_map/ppermute | solution.py:507
  53.4 1.1 pad_maximum_fusion.rest_0_.rest_8_
  54.5 1.2 collective-permute-start.7
  55.7 0.5 collective-permute-start.8
  56.2 0.7 collective-permute-start.9
  56.9 1.3 stack.31.info
  58.2 0.7 fusion.36.fresh_ref
  58.9 2.8 %collective-permute-start.10 = (bf16[4,10,16,576]{3,2,1,0:T(8,128)(2,1)}, bf16[4,10,16,576]{3,2,1,0:T(8,128)(2,1)}, u32[]{:S(2)}, u32[]{:S(2)}) collective-permute-start(bf16[4,10,16,576]{3,2,1,0:T(8,128)(2,1)} %pad_maximum_fusion.rest_0_.rest_8_), channel_id=1, source_target_pairs={{0,1},{1,0},{2,3},{3,2},{4,5},{5,4},{6,7},{7,6},{8,9},{9,8},{10,11... | collective-permute-start | bytes 2211848 | tf_op jit(solution)/shard_map/ppermute | solution.py:490
  61.7 6.7 %collective-permute-done.7.rest_1_.rest_9_ = bf16[4,10,16,576]{3,2,1,0:T(8,128)(2,1)} collective-permute-done((bf16[4,10,16,576]{3,2,1,0:T(8,128)(2,1)}, bf16[4,10,16,576]{3,2,1,0:T(8,128)(2,1)}, u32[]{:S(2)}, u32[]{:S(2)}) %collective-permute-start.7) | collective-permute-done | bytes 737312 | tf_op jit(solution)/shard_map/ppermute | solution.py:507
  68.4 3.1 %collective-permute-done.8.rest_2_.rest_10_ = bf16[4,10,16,576]{3,2,1,0:T(8,128)(2,1)} collective-permute-done((bf16[4,10,16,576]{3,2,1,0:T(8,128)(2,1)}, bf16[4,10,16,576]{3,2,1,0:T(8,128)(2,1)}, u32[]{:S(2)}, u32[]{:S(2)}) %collective-permute-start.8) | collective-permute-done | bytes 737312 | tf_op jit(solution)/shard_map/ppermute | solution.py:507
  71.5 8.9 %collective-permute-done.9.rest_3_.rest_11_ = bf16[4,10,16,576]{3,2,1,0:T(8,128)(2,1)} collective-permute-done((bf16[4,10,16,576]{3,2,1,0:T(8,128)(2,1)}, bf16[4,10,16,576]{3,2,1,0:T(8,128)(2,1)}, u32[]{:S(2)}, u32[]{:S(2)}) %collective-permute-start.9) | collective-permute-done | bytes 737312 | tf_op jit(solution)/shard_map/ppermute | solution.py:507
  80.4 2.2 %collective-permute-start.11 = (bf16[4,10,16,576]{3,2,1,0:T(8,128)(2,1)}, bf16[4,10,16,576]{3,2,1,0:T(8,128)(2,1)}, u32[]{:S(2)}, u32[]{:S(2)}) collective-permute-start(bf16[4,10,16,576]{3,2,1,0:T(8,128)(2,1)} %collective-permute-done.7.rest_1_.rest_9_), channel_id=1, source_target_pairs={{0,1},{1,0},{2,3},{3,2},{4,5},{5,4},{6,7},{7,6},{8,9},{9,8},{10,11... | collective-permute-start | bytes 2211848 | tf_op jit(solution)/shard_map/ppermute | solution.py:490
  82.6 0.5 collective-permute-start.13
  83.1 0.1 slice_convert_fusion
  83.2 0.2 fusion.46.length
  83.4 0.7 fusion.50
  84.7 0.2 convert_reduce_fusion
  84.9 0.7 select_reduce_fusion.order
  85.6 8.5 %attend_cache.1 = (bf16[32,32,512]{2,1,0:T(8,128)(2,1)}, bf16[32,32,128]{2,1,0:T(8,128)(2,1)}) custom-call(s32[32]{0:T(128)} %select_reduce_fusion.order, s32[32]{0:T(128)} %copy-done.6, s32[1]{0:T(128)} %bitcast.10.used, bf16[32,32,640]{2,1,0:T(8,128)(2,1)} %bitcast.87, bf16[32,576,384]{2,1,0:T(8,128)(2,1)} %bitcast.82, bf16[32,576,384]{2,1,0:T(8,128)(2,1)} %bitcast.83, ...), custom_call_target="tpu_custom_call" | custom-call | flops 3422552064 | bytes 14155776 | tf_op jit(solution)/shard_map/attend_cache/pallas_call | solution.py:435
  94.1 2.6 %fusion.23 = bf16[32,2,16,128]{3,0,1,2:T(8,128)(2,1)S(1)} fusion(bf16[16,512,128]{2,1,0:T(8,128)(2,1)S(1)} %copy-done, bf16[32,2,16,512]{3,2,1,0:T(8,128)(2,1)} %bitcast.90), kind=kOutput, calls=%fused_computation.11 | convolution fusion | flops 134348800 | bytes 3407872 | tf_op jit(solution)/shard_map/nshc,hcv->nshv/dot_general | solution.py:631
  96.7 0.2 copy.48
  96.9 0.9 pad_maximum_fusion.1
  97.8 8.0 %all-to-all-start.1 = ((bf16[16,64,256]{2,1,0:T(8,128)(2,1)}), bf16[16,64,256]{2,1,0:T(8,128)(2,1)S(1)}, u32[]{:S(2)}, u32[]{:S(2)}) async-start(bf16[16,64,256]{2,1,0:T(8,128)(2,1)} %pad_maximum_fusion.1), calls=%async_computation.1 | async-start | bytes 1048576 | tf_op jit(solution)/shard_map/all_to_all | solution.py:642
  105.9 17.9 %attend_first.1 = (bf16[1,512,512]{2,1,0:T(8,128)(2,1)}, bf16[512,512]{1,0:T(8,128)(2,1)}, f32[512,128]{1,0:T(8,128)}) custom-call(s32[8]{0:T(128)} %stack.31.info, bf16[4,512,576]{2,1,0:T(8,128)(2,1)} %bitcast.114, bf16[512,576]{1,0:T(8,128)(2,1)} %bitcast.98, bf16[128,576]{1,0:T(8,128)(2,1)} %fusion.36.fresh_ref, ...), custom_call_target="tpu_custom_call" | custom-call | flops 9730785280 | bytes 6635520 | tf_op jit(solution)/shard_map/attend_first/pallas_call | solution.py:211
  123.8 1.6 %fusion.20 = f32[16,2,16,128]{3,0,1,2:T(8,128)S(1)} fusion(bf16[16,512,128]{2,1,0:T(8,128)(2,1)S(1)} %copy-done, bf16[16,2,16,512]{3,2,1,0:T(8,128)(2,1)} %bitcast.101), kind=kOutput, calls=%fused_computation.10 | convolution fusion | flops 67108864 | bytes 2883584 | tf_op jit(solution)/shard_map/rshc,hcv->rshv/dot_general | solution.py:667
  125.4 0.9 copy.50
  126.3 0.8 copy-done.3
  127.1 3.0 %merge_decode.1 = bf16[16,32,128]{2,1,0:T(8,128)(2,1)} custom-call(s32[16]{0:T(128)} %copy-done.8, bf16[32,32,256]{2,1,0:T(8,128)(2,1)} %bitcast.89, f32[16,32,128]{2,1,0:T(8,128)} %bitcast.91, f32[16,32,128]{2,1,0:T(8,128)} %bitcast.104), custom_call_target="tpu_custom_call" | custom-call | tf_op jit(solution)/shard_map/merge_decode/pallas_call | solution.py:479
  130.1 0.6 fusion.26
  130.7 20.9 %attend_later.1 = bf16[3,512,512]{2,1,0:T(8,128)(2,1)} custom-call(s32[8]{0:T(128)} %stack.31.info, bf16[4,512,576]{2,1,0:T(8,128)(2,1)} %bitcast.115, bf16[16,3,192,576]{3,2,1,0:T(8,128)(2,1)} %bitcast.113, bf16[4,10,16,576]{3,2,1,0:T(8,128)(2,1)} %pad_maximum_fusion.rest_0_.rest_8_, bf16[4,10,16,576]{3,2,1,0:T(8,128)(2,1)} %collective-permute-done.7.rest_1_.rest_9_, ...), custom_call_target="tpu_custom_call" | custom-call | flops 14092861440 | bytes 15925248 | tf_op jit(solution)/shard_map/attend_later/pallas_call | solution.py:328
  151.7 3.3 %fusion.12 = bf16[3,32,16,128]{3,1,0,2:T(8,128)(2,1)S(1)} fusion(bf16[16,512,128]{2,1,0:T(8,128)(2,1)S(1)} %copy-done, bf16[3,32,16,512]{3,2,1,0:T(8,128)(2,1)} %bitcast.117), kind=kOutput, calls=%fused_computation.8 | convolution fusion | flops 201523200 | bytes 4063232 | tf_op jit(solution)/shard_map/pthc,hcv->pthv/dot_general | solution.py:686
  155.0 1.1 copy.53
  (42 shorter events, 0.4 us)
Async XLA Ops:
  7.2 86.9 %copy-start = (bf16[16,512,128]{2,1,0:T(8,128)(2,1)S(1)}, bf16[16,512,128]{2,1,0:T(8,128)(2,1)}, u32[]{:S(2)}) copy-start(bf16[16,512,128]{2,1,0:T(8,128)(2,1)} %param.23) | copy-start | bytes 6291460
  7.2 4.5 %copy-start.2 = (bf16[896,576]{0,1:T(8,128)(2,1)S(1)}, bf16[896,576]{0,1:T(8,128)(2,1)}, u32[]{:S(2)}) copy-start(bf16[896,576]{0,1:T(8,128)(2,1)} %param.21) | copy-start | bytes 3096580
  7.2 7.0 %copy-start.11 = (s32[16,1]{0,1:T(1,128)S(1)}, s32[16,1]{0,1:T(1,128)}, u32[]{:S(2)}) copy-start(s32[16,1]{0,1:T(1,128)} %param.19) | copy-start | bytes 196
  7.2 7.8 %copy-start.9 = (s32[16]{0:T(128)S(1)}, s32[16]{0:T(128)}, u32[]{:S(2)}) copy-start(s32[16]{0:T(128)} %param.20) | copy-start | bytes 196
  7.2 123.5 %all-gather.2.cloned.1.call-start = ((), (), s32[]{:S(2)}) async-start(), calls=%async_computation.2 | async-start | bytes 11888640 | tf_op jit(solution)/shard_map/all_gather | solution.py:547
  12.8 14.4 %collective-permute-start = (bf16[96,576]{1,0:T(8,128)(2,1)}, bf16[96,576]{1,0:T(8,128)(2,1)}, u32[]{:S(2)}, u32[]{:S(2)}) collective-permute-start(bf16[96,576]{1,0:T(8,128)(2,1)} %pad_maximum_fusion.5), channel_id=1, source_target_pairs={{0,1},{1,0},{2,3},{3,2},{4,5},{5,4},{6,7},{7,6},{8,9},{9,8},{10,11... | collective-permute-start | bytes 331784 | tf_op jit(solution)/shard_map/ppermute | solution.py:490
  14.4 0.6 copy-start.8
  15.6 10.2 %copy-start.10 = (s32[4]{0:T(128)S(1)}, s32[4]{0:T(128)}, u32[]{:S(2)}) copy-start(s32[4]{0:T(128)} %param.15) | copy-start | bytes 52
  18.0 22.9 %copy-start.7 = (f32[512]{0:T(512)S(1)}, f32[512]{0:T(512)}, u32[]{:S(2)}) copy-start(f32[512]{0:T(512)} %param.22) | copy-start | bytes 6148
  18.1 65.1 %all-to-all-start = ((bf16[16,64,640]{2,1,0:T(8,128)(2,1)}), bf16[16,64,640]{2,1,0:T(8,128)(2,1)S(1)}, u32[]{:S(2)}, u32[]{:S(2)}) async-start(bf16[16,64,640]{2,1,0:T(8,128)(2,1)} %bitcast.88), calls=%async_computation | async-start | bytes 2621440 | tf_op jit(solution)/shard_map/all_to_all | solution.py:610
  28.2 7.7 %collective-permute-start.1 = (bf16[96,576]{1,0:T(8,128)(2,1)S(1)}, bf16[96,576]{1,0:T(8,128)(2,1)S(1)}, u32[]{:S(2)}, u32[]{:S(2)}) collective-permute-start(bf16[96,576]{1,0:T(8,128)(2,1)S(1)} %add_convert_fusion), channel_id=1, source_target_pairs={{2,0},{4,2},{6,4},{0,6},{3,1},{5,3},{7,5},{1,7},{10,8},{12,10},{14... | collective-permute-start | bytes 331784 | tf_op jit(solution)/shard_map/ppermute | solution.py:494
  31.0 5.8 %collective-permute-start.2 = (bf16[96,576]{1,0:T(8,128)(2,1)S(1)}, bf16[96,576]{1,0:T(8,128)(2,1)S(1)}, u32[]{:S(2)}, u32[]{:S(2)}) collective-permute-start(bf16[96,576]{1,0:T(8,128)(2,1)S(1)} %add_convert_fusion), channel_id=1, source_target_pairs={{4,0},{6,2},{0,4},{2,6},{5,1},{7,3},{1,5},{3,7},{12,8},{14,10},{8,... | collective-permute-start | bytes 331784 | tf_op jit(solution)/shard_map/ppermute | solution.py:494
  31.3 9.4 %collective-permute-start.3 = (bf16[96,576]{1,0:T(8,128)(2,1)S(1)}, bf16[96,576]{1,0:T(8,128)(2,1)S(1)}, u32[]{:S(2)}, u32[]{:S(2)}) collective-permute-start(bf16[96,576]{1,0:T(8,128)(2,1)S(1)} %add_convert_fusion), channel_id=1, source_target_pairs={{6,0},{0,2},{2,4},{4,6},{7,1},{1,3},{3,5},{5,7},{14,8},{8,10},{10,... | collective-permute-start | bytes 331784 | tf_op jit(solution)/shard_map/ppermute | solution.py:494
  41.4 7.4 %collective-permute-start.4 = (bf16[10,16,576]{2,1,0:T(8,128)(2,1)S(1)}, bf16[10,16,576]{2,1,0:T(8,128)(2,1)S(1)}, u32[]{:S(2)}, u32[]{:S(2)}) collective-permute-start(bf16[10,16,576]{2,1,0:T(8,128)(2,1)S(1)} %bitcast.93), channel_id=1, source_target_pairs={{8,0},{33,1},{16,8},{41,9},{24,16},{49,17},{0,24},{57,25},{40,32},... | collective-permute-start | bytes 552968 | tf_op jit(solution)/shard_map/ppermute | solution.py:507
  43.9 7.7 %collective-permute-start.5 = (bf16[10,16,576]{2,1,0:T(8,128)(2,1)S(1)}, bf16[10,16,576]{2,1,0:T(8,128)(2,1)S(1)}, u32[]{:S(2)}, u32[]{:S(2)}) collective-permute-start(bf16[10,16,576]{2,1,0:T(8,128)(2,1)S(1)} %bitcast.94), channel_id=1, source_target_pairs={{16,0},{65,1},{24,8},{73,9},{0,16},{81,17},{8,24},{89,25},{48,32},... | collective-permute-start | bytes 552968 | tf_op jit(solution)/shard_map/ppermute | solution.py:507
  44.5 8.9 %collective-permute-start.6 = (bf16[10,16,576]{2,1,0:T(8,128)(2,1)S(1)}, bf16[10,16,576]{2,1,0:T(8,128)(2,1)S(1)}, u32[]{:S(2)}, u32[]{:S(2)}) collective-permute-start(bf16[10,16,576]{2,1,0:T(8,128)(2,1)S(1)} %bitcast.95), channel_id=1, source_target_pairs={{24,0},{97,1},{0,8},{105,9},{8,16},{113,17},{16,24},{121,25},{56,3... | collective-permute-start | bytes 552968 | tf_op jit(solution)/shard_map/ppermute | solution.py:507
  54.5 14.0 %collective-permute-start.7 = (bf16[4,10,16,576]{3,2,1,0:T(8,128)(2,1)}, bf16[4,10,16,576]{3,2,1,0:T(8,128)(2,1)}, u32[]{:S(2)}, u32[]{:S(2)}) collective-permute-start(bf16[4,10,16,576]{3,2,1,0:T(8,128)(2,1)} %pad_maximum_fusion.rest_0_.rest_8_), channel_id=1, source_target_pairs={{32,0},{9,1},{40,8},{17,9},{48,16},{25,17},{56,24},{1,25},{64,32},... | collective-permute-start | bytes 2211848 | tf_op jit(solution)/shard_map/ppermute | solution.py:507
  55.7 15.8 %collective-permute-start.8 = (bf16[4,10,16,576]{3,2,1,0:T(8,128)(2,1)}, bf16[4,10,16,576]{3,2,1,0:T(8,128)(2,1)}, u32[]{:S(2)}, u32[]{:S(2)}) collective-permute-start(bf16[4,10,16,576]{3,2,1,0:T(8,128)(2,1)} %pad_maximum_fusion.rest_0_.rest_8_), channel_id=1, source_target_pairs={{64,0},{17,1},{72,8},{25,9},{80,16},{1,17},{88,24},{9,25},{96,32},... | collective-permute-start | bytes 2211848 | tf_op jit(solution)/shard_map/ppermute | solution.py:507
  56.2 24.2 %collective-permute-start.9 = (bf16[4,10,16,576]{3,2,1,0:T(8,128)(2,1)}, bf16[4,10,16,576]{3,2,1,0:T(8,128)(2,1)}, u32[]{:S(2)}, u32[]{:S(2)}) collective-permute-start(bf16[4,10,16,576]{3,2,1,0:T(8,128)(2,1)} %pad_maximum_fusion.rest_0_.rest_8_), channel_id=1, source_target_pairs={{96,0},{25,1},{104,8},{1,9},{112,16},{9,17},{120,24},{17,25},{0,32... | collective-permute-start | bytes 2211848 | tf_op jit(solution)/shard_map/ppermute | solution.py:507
  58.9 46.9 %collective-permute-start.10 = (bf16[4,10,16,576]{3,2,1,0:T(8,128)(2,1)}, bf16[4,10,16,576]{3,2,1,0:T(8,128)(2,1)}, u32[]{:S(2)}, u32[]{:S(2)}) collective-permute-start(bf16[4,10,16,576]{3,2,1,0:T(8,128)(2,1)} %pad_maximum_fusion.rest_0_.rest_8_), channel_id=1, source_target_pairs={{0,1},{1,0},{2,3},{3,2},{4,5},{5,4},{6,7},{7,6},{8,9},{9,8},{10,11... | collective-permute-start | bytes 2211848 | tf_op jit(solution)/shard_map/ppermute | solution.py:490
  80.4 25.4 %collective-permute-start.11 = (bf16[4,10,16,576]{3,2,1,0:T(8,128)(2,1)}, bf16[4,10,16,576]{3,2,1,0:T(8,128)(2,1)}, u32[]{:S(2)}, u32[]{:S(2)}) collective-permute-start(bf16[4,10,16,576]{3,2,1,0:T(8,128)(2,1)} %collective-permute-done.7.rest_1_.rest_9_), channel_id=1, source_target_pairs={{0,1},{1,0},{2,3},{3,2},{4,5},{5,4},{6,7},{7,6},{8,9},{9,8},{10,11... | collective-permute-start | bytes 2211848 | tf_op jit(solution)/shard_map/ppermute | solution.py:490
  82.6 23.3 %collective-permute-start.12 = (bf16[4,10,16,576]{3,2,1,0:T(8,128)(2,1)}, bf16[4,10,16,576]{3,2,1,0:T(8,128)(2,1)}, u32[]{:S(2)}, u32[]{:S(2)}) collective-permute-start(bf16[4,10,16,576]{3,2,1,0:T(8,128)(2,1)} %collective-permute-done.8.rest_2_.rest_10_), channel_id=1, source_target_pairs={{0,1},{1,0},{2,3},{3,2},{4,5},{5,4},{6,7},{7,6},{8,9},{9,8},{10,11... | collective-permute-start | bytes 2211848 | tf_op jit(solution)/shard_map/ppermute | solution.py:490
  82.6 23.3 %collective-permute-start.13 = (bf16[4,10,16,576]{3,2,1,0:T(8,128)(2,1)}, bf16[4,10,16,576]{3,2,1,0:T(8,128)(2,1)}, u32[]{:S(2)}, u32[]{:S(2)}) collective-permute-start(bf16[4,10,16,576]{3,2,1,0:T(8,128)(2,1)} %collective-permute-done.9.rest_3_.rest_11_), channel_id=1, source_target_pairs={{0,1},{1,0},{2,3},{3,2},{4,5},{5,4},{6,7},{7,6},{8,9},{9,8},{10,11... | collective-permute-start | bytes 2211848 | tf_op jit(solution)/shard_map/ppermute | solution.py:490
  83.1 2.5 %copy-start.1 = (bf16[16,64,640]{2,1,0:T(8,128)(2,1)}, bf16[16,64,640]{2,1,0:T(8,128)(2,1)S(1)}, u32[]{:S(2)}) copy-start(bf16[16,64,640]{2,1,0:T(8,128)(2,1)S(1)} %all-to-all-done) | copy-start | bytes 3932164
  83.4 2.2 %copy-start.6 = (s32[32]{0:T(128)}, s32[32]{0:T(128)S(1)}, u32[]{:S(2)}) copy-start(s32[32]{0:T(128)S(1)} %fusion.46.length) | copy-start | bytes 388
  94.1 2.8 %copy-start.5 = (bf16[32,32,128]{2,1,0:T(8,128)(2,1)S(1)}, bf16[32,32,128]{2,1,0:T(8,128)(2,1)}, u32[]{:S(2)}) copy-start(bf16[32,32,128]{2,1,0:T(8,128)(2,1)} %get-tuple-element.18) | copy-start | bytes 786436
  97.8 28.5 %all-to-all-start.1 = ((bf16[16,64,256]{2,1,0:T(8,128)(2,1)}), bf16[16,64,256]{2,1,0:T(8,128)(2,1)S(1)}, u32[]{:S(2)}, u32[]{:S(2)}) async-start(bf16[16,64,256]{2,1,0:T(8,128)(2,1)} %pad_maximum_fusion.1), calls=%async_computation.1 | async-start | bytes 1048576 | tf_op jit(solution)/shard_map/all_to_all | solution.py:642
  123.8 6.3 %copy-start.4 = (bf16[1,512,512]{2,1,0:T(8,128)(2,1)S(1)}, bf16[1,512,512]{2,1,0:T(8,128)(2,1)}, u32[]{:S(2)}) copy-start(bf16[1,512,512]{2,1,0:T(8,128)(2,1)} %get-tuple-element.17) | copy-start | bytes 1572868
  126.3 0.8 copy-start.3
Sparse Core Ops, SparseCore 0:
  11.0 96.9 all-gather.1
